TPU v7x, 32 devices: a whole 2x2x4 slice. The times are simulated.
32 devices in a mesh: dp: 2 (over x), expert: 4 (over z), head: 4 (over y, core).
Axes of the slice: x: 2, y: 2, z: 4, core: 2. Of those that a mesh axis runs over, the one named last changes fastest.
Arguments:
- inputs: bfloat16 [16, 784, 768], P(('dp', 'expert')), may hold values from -6 to 6
- w_qkv: bfloat16 [768, 3, 768], P(('dp', 'expert'), None, 'head'), may hold values from -0.21875 to 0.21875
- w_out: bfloat16 [768, 768], P('head', ('dp', 'expert')), may hold values from -0.875 to 0.875
- w_router: bfloat16 [768, 4], P(('dp', 'expert')), may hold values from -0.109375 to 0.109375
- gain_one: float32 [768], P(('dp', 'expert')), may hold values from 0.1 to 1.9
- gain_two: float32 [768], P(('dp', 'expert')), may hold values from 0.1 to 1.9
- w_in: bfloat16 [4, 768, 3072], P('expert', 'dp', 'head'), may hold values from -0.21875 to 0.21875
- w_back: bfloat16 [4, 3072, 768], P('expert', 'head', 'dp'), may hold values from -0.4375 to 0.4375
- experts: int32 [16, 784, 2], P(('dp', 'expert')), may hold values from 0 to 3, all different within a row
- priority: int32 [16, 784], P(('dp', 'expert')), may hold values from 0 to 783, each once within a row
- cotangent: bfloat16 [16, 784, 768], P(('dp', 'expert')), may hold values from -6 to 6
Outputs:
- mixed: bfloat16 [16, 784, 768], P(('dp', 'expert'), 'head')
- grad_inputs: bfloat16 [16, 784, 768], P(('dp', 'expert'))
- grad_qkv: float32 [768, 3, 768], P(('dp', 'expert'), None, 'head')
- grad_w_out: float32 [768, 768], P('head', ('dp', 'expert'))
- grad_router: float32 [768, 4], P(('dp', 'expert'))
- grad_gain_one: float32 [768], P(('dp', 'expert'))
- grad_gain_two: float32 [768], P(('dp', 'expert'))
- grad_w_in: float32 [4, 768, 3072], P('expert', 'dp', 'head')
- grad_w_back: float32 [4, 3072, 768], P('expert', 'head', 'dp')
Inputs may be any that keep to these rules, and one draw needn't show every extreme that they name: Each token names two different experts; every expert is named by some token. Each row of priority holds every one of the 784 ranks once.
All inputs are finite; a program needn't handle non-finite values.
Results may differ from a plain program's by a relative error of at most 0.038.
Values may be sent and summed in bfloat16 or wider, within the bound.
A program may use at most 192 MiB of HBM per device.

v0:
```python
import jax
import jax.numpy as jnp
from jax import lax
from jax.sharding import PartitionSpec as P

HD = 64
SEQ = 196


def split_up(shard, dim, length):
    dims = shard.shape
    pieces = shard.reshape(*dims[:dim], length, dims[dim] // length, *dims[dim + 1 :])
    return jnp.moveaxis(pieces, dim, 0)


def sent_and_summed(shard, axis, dim):
    pieces = split_up(shard, dim, lax.axis_size(axis))
    arrived = lax.all_to_all(pieces, axis, split_axis=0, concat_axis=0, tiled=True)
    return arrived.astype(jnp.float32).sum(axis=0)


def sent_together(arrays, axis, dim, along):
    columns = [a.reshape(*a.shape[:along], -1) for a in arrays]
    both = jnp.concatenate(columns, axis=along)
    filled, at, gathered = (sent_and_summed(both, axis, dim), 0, [])
    for a, column in zip(arrays, columns):
        share = filled[..., at : at + column.shape[along]]
        gathered.append(share.reshape(*share.shape[:along], *a.shape[along:]))
        at += column.shape[along]
    return tuple(gathered)


def normalize(values):
    centered = values - jnp.mean(values, axis=1, keepdims=True)
    inverse = lax.rsqrt(jnp.mean(centered * centered, axis=1, keepdims=True) + 1e-06)
    return (centered * inverse, inverse)


def norm_backward(upstream, normed, inverse, gain):
    scaled = upstream * gain
    return inverse * (
        scaled
        - jnp.mean(scaled, axis=1, keepdims=True)
        - normed * jnp.mean(scaled * normed, axis=1, keepdims=True)
    )


def gelu_parts(pre_act):
    inner = 0.7978845608028654 * (pre_act + 0.044715 * pre_act * pre_act * pre_act)
    tangent = jnp.tanh(inner)
    value = 0.5 * pre_act * (1.0 + tangent)
    gelu_slope = 0.5 * (1.0 + tangent) + 0.5 * pre_act * (
        1.0 - tangent * tangent
    ) * 0.7978845608028654 * (1.0 + 3.0 * 0.044715 * pre_act * pre_act)
    return (value, gelu_slope)


def route_slots(chosen, ranks, expert_count, capacity):
    total_rows = ranks.shape[0]
    positions = jnp.arange(total_rows, dtype=jnp.int32)
    by_rank = jnp.zeros((total_rows,), jnp.int32).at[ranks].set(positions)
    ordered = jnp.concatenate([chosen[by_rank, 0], chosen[by_rank, 1]])
    onehot = (ordered[:, None] == jnp.arange(expert_count, dtype=jnp.int32)[None, :]).astype(
        jnp.int32
    )
    earlier = jnp.cumsum(onehot, axis=0) - onehot
    seq_slot = jnp.sum(earlier * onehot, axis=1)
    slot_pos = jnp.stack([seq_slot[ranks], seq_slot[total_rows + ranks]], axis=1)
    kept_mask = slot_pos < capacity
    target = jnp.where(kept_mask, chosen * capacity + slot_pos, expert_count * capacity)
    return (kept_mask, target)


def pack_pairs(first_rows, second_rows, target, slots_total):
    columns = first_rows.shape[1]
    buffer = jnp.zeros((slots_total + 1, columns), first_rows.dtype)
    buffer = buffer.at[target[:, 0]].set(first_rows).at[target[:, 1]].set(second_rows)
    return buffer[:slots_total]


def unpack_pairs(packed, target):
    extended = jnp.concatenate([packed, jnp.zeros((1, packed.shape[1]), packed.dtype)], axis=0)
    return extended[target]


def reduce_expert(grad_first, grad_second):
    return (
        lax.psum_scatter(
            grad_first[None].astype(jnp.bfloat16), "dp", scatter_dimension=1, tiled=True
        ).astype(jnp.float32),
        lax.psum_scatter(
            grad_second[None].astype(jnp.bfloat16), "dp", scatter_dimension=2, tiled=True
        ).astype(jnp.float32),
    )


def shards(
    inputs, w_qkv, w_out, w_router, gain_one, gain_two, w_in, w_back, experts, priority, cotangent
):
    qkv_w, out_w, router_w, gain_a, gain_b = (
        lax.all_gather(w_qkv, ("dp", "expert"), axis=0, tiled=True),
        lax.all_gather(w_out, ("dp", "expert"), axis=1, tiled=True),
        lax.all_gather(w_router, ("dp", "expert"), axis=0, tiled=True),
        lax.all_gather(gain_one.astype(jnp.bfloat16), ("dp", "expert"), axis=0, tiled=True).astype(
            gain_one.dtype
        ),
        lax.all_gather(gain_two.astype(jnp.bfloat16), ("dp", "expert"), axis=0, tiled=True).astype(
            gain_two.dtype
        ),
    )
    first_w, second_w = (
        lax.all_gather(w_in, "dp", axis=1, tiled=True),
        lax.all_gather(w_back, "dp", axis=2, tiled=True),
    )
    first_w = first_w[0]
    second_w = second_w[0]
    model_width = qkv_w.shape[0]
    local_width = qkv_w.shape[2]
    heads_here = local_width // HD
    qkv_flat = qkv_w.reshape(model_width, 3 * local_width)
    expert_count = router_w.shape[1]
    block_count = inputs.shape[0]
    row_count = inputs.shape[1]
    capacity = row_count // expert_count
    slots_total = expert_count * capacity
    images = row_count // SEQ
    quarter = row_count // lax.axis_size("head")
    share_start = lax.axis_index("head") * quarter
    score_scale = HD ** (-0.5)
    acc_qkv = jnp.zeros((model_width, 3 * local_width), jnp.float32)
    acc_out = jnp.zeros((local_width, model_width), jnp.float32)
    acc_router = jnp.zeros((model_width, expert_count), jnp.float32)
    acc_gain_a = jnp.zeros((model_width,), jnp.float32)
    acc_gain_b = jnp.zeros((model_width,), jnp.float32)
    acc_first = jnp.zeros(first_w.shape, jnp.float32)
    acc_second = jnp.zeros(second_w.shape, jnp.float32)
    outputs = []
    grads_in = []
    for micro_index in range(block_count):
        tokens = inputs[micro_index].astype(jnp.float32)
        normed_a, inverse_a = normalize(tokens)
        act_a = (normed_a * gain_a).astype(jnp.bfloat16)
        projected = jnp.dot(act_a, qkv_flat, preferred_element_type=jnp.float32).reshape(
            row_count, 3, local_width
        )
        query_low = (
            (projected[:, 0] * score_scale)
            .astype(jnp.bfloat16)
            .reshape(images, SEQ, heads_here, HD)
        )
        key_low = projected[:, 1].astype(jnp.bfloat16).reshape(images, SEQ, heads_here, HD)
        value_low = projected[:, 2].astype(jnp.bfloat16).reshape(images, SEQ, heads_here, HD)
        scores = jnp.einsum(
            "ishd,ithd->ihst", query_low, key_low, preferred_element_type=jnp.float32
        )
        row_max = jnp.max(scores, axis=-1, keepdims=True)
        row_total = jnp.sum(jnp.exp(scores - row_max), axis=-1, keepdims=True)
        log_total = row_max + jnp.log(row_total)
        probs_low = jnp.exp(scores - log_total).astype(jnp.bfloat16)
        attended = jnp.einsum(
            "ihst,ithd->ishd", probs_low, value_low, preferred_element_type=jnp.float32
        )
        attended_low = attended.reshape(row_count, local_width).astype(jnp.bfloat16)
        partial_out = jnp.dot(attended_low, out_w, preferred_element_type=jnp.float32)
        attn_sum = lax.psum(partial_out.astype(jnp.bfloat16), "head").astype(jnp.float32)
        hidden = tokens + attn_sum
        normed_b, inverse_b = normalize(hidden)
        act_b = (normed_b * gain_b).astype(jnp.bfloat16)
        hidden_share = lax.dynamic_slice_in_dim(hidden, share_start, quarter, 0)
        logits = jnp.dot(act_b, router_w, preferred_element_type=jnp.float32)
        router_probs = jax.nn.softmax(logits, axis=1)
        chosen = experts[micro_index]
        kept_mask, target = route_slots(chosen, priority[micro_index], expert_count, capacity)
        choice_hot = (
            chosen[:, :, None] == jnp.arange(expert_count, dtype=jnp.int32)[None, None, :]
        ).astype(jnp.float32)
        live_gates = jnp.sum(choice_hot * router_probs[:, None, :], axis=2) * kept_mask.astype(
            jnp.float32
        )
        packed = pack_pairs(act_b, act_b, target, slots_total).reshape(
            expert_count, capacity, model_width
        )
        arrived = lax.all_to_all(packed, "expert", split_axis=0, concat_axis=0, tiled=True).reshape(
            slots_total, model_width
        )
        pre_act = jnp.dot(arrived, first_w, preferred_element_type=jnp.float32)
        activated, gelu_slope = gelu_parts(pre_act)
        act_low = activated.astype(jnp.bfloat16)
        expert_out = jnp.dot(act_low, second_w, preferred_element_type=jnp.float32).astype(
            jnp.bfloat16
        )
        returned = lax.all_to_all(
            expert_out.reshape(expert_count, capacity, model_width),
            "expert",
            split_axis=0,
            concat_axis=0,
            tiled=True,
        ).reshape(slots_total, model_width)
        pair_out = unpack_pairs(returned, target).astype(jnp.float32)
        mixed_part = jnp.sum(live_gates[:, :, None] * pair_out, axis=1)
        mixed_share = lax.psum_scatter(
            mixed_part.astype(jnp.bfloat16), "head", scatter_dimension=0, tiled=True
        ).astype(jnp.float32)
        outputs.append((hidden_share + mixed_share).astype(jnp.bfloat16))
        upstream = cotangent[micro_index].astype(jnp.float32)
        gate_dots = jnp.sum(pair_out * upstream[:, None, :], axis=2)
        grad_pairs = (live_gates[:, :, None] * upstream[:, None, :]).astype(jnp.bfloat16)
        grad_packed = pack_pairs(grad_pairs[:, 0], grad_pairs[:, 1], target, slots_total)
        grad_arrived = lax.all_to_all(
            grad_packed.reshape(expert_count, capacity, model_width),
            "expert",
            split_axis=0,
            concat_axis=0,
            tiled=True,
        ).reshape(slots_total, model_width)
        step_second = jnp.dot(act_low.T, grad_arrived, preferred_element_type=jnp.float32)
        grad_act = jnp.dot(grad_arrived, second_w.T, preferred_element_type=jnp.float32)
        grad_pre = (grad_act * gelu_slope).astype(jnp.bfloat16)
        step_first = jnp.dot(arrived.T, grad_pre, preferred_element_type=jnp.float32)
        grad_rows = jnp.dot(grad_pre, first_w.T, preferred_element_type=jnp.float32).astype(
            jnp.bfloat16
        )
        grad_returned = lax.all_to_all(
            grad_rows.reshape(expert_count, capacity, model_width),
            "expert",
            split_axis=0,
            concat_axis=0,
            tiled=True,
        ).reshape(slots_total, model_width)
        dispatch_grad = jnp.sum(unpack_pairs(grad_returned, target).astype(jnp.float32), axis=1)
        grad_share, dots_share = (
            lax.psum_scatter(
                dispatch_grad.astype(jnp.bfloat16), "head", scatter_dimension=0, tiled=True
            ).astype(jnp.float32),
            lax.psum_scatter(
                gate_dots.astype(jnp.bfloat16), "head", scatter_dimension=0, tiled=True
            ).astype(jnp.float32),
        )
        probs_share = lax.dynamic_slice_in_dim(router_probs, share_start, quarter, 0)
        hot_share = lax.dynamic_slice_in_dim(choice_hot, share_start, quarter, 0)
        grad_probs = jnp.sum(hot_share * dots_share[:, :, None], axis=1)
        grad_logits = probs_share * (
            grad_probs - jnp.sum(probs_share * grad_probs, axis=1, keepdims=True)
        )
        logits_low = grad_logits.astype(jnp.bfloat16)
        grad_share = grad_share + jnp.dot(
            logits_low, router_w.T, preferred_element_type=jnp.float32
        )
        grad_norm_b, logits_all = (
            lax.all_gather(grad_share.astype(jnp.bfloat16), "head", axis=0, tiled=True).astype(
                grad_share.dtype
            ),
            lax.all_gather(
                logits_low.astype(jnp.float32).astype(jnp.bfloat16), "head", axis=0, tiled=True
            ).astype(jnp.float32),
        )
        acc_gain_b = acc_gain_b + jnp.sum(grad_norm_b * normed_b, axis=0)
        grad_hidden = upstream + norm_backward(grad_norm_b, normed_b, inverse_b, gain_b)
        acc_router = acc_router + jnp.dot(
            act_b.T, logits_all.astype(jnp.bfloat16), preferred_element_type=jnp.float32
        )
        grad_hidden_low = grad_hidden.astype(jnp.bfloat16)
        acc_out = acc_out + jnp.dot(
            attended_low.T, grad_hidden_low, preferred_element_type=jnp.float32
        )
        grad_att = jnp.dot(grad_hidden_low, out_w.T, preferred_element_type=jnp.float32).astype(
            jnp.bfloat16
        )
        grad_att = grad_att.reshape(images, SEQ, heads_here, HD)
        again_scores = jnp.einsum(
            "ishd,ithd->ihst", query_low, key_low, preferred_element_type=jnp.float32
        )
        attn_probs = jnp.exp(again_scores - log_total)
        grad_probs_att = jnp.einsum(
            "ishd,ithd->ihst", grad_att, value_low, preferred_element_type=jnp.float32
        )
        grad_value = jnp.einsum(
            "ihst,ishd->ithd", probs_low, grad_att, preferred_element_type=jnp.float32
        ).astype(jnp.bfloat16)
        grad_scores = (
            attn_probs
            * (grad_probs_att - jnp.sum(attn_probs * grad_probs_att, axis=-1, keepdims=True))
        ).astype(jnp.bfloat16)
        grad_query = jnp.einsum(
            "ihst,ithd->ishd", grad_scores, key_low, preferred_element_type=jnp.float32
        ).astype(jnp.bfloat16)
        grad_key = jnp.einsum(
            "ihst,ishd->ithd", grad_scores, query_low, preferred_element_type=jnp.float32
        ).astype(jnp.bfloat16)
        grad_proj = jnp.concatenate(
            [
                (grad_query * score_scale).reshape(row_count, local_width),
                grad_key.reshape(row_count, local_width),
                grad_value.reshape(row_count, local_width),
            ],
            axis=1,
        )
        acc_qkv = acc_qkv + jnp.dot(act_a.T, grad_proj, preferred_element_type=jnp.float32)
        grad_norm_a = lax.psum(
            jnp.dot(grad_proj, qkv_flat.T, preferred_element_type=jnp.float32).astype(jnp.bfloat16),
            "head",
        ).astype(jnp.float32)
        acc_gain_a = acc_gain_a + jnp.sum(grad_norm_a * normed_a, axis=0)
        grad_tokens = grad_hidden + norm_backward(grad_norm_a, normed_a, inverse_a, gain_a)
        grads_in.append(grad_tokens.astype(jnp.bfloat16))
        acc_first = acc_first + step_first
        acc_second = acc_second + step_second
    share_first, share_second = reduce_expert(acc_first, acc_second)
    grad_qkv, grad_w_out, grad_router, grad_gain_one, grad_gain_two = (
        sent_and_summed(
            acc_qkv.reshape(model_width, 3, local_width).astype(jnp.bfloat16), ("dp", "expert"), 0
        ),
        sent_and_summed(acc_out.astype(jnp.bfloat16), ("dp", "expert"), 1),
        *sent_together(
            (acc_router.astype(jnp.bfloat16), acc_gain_a.astype(jnp.bfloat16)),
            ("dp", "expert"),
            0,
            1,
        ),
        sent_and_summed(acc_gain_b.astype(jnp.bfloat16), ("dp", "expert"), 0),
    )
    return (
        jnp.stack(outputs),
        jnp.stack(grads_in),
        grad_qkv,
        grad_w_out,
        grad_router,
        grad_gain_one,
        grad_gain_two,
        share_first,
        share_second,
    )


def solution(mesh):
    in_specs = (
        P(("dp", "expert"), None, None),
        P(("dp", "expert"), None, "head"),
        P("head", ("dp", "expert")),
        P(("dp", "expert"), None),
        P(("dp", "expert")),
        P(("dp", "expert")),
        P("expert", "dp", "head"),
        P("expert", "head", "dp"),
        P(("dp", "expert"), None, None),
        P(("dp", "expert"), None),
        P(("dp", "expert"), None, None),
    )
    out_specs = (
        P(("dp", "expert"), "head", None),
        P(("dp", "expert"), None, None),
        P(("dp", "expert"), None, "head"),
        P("head", ("dp", "expert")),
        P(("dp", "expert"), None),
        P(("dp", "expert")),
        P(("dp", "expert")),
        P("expert", "dp", "head"),
        P("expert", "head", "dp"),
    )
    return jax.shard_map(shards, mesh=mesh, in_specs=in_specs, out_specs=out_specs, check_vma=False)
```

profile of v0, /device:TPU:0, one launch (start us, length us, event | category | flops | bytes accessed | tf_op | source)
XLA Modules:
  0.0 909.8 jit_solution(1978699250883668652)
XLA Ops:
  10.6 42.7 %all_gather.34 = bf16[768,3,192]{2,1,0:T(4,128)(2,1)} all-gather(bf16[96,3,192]{2,1,0:T(4,128)(2,1)S(1)} %copy.269), channel_id=1, replica_groups=mesh['dp'=2,'expert'=4,'head'=4] {'dp','expert'}, dimensions={0}, use_global_device_ids=true | all-gather | bytes 995328 | tf_op jit(solution)/shard_map/all_gather | solution.py:101
  57.7 20.5 %all-reduce.24 = (bf16[768]{0:T(1024)(128)(2,1)}, bf16[768]{0:T(1024)(128)(2,1)S(1)}) all-reduce(bf16[768]{0:T(1024)(128)(2,1)S(1)} %dynamic-update-slice.1, bf16[768]{0:T(1024)(128)(2,1)S(1)} %dynamic-update-slice), channel_id=1, replica_groups=mesh['dp'=2,'expert'=4,'head'=4] {'dp','expert'}, use_global_device_ids=true, to_apply=%add.11 | all-reduce | flops 1536 | bytes 6144
  89.3 31.4 %all_gather.35 = bf16[192,768]{0,1:T(8,128)(2,1)S(1)} all-gather(bf16[192,96]{0,1:T(8,128)(2,1)S(1)} %copy.276), channel_id=1, replica_groups=mesh['dp'=2,'expert'=4,'head'=4] {'dp','expert'}, dimensions={1}, use_global_device_ids=true | all-gather | bytes 331776 | tf_op jit(solution)/shard_map/all_gather | solution.py:102
  122.4 5.3 scatter_custom_fusion
  127.7 10.5 %gather_fusion.1 = s32[784]{0:T(1024)S(1)} fusion(s32[784,2]{0,1:T(2,128)S(1)} %get-tuple-element.135, s32[784]{0:T(1024)S(1)} %get-tuple-element.138), kind=kCustom, calls=%fused_computation.1 | custom fusion | bytes 12544 | tf_op jit(solution)/shard_map/gather | solution.py:62
  138.2 10.5 %gather_fusion = s32[784]{0:T(1024)S(1)} fusion(s32[784,2]{0,1:T(2,128)S(1)} %get-tuple-element.135, s32[784]{0:T(1024)S(1)} %get-tuple-element.137), kind=kCustom, calls=%fused_computation | custom fusion | bytes 12544 | tf_op jit(solution)/shard_map/gather | solution.py:62
  150.5 5.5 scatter_custom_fusion.3
  156.1 10.5 %gather_fusion.6 = s32[784]{0:T(1024)S(1)} fusion(s32[784,2]{0,1:T(2,128)S(1)} %get-tuple-element.136, s32[784]{0:T(1024)S(1)} %get-tuple-element.140), kind=kCustom, calls=%fused_computation.6 | custom fusion | bytes 12544 | tf_op jit(solution)/shard_map/gather | solution.py:62
  166.6 10.5 %gather_fusion.5 = s32[784]{0:T(1024)S(1)} fusion(s32[784,2]{0,1:T(2,128)S(1)} %get-tuple-element.136, s32[784]{0:T(1024)S(1)} %get-tuple-element.139), kind=kCustom, calls=%fused_computation.5 | custom fusion | bytes 12544 | tf_op jit(solution)/shard_map/gather | solution.py:62
  199.5 4.9 gather_fusion.3
  214.2 4.9 gather_fusion.7
  219.2 15.5 %all-reduce.33.cloned.1.call-done = bf16[784,768]{1,0:T(8,128)(2,1)} async-done(((bf16[784,768]{1,0:T(8,128)(2,1)}), bf16[784,768]{1,0:T(8,128)(2,1)}) %all-reduce.33.cloned.1.call-update) | async-done | bytes 1204240 | tf_op jit(solution)/shard_map/psum | solution.py:165
  241.0 6.9 scatter_custom_fusion.4
  247.9 6.9 scatter_fusion.1
  263.4 5.9 scatter_custom_fusion.1
  269.3 6.5 scatter_fusion
  277.1 15.4 %all-to-all-done.2 = bf16[4,196,768]{2,1,0:T(8,128)(2,1)} async-done(((bf16[4,196,768]{2,1,0:T(8,128)(2,1)}), bf16[4,196,768]{2,1,0:T(8,128)(2,1)}, u32[]{:S(2)}, u32[]{:S(2)}) %all-to-all-start.2) | async-done | bytes 1204256 | tf_op jit(solution)/shard_map/all_to_all | solution.py:183
  303.0 19.1 %all-gather.12.cloned.1.call-done = bf16[1,768,768]{2,1,0:T(8,128)(2,1)} async-done(((bf16[1,768,384]{2,1,0:T(8,128)(2,1)}), bf16[1,768,768]{2,1,0:T(8,128)(2,1)}) %all-gather.12.cloned.1.call-update) | async-done | bytes 1179664 | tf_op jit(solution)/shard_map/all_gather | solution.py:113
  334.2 39.0 %all-gather = bf16[8,96,4]{1,2,0:T(4,128)(2,1)S(1)} all-gather(bf16[1,96,4]{1,2,0:T(4,128)(2,1)S(1)} %bitcast.378), channel_id=1, replica_groups=mesh['dp'=2,'expert'=4,'head'=4] {'dp','expert'}, dimensions={0}, use_global_device_ids=true | all-gather | bytes 6912 | tf_op jit(solution)/shard_map/all_gather | solution.py:103
  394.3 6.2 gather_fusion.9
  400.5 6.4 reshape.926
  406.9 7.0 multiply_reduce_fusion
  413.9 6.5 scatter_custom_fusion.8
  420.4 6.9 scatter_custom_fusion.9
  430.6 5.5 all-to-all-start.6
  440.1 6.2 gather_fusion.4
  446.4 6.4 reshape.925
  452.7 6.9 multiply_reduce_fusion.1
  459.7 6.5 scatter_custom_fusion.6
  466.2 6.9 scatter_custom_fusion.7
  476.4 5.3 all-to-all-start.4
  492.8 14.3 %all-to-all-done.4 = bf16[4,196,768]{2,1,0:T(8,128)(2,1)} async-done(((bf16[4,196,768]{2,1,0:T(8,128)(2,1)}), bf16[4,196,768]{2,1,0:T(8,128)(2,1)}, u32[]{:S(2)}, u32[]{:S(2)}) %all-to-all-start.4) | async-done | bytes 1204256 | tf_op jit(solution)/shard_map/all_to_all | solution.py:209
  520.6 6.5 copy.333
  557.3 6.2 gather_fusion.11
  563.5 6.1 reshape.838
  576.1 6.2 gather_fusion.10
  582.3 6.4 reshape.830
  588.7 8.5 reduce_sum.429
  597.3 8.8 reduce_sum.420
  606.1 50.0 %fusion.189 = (bf16[200,768]{1,0:T(8,128)(2,1)S(1)}, bf16[200,768]{1,0:T(8,128)(2,1)S(1)}, bf16[208,2]{1,0:T(8,128)(2,1)S(1)}, bf16[200,768]{1,0:T(8,128)(2,1)S(...) fusion(bf16[784,768]{1,0:T(8,128)(2,1)S(1)} %copy-done.23, bf16[784,768]{1,0:T(8,128)(2,1)} %get-tuple-element.68, ...), kind=kCustom, calls=%all-reduce-scatter.6 | all-reduce-scatter fusion | flops 2460930 | bytes 6054144
  687.9 5.2 all-gather.3
  693.2 5.2 all-gather.4
  717.5 6.1 multiply_reduce_fusion.7
  798.4 5.9 all-to-all-start.9
  817.8 32.3 %all-reduce.35.cloned.1.call-done = (bf16[784,768]{1,0:T(8,128)(2,1)}, bf16[784,768]{1,0:T(8,128)(2,1)}) async-done(((bf16[784,768]{1,0:T(8,128)(2,1)}, bf16[784,768]{1,0:T(8,128)(2,1)}), (bf16[784,768]{1,0:T(8,128)(2,1)}, bf16[784,768]{1,0:T(8,128)(2,1)})) %all-reduce.35.cloned.1.call-update) | async-done | bytes 2408464 | tf_op jit(solution)/shard_map/psum | solution.py:299
  855.0 5.5 all-to-all-start.10
  860.5 6.5 all-to-all-done.10
  878.2 21.4 %all-to-all-done.8 = bf16[8,96,3,192]{1,3,2,0:T(8,128)(2,1)} async-done(((bf16[8,96,3,192]{1,3,2,0:T(8,128)(2,1)}), bf16[8,96,3,192]{1,3,2,0:T(8,128)(2,1)}, u32[]{:S(2)}, u32[]{:S(2)}) %all-to-all-start.8) | async-done | bytes 884768 | tf_op jit(solution)/shard_map/all_to_all | solution.py:18
  (519 shorter events, 339.8 us)
Async XLA Ops:
  8.0 47.9 %copy-start.95 = (u32[32]{0:T(128)S(1)}, u32[32]{0:T(128)}, u32[]{:S(2)}) copy-start(u32[32]{0:T(128)} %constant.169) | copy-start | bytes 388
  8.0 70.2 %copy-start = (bf16[2,784,768]{2,1,0:T(8,128)(2,1)S(1)}, bf16[2,784,768]{2,1,0:T(8,128)(2,1)}, u32[]{:S(2)}) copy-start(bf16[2,784,768]{2,1,0:T(8,128)(2,1)} %param.11) | copy-start | bytes 7225348
  8.0 171.1 %all-reduce.31.cloned.1.call-start = ((), (), s32[]{:S(2)}) async-start(), calls=%async_computation.14 | async-start | bytes 2408448 | tf_op jit(solution)/shard_map/psum | solution.py:165
  55.9 26.4 %copy-start.46 = (bf16[768,3,192]{0,2,1:T(8,128)(2,1)}, bf16[768,3,192]{0,2,1:T(8,128)(2,1)S(1)}, u32[]{:S(2)}) copy-start(bf16[768,3,192]{0,2,1:T(8,128)(2,1)S(1)} %copy.270) | copy-start | bytes 2654212
  88.8 33.5 %copy-start.53 = (s32[2,784,2]{1,2,0:T(2,128)S(1)}, s32[2,784,2]{1,2,0:T(2,128)}, u32[]{:S(2)}) copy-start(s32[2,784,2]{1,2,0:T(2,128)} %param.19) | copy-start | bytes 37636
  88.8 33.5 %copy-start.87 = (s32[2,784]{1,0:T(2,128)S(1)}, s32[2,784]{1,0:T(2,128)}, u32[]{:S(2)}) copy-start(s32[2,784]{1,0:T(2,128)} %param.20) | copy-start | bytes 18820
  89.1 49.1 %copy-start.34 = (bf16[784,192]{0,1:T(8,128)(2,1)}, bf16[784,192]{0,1:T(8,128)(2,1)S(1)}, u32[]{:S(2)}) copy-start(bf16[784,192]{0,1:T(8,128)(2,1)S(1)} %convert_element_type.409) | copy-start | bytes 903172
  120.6 77.3 %copy-start.19 = (bf16[192,768]{0,1:T(8,128)(2,1)}, bf16[192,768]{0,1:T(8,128)(2,1)S(1)}, u32[]{:S(2)}) copy-start(bf16[192,768]{0,1:T(8,128)(2,1)S(1)} %all_gather.35) | copy-start | bytes 884740
  122.2 112.5 %all-reduce.33.cloned.1.call-start = ((), (), s32[]{:S(2)}) async-start(), calls=%async_computation.17 | async-start | bytes 2408448 | tf_op jit(solution)/shard_map/psum | solution.py:165
  166.6 12.5 %copy-start.86 = (f32[784]{0:T(1024)S(1)}, f32[784]{0:T(1024)}, u32[]{:S(2)}) copy-start(f32[784]{0:T(1024)} %get-tuple-element.86) | copy-start | bytes 9412
  186.1 8.3 copy-start.26
  219.1 19.0 %copy-start.65 = (f32[768]{0:T(1024)}, f32[768]{0:T(1024)S(1)}, u32[]{:S(2)}) copy-start(f32[768]{0:T(1024)S(1)} %convert_element_type.414) | copy-start | bytes 9220
  219.2 18.9 %copy-start.59 = (f32[784]{0:T(1024)}, f32[784]{0:T(1024)S(1)}, u32[]{:S(2)}) copy-start(f32[784]{0:T(1024)S(1)} %broadcast_multiply_fusion.10) | copy-start | bytes 9412
  255.9 7.5 copy-start.16
  258.2 34.3 %all-to-all-start.2 = ((bf16[4,196,768]{2,1,0:T(8,128)(2,1)}), bf16[4,196,768]{2,1,0:T(8,128)(2,1)}, u32[]{:S(2)}, u32[]{:S(2)}) async-start(bf16[4,196,768]{2,1,0:T(8,128)(2,1)} %reshape.727), calls=%async_computation.2 | async-start | bytes 2457600 | tf_op jit(solution)/shard_map/all_to_all | solution.py:183
  262.8 36.0 %all-gather.10.cloned.1.call-start = ((), (), s32[]{:S(2)}) async-start(), calls=%async_computation.15 | async-start | bytes 1769472 | tf_op jit(solution)/shard_map/all_gather | solution.py:112
  292.5 36.7 %all-to-all-start = ((bf16[4,196,768]{2,1,0:T(8,128)(2,1)}), bf16[4,196,768]{2,1,0:T(8,128)(2,1)}, u32[]{:S(2)}, u32[]{:S(2)}) async-start(bf16[4,196,768]{2,1,0:T(8,128)(2,1)} %reshape.721), calls=%async_computation | async-start | bytes 2457600 | tf_op jit(solution)/shard_map/all_to_all | solution.py:183
  296.8 25.4 %all-gather.12.cloned.1.call-start = ((), (), s32[]{:S(2)}) async-start(), calls=%async_computation.16 | async-start | bytes 1769472 | tf_op jit(solution)/shard_map/all_gather | solution.py:113
  326.7 7.5 copy-start.89
  326.7 46.6 %copy-start.21 = (bf16[2,784,768]{2,1,0:T(8,128)(2,1)S(1)}, bf16[2,784,768]{2,1,0:T(8,128)(2,1)}, u32[]{:S(2)}) copy-start(bf16[2,784,768]{2,1,0:T(8,128)(2,1)} %param.21) | copy-start | bytes 7225348
  329.1 55.8 %all-to-all-start.3 = ((bf16[4,196,768]{2,1,0:T(8,128)(2,1)}), bf16[4,196,768]{2,1,0:T(8,128)(2,1)}, u32[]{:S(2)}, u32[]{:S(2)}) async-start(bf16[4,196,768]{2,1,0:T(8,128)(2,1)} %reshape.729), calls=%async_computation.3 | async-start | bytes 2457600 | tf_op jit(solution)/shard_map/all_to_all | solution.py:192
  382.6 7.0 copy-start.15
  384.9 45.7 %all-to-all-start.1 = ((bf16[4,196,768]{2,1,0:T(8,128)(2,1)}), bf16[4,196,768]{2,1,0:T(8,128)(2,1)}, u32[]{:S(2)}, u32[]{:S(2)}) async-start(bf16[4,196,768]{2,1,0:T(8,128)(2,1)} %reshape.723), calls=%async_computation.1 | async-start | bytes 2457600 | tf_op jit(solution)/shard_map/all_to_all | solution.py:192
  430.6 45.8 %all-to-all-start.6 = ((bf16[4,196,768]{2,1,0:T(8,128)(2,1)}), bf16[4,196,768]{2,1,0:T(8,128)(2,1)}, u32[]{:S(2)}, u32[]{:S(2)}) async-start(bf16[4,196,768]{2,1,0:T(8,128)(2,1)} %reshape.739), calls=%async_computation.6 | async-start | bytes 2457600 | tf_op jit(solution)/shard_map/all_to_all | solution.py:209
  476.4 30.6 %all-to-all-start.4 = ((bf16[4,196,768]{2,1,0:T(8,128)(2,1)}), bf16[4,196,768]{2,1,0:T(8,128)(2,1)}, u32[]{:S(2)}, u32[]{:S(2)}) async-start(bf16[4,196,768]{2,1,0:T(8,128)(2,1)} %reshape.731), calls=%async_computation.4 | async-start | bytes 2457600 | tf_op jit(solution)/shard_map/all_to_all | solution.py:209
  507.1 32.0 %all-to-all-start.7 = ((bf16[4,196,768]{2,1,0:T(8,128)(2,1)}), bf16[4,196,768]{2,1,0:T(8,128)(2,1)}, u32[]{:S(2)}, u32[]{:S(2)}) async-start(bf16[4,196,768]{2,1,0:T(8,128)(2,1)} %reshape.741), calls=%async_computation.7 | async-start | bytes 2457600 | tf_op jit(solution)/shard_map/all_to_all | solution.py:223
  511.3 194.0 %reduce-scatter.19.cloned.1.call-start = ((), (), s32[]{:S(2)}) async-start(), calls=%async_computation.21 | async-start | bytes 1769472
  539.1 33.4 %all-to-all-start.5 = ((bf16[4,196,768]{2,1,0:T(8,128)(2,1)}), bf16[4,196,768]{2,1,0:T(8,128)(2,1)}, u32[]{:S(2)}, u32[]{:S(2)}) async-start(bf16[4,196,768]{2,1,0:T(8,128)(2,1)} %reshape.733), calls=%async_computation.5 | async-start | bytes 2457600 | tf_op jit(solution)/shard_map/all_to_all | solution.py:223
  543.4 166.4 %reduce-scatter.17.cloned.1.call-start = ((), (), s32[]{:S(2)}) async-start(), calls=%async_computation.18 | async-start | bytes 1769472 | tf_op jit(solution)/shard_map/reduce_scatter | solution.py:88
  549.4 162.5 %all-gather.14.cloned.1.call-start = ((), (), s32[]{:S(2)}) async-start(), calls=%async_computation.19 | async-start | bytes 1536000 | tf_op jit(solution)/shard_map/all_gather | solution.py:250
  597.3 8.8 copy-start.23
  606.1 58.6 %copy-start.64 = (f32[784,4]{0,1:T(4,128)S(1)}, f32[784,4]{0,1:T(4,128)}, u32[]{:S(2)}) copy-start(f32[784,4]{0,1:T(4,128)} %copy-done.63) | copy-start | bytes 37636
  606.1 70.9 %copy-start.62 = (f32[784,4]{0,1:T(4,128)S(1)}, f32[784,4]{0,1:T(4,128)}, u32[]{:S(2)}) copy-start(f32[784,4]{0,1:T(4,128)} %copy-done.61) | copy-start | bytes 37636
  656.0 42.4 %copy-start.18 = (bf16[784,768]{1,0:T(8,128)(2,1)S(1)}, bf16[784,768]{1,0:T(8,128)(2,1)}, u32[]{:S(2)}) copy-start(bf16[784,768]{1,0:T(8,128)(2,1)} %get-tuple-element.123) | copy-start | bytes 3612676
  656.1 6.7 collective-permute-start.3
  659.4 5.5 collective-permute-start.2
  670.9 43.7 %all-gather.16.cloned.1.call-start = ((), (), s32[]{:S(2)}) async-start(), calls=%async_computation.20 | async-start | bytes 1536000 | tf_op jit(solution)/shard_map/all_gather | solution.py:250
  671.0 4.7 collective-permute-start.5
  672.3 4.8 collective-permute-start.4
  682.0 17.8 %collective-permute-start.1 = (bf16[12,768]{1,0:T(8,128)(2,1)S(1)}, bf16[12,768]{1,0:T(8,128)(2,1)S(1)}, u32[]{:S(2)}, u32[]{:S(2)}) collective-permute-start(bf16[12,768]{1,0:T(8,128)(2,1)S(1)} %slice.191), channel_id=1, source_target_pairs={{0,1},{1,2},{2,3},{4,5},{5,6},{6,7},{8,9},{9,10},{10,11},{12,13},{... | collective-permute-start | bytes 55304
  683.9 18.7 %collective-permute-start = (bf16[12,768]{1,0:T(8,128)(2,1)S(1)}, bf16[12,768]{1,0:T(8,128)(2,1)S(1)}, u32[]{:S(2)}, u32[]{:S(2)}) collective-permute-start(bf16[12,768]{1,0:T(8,128)(2,1)S(1)} %slice.190), channel_id=1, source_target_pairs={{0,1},{1,2},{2,3},{4,5},{5,6},{6,7},{8,9},{9,10},{10,11},{12,13},{... | collective-permute-start | bytes 55304
  786.4 12.0 %all-to-all-start.11 = ((bf16[8,1,96]{2,1,0:T(2,128)(2,1)}), bf16[8,1,96]{2,1,0:T(2,128)(2,1)S(1)}, u32[]{:S(2)}, u32[]{:S(2)}) async-start(bf16[8,1,96]{2,1,0:T(2,128)(2,1)} %convert_element_type.517), calls=%async_computation.11 | async-start | bytes 8192 | tf_op jit(solution)/shard_map/all_to_all | solution.py:18
  789.7 60.3 %all-reduce.35.cloned.1.call-start = ((), (), s32[]{:S(2)}) async-start(), calls=%async_computation.22 | async-start | bytes 4816896 | tf_op jit(solution)/shard_map/psum | solution.py:299
  796.2 9.5 %copy-start.74 = (f32[784]{0:T(1024)S(1)}, f32[784]{0:T(1024)}, u32[]{:S(2)}) copy-start(f32[784]{0:T(1024)} %copy-done.73) | copy-start | bytes 9412
  796.2 9.5 %copy-start.82 = (f32[784]{0:T(1024)S(1)}, f32[784]{0:T(1024)}, u32[]{:S(2)}) copy-start(f32[784]{0:T(1024)} %copy-done.81) | copy-start | bytes 9412
  798.4 18.6 %all-to-all-start.9 = ((bf16[8,192,96]{2,1,0:T(8,128)(2,1)}), bf16[8,192,96]{2,1,0:T(8,128)(2,1)S(1)}, u32[]{:S(2)}, u32[]{:S(2)}) async-start(bf16[8,192,96]{2,1,0:T(8,128)(2,1)} %bitcast.361), calls=%async_computation.9 | async-start | bytes 786432 | tf_op jit(solution)/shard_map/all_to_all | solution.py:18
  855.0 12.0 %all-to-all-start.10 = ((bf16[8,2,240]{2,1,0:T(2,128)(2,1)}), bf16[8,2,240]{2,1,0:T(2,128)(2,1)S(1)}, u32[]{:S(2)}, u32[]{:S(2)}) async-start(bf16[8,2,240]{2,1,0:T(2,128)(2,1)} %reshape.1006), calls=%async_computation.10 | async-start | bytes 16384 | tf_op jit(solution)/shard_map/all_to_all | solution.py:18
  867.0 32.6 %all-to-all-start.8 = ((bf16[8,96,3,192]{1,3,2,0:T(8,128)(2,1)}), bf16[8,96,3,192]{1,3,2,0:T(8,128)(2,1)}, u32[]{:S(2)}, u32[]{:S(2)}) async-start(bf16[8,96,3,192]{1,3,2,0:T(8,128)(2,1)} %copy.315), calls=%async_computation.8 | async-start | bytes 2359296 | tf_op jit(solution)/shard_map/all_to_all | solution.py:18
  (80 other events, 253.5 us)
Sparse Core Ops, SparseCore 0:
  122.3 35.0 all-reduce.30
  199.6 35.0 all-reduce.32
  671.0 15.0 all-gather.13
  687.5 17.7 all-gather.15
  792.8 57.2 all-reduce.34
Sparse Core Ops, SparseCore 1:
  264.8 23.2 all-gather.9
  298.8 23.3 all-gather.11
  530.2 22.0 reduce-scatter.18
  555.1 21.6 reduce-scatter.16
where the time goes:
time: 923 us; the launch traced here: 910 us
  local copies, waits for them, and re-layouts  321 us (35%)
  blocking collectives  194 us (21%)
  waiting for transfers between devices  132 us (14%)
  matrix products  85.9 us (9%)
  other arithmetic  84.6 us (9%)
  starting transfers between devices  72.8 us (8%)
  between operations  19.9 us (2%)
    unnamed x2, blocking collectives  70.5 us
    scatter x8, local copies, waits for them, and re-layouts, pack_pairs(): buffer.at[target[:, 0]].set(first_rows).at[target[:, 1]].set(second_rows)  52.9 us
    unnamed x241, local copies, waits for them, and re-layouts  46.8 us
    all_gather x1, blocking collectives, shards(): lax.all_gather(w_qkv, ('dp', 'expert'), axis=0, tiled=True)  42.7 us
    gather x4, local copies, waits for them, and re-layouts, route_slots(): ordered = jnp.concatenate([chosen[by_rank, 0], chosen[by_rank, 1]])  42.1 us
    all_gather x1, blocking collectives, shards(): lax.all_gather(w_router, ('dp', 'expert'), axis=0, tiled=True)  39 us
    gather x6, local copies, waits for them, and re-layouts, unpack_pairs(): return extended[target]  37.4 us
    psum x1, waiting for transfers between devices, shards(): lax.psum(jnp.dot(grad_proj, qkv_flat.T, preferred_element_type=jnp.float3...  32.3 us
  transfers between devices with their start and end apart: 27, of which 10 were waited for; matrix products, arithmetic and copies ran while one was open for 44% of the time, Pallas kernels for 0%

commit v1 on v0

v1 whole, which is shorter than its diff:
```python
import functools
import types

import jax
import jax.numpy as jnp
from jax import lax
from jax.experimental import pallas as pl
from jax.experimental.pallas import tpu as pltpu
from jax.sharding import PartitionSpec as P

HD = 64
SEQ = 196
MESH = pl.DeviceIdType.MESH
F32, BF16 = jnp.float32, jnp.bfloat16
LIMIT = 62 * 2**20


def up16(n):
    return -(-n // 16) * 16


def nn(a, b):
    return lax.dot_general(a, b, (((1,), (0,)), ((), ())), preferred_element_type=F32)


def nt(a, b):
    return lax.dot_general(a, b, (((1,), (1,)), ((), ())), preferred_element_type=F32)


def tn(a, b):
    return lax.dot_general(a, b, (((0,), (0,)), ((), ())), preferred_element_type=F32)


def loop(count, body):
    def step(i, carry):
        body(i)
        return carry

    lax.fori_loop(0, count, step, 0)


def iota(shape, dim):
    return lax.broadcasted_iota(jnp.int32, shape, dim)


def fiota(shape, dim):
    return iota(shape, dim).astype(F32)


def normalize(v):
    centered = v - jnp.mean(v, axis=1, keepdims=True)
    inverse = lax.rsqrt(jnp.mean(centered * centered, axis=1, keepdims=True) + 1e-06)
    return centered * inverse, inverse


def norm_backward(upstream, normed, inverse, gain):
    scaled = upstream * gain
    return inverse * (
        scaled
        - jnp.mean(scaled, axis=1, keepdims=True)
        - normed * jnp.mean(scaled * normed, axis=1, keepdims=True)
    )


class Sizes:
    def __init__(self, mesh, model, rows, hidden):
        self.nd, self.ne, self.nh = mesh.shape["dp"], mesh.shape["expert"], mesh.shape["head"]
        self.D, self.DH = model, model // 2
        self.M = rows
        self.CAP = rows // self.ne
        self.CP = up16(self.CAP + 2)
        self.IP = up16(SEQ)
        self.NI = rows // SEQ
        self.TP = self.NI * self.IP
        self.SL = self.ne * self.CP
        self.F = hidden
        self.PR = model // (self.nd * self.ne)
        self.aligned = self.PR % 16 == 0
        self.SG = 1
        while self.SG * 2 * self.CP <= self.IP and self.ne % (self.SG * 2) == 0:
            self.SG *= 2
        self.R = self.SG * 2 * self.CP
        self.LW = model // self.nh
        assert self.nd == 2 and self.nh == 4 and self.NI == 4 and self.LW == 3 * HD
        assert self.ne <= 64 and 0 <= self.CAP - (self.CP - 16) <= 14


class Place:
    def __init__(self, g):
        self.ne = g.ne
        self.d = lax.axis_index("dp")
        self.e = lax.axis_index("expert")
        self.h = lax.axis_index("head")
        self.y = lax.div(self.h, 2)
        self.c = lax.rem(self.h, 2)
        self.oy, self.oc, self.od = 1 - self.y, 1 - self.c, 1 - self.d
        self.hcore = 2 * self.y + self.oc
        self.hy = 2 * self.oy + self.c
        self.hdiag = 2 * self.oy + self.oc
        self.core = (self.d, self.e, self.hcore)
        self.across = (self.d, self.e, self.hy)
        self.diag = (self.d, self.e, self.hdiag)
        self.twin = (self.od, self.e, self.h)

    def other(self, k):
        return lax.rem(self.e + k, self.ne)

    def along(self, e2):
        return (self.d, e2, self.h)

    def enter(self):
        barrier = pltpu.get_barrier_semaphore()

        def tell(device):
            pl.semaphore_signal(barrier, inc=1, device_id=device, device_id_type=MESH)

        for device in (self.core, self.across, self.diag, self.twin):
            tell(device)
        loop(self.ne - 1, lambda k: tell(self.along(self.other(k + 1))))
        pl.semaphore_wait(barrier, 4 + self.ne - 1)


def copy(b, name, src, dst, si, ri, device):
    return pltpu.make_async_remote_copy(
        src_ref=src,
        dst_ref=dst,
        send_sem=getattr(b, name + "_s").at[si],
        recv_sem=getattr(b, name + "_r").at[ri],
        device_id=device,
        device_id_type=MESH,
    )


def send(b, name, src, dst, si, ri, device):
    copy(b, name, src, dst, si, ri, device).start()


def arrived(b, p, name, ref, ri):
    copy(b, name, ref, ref, 0, ri, p.core).wait_recv()


def left(b, p, name, ref, si):
    copy(b, name, ref, ref, si, 0, p.core).wait_send()


def route(g, p, b):
    c = p.c
    pr_row, e0r, e1r = b.mr[c, 2:3, :], b.mr[c, 0:1, :], b.mr[c, 1:2, :]
    lane = fiota((g.IP, 128), 1)
    base = jnp.zeros((1, 128), F32)
    for i in range(g.NI):
        rows = slice(i * g.IP, (i + 1) * g.IP)
        col = b.mc[c, rows, :]
        e0c, e1c, prc = col[:, 0:1], col[:, 1:2], col[:, 2:3]
        b.L[rows, :] = jnp.where(pr_row < prc, 1.0, 0.0).astype(BF16)
        b.O[rows, :] = jnp.where((lane == e0c) | (lane == e1c + 64.0), 1.0, 0.0).astype(BF16)
        base = base + jnp.sum(jnp.where(lane == e0c + 64.0, 1.0, 0.0), axis=0, keepdims=True)
    slot_lane = fiota((g.IP, g.SL), 1)
    for i in range(g.NI):
        rows = slice(i * g.IP, (i + 1) * g.IP)
        col = b.mc[c, rows, :]
        e0c, e1c = col[:, 0:1], col[:, 1:2]
        own = b.O[rows, :].astype(F32)
        earlier = nn(b.L[rows, :], b.O[...])
        s0 = jnp.sum(jnp.where(lane < 64.0, earlier * own, 0.0), axis=1, keepdims=True)
        s1 = jnp.sum(jnp.where(lane < 64.0, 0.0, (earlier + base) * own), axis=1, keepdims=True)
        t0 = jnp.where(s0 < g.CAP, e0c * g.CP + s0, -1.0)
        t1 = jnp.where(s1 < g.CAP, e1c * g.CP + s1, -1.0)
        b.PT[rows, :] = jnp.where((slot_lane == t0) | (slot_lane == t1), 1.0, 0.0).astype(BF16)
    sub = fiota((128, g.TP), 0)
    own = jnp.where((sub == e0r) | (sub == e1r + 64.0), 1.0, 0.0)
    base = jnp.sum(jnp.where(sub == e0r + 64.0, 1.0, 0.0), axis=1, keepdims=True)
    earlier = nt(own.astype(BF16), b.L[...])
    s0 = jnp.sum(jnp.where(sub < 64.0, earlier * own, 0.0), axis=0, keepdims=True)
    s1 = jnp.sum(jnp.where(sub < 64.0, 0.0, (earlier + base) * own), axis=0, keepdims=True)
    t0 = jnp.where(s0 < g.CAP, e0r * g.CP + s0, -1.0)
    t1 = jnp.where(s1 < g.CAP, e1r * g.CP + s1, -1.0)
    slot_sub = fiota((g.CP, g.TP), 0)

    def fill(e2):
        at = slot_sub + (e2 * g.CP).astype(F32)
        b.P[pl.ds(pl.multiple_of(e2 * g.CP, 16), g.CP), :] = jnp.where(
            (at == t0) | (at == t1), 1.0, 0.0
        ).astype(BF16)

    loop(g.ne, fill)


def pack_rows(g, e2):
    return pl.ds(pl.multiple_of(e2 * g.CP, 16), g.CP)


def piece_rows(g, d, e2):
    return pl.ds(pl.multiple_of((d * g.ne + e2) * g.PR, 16), g.PR)


def weights_out(g, p, b):
    own = piece_rows(g, p.d, p.e)
    if g.aligned:
        mine = p.d * g.ne + p.e

        def to_expert(k):
            device = p.along(p.other(k + 1))
            send(b, "wz", b.wp, b.W.at[p.h, own, :], k, p.e, device)
            send(b, "mz", b.mp, b.MI.at[own, :], k, p.e, device)

        loop(g.ne - 1, to_expert)
        send(b, "wx", b.wp, b.W.at[p.h, own, :], p.e, p.e, p.twin)
        send(b, "mx", b.mp, b.MI.at[own, :], p.e, p.e, p.twin)
        send(b, "wy", b.wp, b.W.at[p.h, own, :], mine, mine, p.across)
        send(b, "wc", b.wp, b.W.at[p.h, own, :], mine, mine, p.core)
        b.W[p.h, own, :] = b.wp[...]
        b.MI[own, :] = b.mp[...]
    else:
        send(b, "wy", b.wp, b.W.at[p.h], 0, 0, p.across)
        send(b, "wc", b.wp, b.W.at[p.h], 0, 0, p.core)
        b.W[p.h] = b.wp[...]
        b.MI[...] = b.mp[...]


def weights_on(g, p, b):
    if not g.aligned:
        return

    def relay(k):
        e2 = p.other(k + 1)
        rows = piece_rows(g, p.d, e2)
        at = p.d * g.ne + e2
        part = b.W.at[p.h, rows, :]
        arrived(b, p, "wz", part, e2)
        send(b, "wx", part, part, e2, e2, p.twin)
        send(b, "wy", part, part, at, at, p.across)
        send(b, "wc", part, part, at, at, p.core)
        part = b.MI.at[rows, :]
        arrived(b, p, "mz", part, e2)
        send(b, "mx", part, part, e2, e2, p.twin)

    loop(g.ne - 1, relay)


def weights_end(g, p, b):
    if not g.aligned:
        return

    def relay(k):
        e2 = p.other(k)
        rows = piece_rows(g, p.od, e2)
        at = p.od * g.ne + e2
        part = b.W.at[p.h, rows, :]
        arrived(b, p, "wx", part, e2)
        send(b, "wy", part, part, at, at, p.across)
        send(b, "wc", part, part, at, at, p.core)
        arrived(b, p, "mx", b.MI.at[rows, :], e2)

    loop(g.ne, relay)


def pieces(g):
    return g.nd * g.ne if g.aligned else 1


def piece_of(g, ref, group, i):
    if not g.aligned:
        return ref.at[group]
    return ref.at[group, pl.ds(pl.multiple_of(i * g.PR, 16), g.PR), :]


def group_in(g, p, b, k):
    @pl.when(k == 1)
    def _():
        loop(pieces(g), lambda i: arrived(b, p, "wc", piece_of(g, b.W, p.hcore, i), i))

    @pl.when(k == 2)
    def _():
        def on(i):
            part = piece_of(g, b.W, p.hy, i)
            arrived(b, p, "wy", part, i)
            send(b, "wd", part, part, i, i, p.core)

        loop(pieces(g), on)

    @pl.when(k == 3)
    def _():
        loop(pieces(g), lambda i: arrived(b, p, "wd", piece_of(g, b.W, p.hdiag, i), i))


def masks(rows):
    lane = iota((rows, 128), 1)
    return lane < 64, lane >= 64


def attention(g, p, b):
    low, high = masks(g.IP)
    live = iota((g.IP, g.IP), 1) < SEQ
    zero = jnp.zeros((g.IP, 128), BF16)

    def group(k):
        group_in(g, p, b, k)
        gi = 2 * lax.rem(p.y + lax.div(k, 2), 2) + lax.rem(p.c + k, 2)
        for blk in range(2):
            rows = slice(blk * g.IP, (blk + 1) * g.IP)
            b.QKV[gi, rows, :] = nn(b.ACT1[rows, :], b.W[gi, :, 0:640]).astype(BF16)
        for blk in range(2):
            rows = slice(blk * g.IP, (blk + 1) * g.IP)
            outs = []
            for j in range(3):
                qt = b.QKV[gi, rows, (j // 2) * 128 : (j // 2) * 128 + 128]
                kt = b.QKV[gi, rows, 384 + (j // 2) * 128 : 384 + (j // 2) * 128 + 128]
                vt = b.QKV[gi, rows, 128 + ((j + 1) // 2) * 128 : 256 + ((j + 1) // 2) * 128]
                scores = nt(jnp.where(high if j == 1 else low, qt, zero), kt) * (HD**-0.5)
                scores = jnp.where(live, scores, -1e30)
                scores = jnp.exp(scores - jnp.max(scores, axis=1, keepdims=True))
                probs = (scores / jnp.sum(scores, axis=1, keepdims=True)).astype(BF16)
                b.PB[gi, blk * 3 + j] = probs
                outs.append(nn(probs, vt))
            b.ATT[gi, rows, 0:128] = jnp.where(high, outs[0], 0.0).astype(BF16)
            b.ATT[gi, rows, 128:256] = jnp.where(low, outs[1], outs[2]).astype(BF16)
        for blk in range(2):
            rows = slice(blk * g.IP, (blk + 1) * g.IP)
            b.HID[rows, :] += nt(b.ATT[gi, rows, :], b.W[gi, :, 512:768])

    loop(4, group)


def first_norm(g, b):
    def rows16(i):
        rows = pl.ds(pl.multiple_of(i * 16, 16), 16)
        x = b.x[rows, :].astype(F32)
        normed, _ = normalize(x)
        b.ACT1[rows, :] = (normed * b.GN[0:1, :]).astype(BF16)
        b.HID[rows, :] = x

    loop(2 * g.IP // 16, rows16)


def second_norm(g, b):
    def rows16(i):
        rows = pl.ds(pl.multiple_of(i * 16, 16), 16)
        normed, _ = normalize(b.HID[rows, :])
        b.ACT2[rows, :] = (normed * b.GN[1:2, :]).astype(BF16)

    loop(2 * g.IP // 16, rows16)
    lane = iota((g.IP, 128), 1)
    for blk in range(2):
        rows = slice(blk * g.IP, (blk + 1) * g.IP)
        logits = jnp.where(lane < g.ne, nn(b.ACT2[rows, :], b.RW[...]), -1e30)
        weight = jnp.exp(logits - jnp.max(logits, axis=1, keepdims=True))
        probs = weight / jnp.sum(weight, axis=1, keepdims=True)
        b.PRB[rows, :] = probs
        top = probs.astype(BF16).astype(F32)
        rest = probs - top
        b.PRH[rows, :] = (top + pltpu.roll(rest, 64, 1)).astype(BF16)


def small_weights(g, b):
    lane = iota((g.D, 128), 1)
    small = b.MI[...].astype(F32)
    b.RW[...] = jnp.where(lane < g.ne, small, 0.0).astype(BF16)
    gains = jnp.transpose(small)[120:128, :]
    b.GN[0:1, :] = gains[0:1, :] + gains[1:2, :]
    b.GN[1:2, :] = gains[2:3, :] + gains[3:4, :]


def half_of(g, i):
    return pl.ds(pl.multiple_of(i * g.DH, 128), g.DH)


def tokens_of(g, blk):
    return pl.ds(pl.multiple_of(blk * g.IP, 16), g.IP)


def tokens_out(g, p, b):
    for at, (device, yy, cc) in enumerate(
        ((p.across, p.oy, p.c), (p.diag, p.oy, p.oc), (p.core, p.y, p.oc))
    ):
        send(b, "ta", b.ACT2.at[tokens_of(g, cc), half_of(g, yy)], b.TA.at[p.h], at, p.h, device)
        send(b, "tp", b.PRH.at[tokens_of(g, cc), :], b.TG.at[p.h], at, p.h, device)
    b.TA[p.h] = b.ACT2[tokens_of(g, p.c), half_of(g, p.y)]
    b.TG[p.h] = b.PRH[tokens_of(g, p.c), :]


def tokens_in(g, p, b):
    for src in (p.hcore, p.hy, p.hdiag):
        arrived(b, p, "ta", b.TA.at[src], src)
        arrived(b, p, "tp", b.TG.at[src], src)


def cotangent_out(g, p, b):
    def pack(k):
        e2 = p.other(k + 1)
        rows = nn(b.P[pack_rows(g, e2), :], b.up[p.c]).astype(BF16)
        b.PKU[e2] = rows
        b.UPK[e2] = b.PKU[e2, :, half_of(g, p.y)]

        @pl.when(k < g.ne - 1)
        def _():
            send(b, "uz", b.PKU.at[e2], b.US.at[p.e, p.c], k, p.e, p.along(e2))

        @pl.when(k == g.ne - 1)
        def _():
            b.US[p.e, p.c] = rows
            send(b, "uc", b.US.at[p.e, p.c], b.US.at[p.e, p.c], p.e, p.e, p.core)

    loop(g.ne, pack)


def cotangent_on(g, p, b):
    def relay(k):
        e2 = p.other(k + 1)
        part = b.US.at[e2, p.c]
        arrived(b, p, "uz", part, e2)
        send(b, "uc", part, part, e2, e2, p.core)

    loop(g.ne - 1, relay)


def slots_out(g, p, b):
    row = iota((g.CP, g.DH), 0)
    eye = row == iota((g.CP, g.DH), 1)
    lane = iota((g.CP, 128), 1)

    def pack(k):
        e2 = p.other(k + 1)
        hot = b.P[pack_rows(g, e2), :]
        tok = nn(hot, b.TA[...].reshape(g.TP, g.DH))
        gates = nn(hot, b.TG[...].reshape(g.TP, 128))
        gate = jnp.sum(
            jnp.where((lane == e2) | (lane == e2 + 64), gates, 0.0), axis=1, keepdims=True
        )
        b.GC[e2] = jnp.broadcast_to(gate, (g.CP, 128))
        across = jnp.sum(jnp.where(eye, gate, 0.0), axis=0, keepdims=True)
        top = across.astype(BF16).astype(F32)
        rows = jnp.where(row == g.CAP, top, jnp.where(row == g.CAP + 1, across - top, tok))
        rows = rows.astype(BF16)

        @pl.when(k < g.ne - 1)
        def _():
            b.PKA[e2] = rows
            send(b, "xz", b.PKA.at[e2], b.XS.at[p.e, p.c, p.y], k, p.e, p.along(e2))

        @pl.when(k == g.ne - 1)
        def _():
            part = b.XS.at[p.e, p.c, p.y]
            b.XS[p.e, p.c, p.y] = rows
            send(b, "xy", part, part, p.e, p.e, p.across)
            send(b, "xc", part, part, p.e, p.e, p.core)

    loop(g.ne, pack)


def slots_on(g, p, b):
    def relay(k):
        e2 = p.other(k + 1)
        part = b.XS.at[e2, p.c, p.y]
        arrived(b, p, "xz", part, e2)
        send(b, "xy", part, part, e2, e2, p.across)
        send(b, "xc", part, part, e2, e2, p.core)

    loop(g.ne - 1, relay)


def slots_in(g, p, b):
    def relay(k):
        e2 = p.other(k)
        part = b.XS.at[e2, p.c, p.oy]
        arrived(b, p, "xy", part, e2)
        send(b, "xd", part, part, e2, e2, p.core)

    loop(g.ne, relay)

    def rest(k):
        e2 = p.other(k)
        arrived(b, p, "xc", b.XS.at[e2, p.oc, p.y], e2)
        arrived(b, p, "xd", b.XS.at[e2, p.oc, p.oy], e2)
        arrived(b, p, "uc", b.US.at[e2, p.oc], e2)

    loop(g.ne, rest)


def experts_out(g, p, b):
    b.WI[p.d] = b.wi[...]
    b.WB[p.d] = b.wb[...]
    send(b, "ei", b.wi, b.WI.at[p.d], 0, 0, p.twin)
    send(b, "eb", b.wb, b.WB.at[p.d], 0, 0, p.twin)


def gelu_parts(u):
    inner = 0.7978845608028654 * (u + 0.044715 * u * u * u)
    tangent = jnp.tanh(inner)
    value = 0.5 * u * (1.0 + tangent)
    slope = 0.5 * (1.0 + tangent) + 0.5 * u * (1.0 - tangent * tangent) * 0.7978845608028654 * (
        1.0 + 3.0 * 0.044715 * u * u
    )
    return value, slope


def expert(g, b):
    base = g.CP - 16
    eye = iota((g.CP, g.DH), 0) == iota((g.CP, g.DH), 1)

    def sources(t):
        first = t * g.SG
        for i in range(g.SG):
            for blk in range(2):
                tail = b.XS[first + i, blk, 0, base:, :].astype(F32)
                row = tail[g.CAP - base : g.CAP - base + 1] + tail[g.CAP - base + 1 : g.CAP - base + 2]
                gate = jnp.sum(jnp.where(eye, row, 0.0), axis=1, keepdims=True)
                at = (i * 2 + blk) * g.CP
                b.GP[at : at + g.CP, :] = (b.US[first + i, blk].astype(F32) * gate).astype(BF16)
        x = [b.XS[pl.ds(first, g.SG), :, q].reshape(g.R, g.DH) for q in range(2)]
        for n in range(g.F // 256):
            cols = slice(n * 256, n * 256 + 256)
            pre = nn(x[0], b.WI[0, :, cols]) + nn(x[1], b.WI[1, :, cols])
            value, slope = gelu_parts(pre)
            b.HQ[:, cols] = value.astype(BF16)
            grad = nt(b.GP[:, : g.DH], b.WB[0, cols, :]) + nt(b.GP[:, g.DH :], b.WB[1, cols, :])
            b.GR[:, cols] = (grad * slope).astype(BF16)
        shape = (g.SG, 2, g.CP, g.DH)
        for q in range(2):
            b.PO[pl.ds(first, g.SG), :, q] = nn(b.HQ[...], b.WB[q]).astype(BF16).reshape(shape)
            b.PG[pl.ds(first, g.SG), :, q] = nt(b.GR[...], b.WI[q]).astype(BF16).reshape(shape)
            b.DB[q] += tn(b.HQ[...], b.GP[:, q * g.DH : (q + 1) * g.DH])
            b.DI[q] += tn(x[q], b.GR[...])

    b.DB[...] = jnp.zeros_like(b.DB)
    b.DI[...] = jnp.zeros_like(b.DI)
    loop(g.ne // g.SG, sources)


def first_sends_end(g, p, b):
    n = g.ne
    if g.aligned:
        own = piece_rows(g, p.d, p.e)

        def z(k):
            left(b, p, "wz", b.wp, k)
            left(b, p, "mz", b.mp, k)

        loop(n - 1, z)

        def x(k):
            left(b, p, "wx", b.wp, k)
            left(b, p, "mx", b.mp, k)

        loop(n, x)

    def w(i):
        for name in ("wy", "wc", "wd"):
            left(b, p, name, piece_of(g, b.W, p.h, i), i)

    loop(pieces(g), w)
    for at in range(3):
        left(b, p, "ta", b.TA.at[0], at)
        left(b, p, "tp", b.TG.at[0], at)

    def slots(k):
        left(b, p, "uz", b.PKU.at[0], k)
        left(b, p, "xz", b.PKA.at[0], k)

    loop(n - 1, slots)

    def on(k):
        left(b, p, "uc", b.US.at[0, 0], k)
        for name in ("xy", "xc", "xd"):
            left(b, p, name, b.XS.at[0, 0, 0], k)

    loop(n, on)
    left(b, p, "ei", b.wi, 0)
    left(b, p, "eb", b.wb, 0)


def first_kernel(g, b):
    p = Place(g)
    p.enter()
    weights_out(g, p, b)
    route(g, p, b)
    weights_on(g, p, b)
    cotangent_out(g, p, b)
    weights_end(g, p, b)
    experts_out(g, p, b)
    small_weights(g, b)
    first_norm(g, b)
    attention(g, p, b)
    second_norm(g, b)
    tokens_out(g, p, b)
    cotangent_on(g, p, b)
    tokens_in(g, p, b)
    slots_out(g, p, b)
    slots_on(g, p, b)
    slots_in(g, p, b)
    arrived(b, p, "ei", b.WI.at[p.od], 0)
    arrived(b, p, "eb", b.WB.at[p.od], 0)
    expert(g, b)
    b.KI[...] = b.DI[p.d]
    b.KB[...] = b.DB[p.d]
    b.SI[...] = b.DI[p.od].astype(BF16)
    b.SB[...] = b.DB[p.od].astype(BF16)
    first_sends_end(g, p, b)


def grads_of_expert_out(g, p, b):
    send(b, "gi", b.SI, b.XI, 0, 0, p.twin)
    send(b, "gb", b.SB, b.XB, 0, 0, p.twin)


def grads_of_expert_in(g, p, b):
    arrived(b, p, "gi", b.XI, 0)
    b.o_gi[...] = b.KI[...] + b.XI[...].astype(F32)
    arrived(b, p, "gb", b.XB, 0)
    b.o_gb[...] = b.KB[...] + b.XB[...].astype(F32)


def returns(g, p, b):
    n = g.ne
    for kind, part in enumerate((b.PO, b.PG)):

        def to_core(k, kind=kind, part=part):
            s = p.other(k + 1)
            send(b, "rc", part.at[s, p.oc], b.RC.at[kind, s], kind * n + s, kind * n + s, p.core)

        loop(n, to_core)
    for kind, part in enumerate((b.PO, b.PG)):

        def to_across(k, kind=kind, part=part):
            s = p.other(k + 1)
            at = kind * n + s
            arrived(b, p, "rc", b.RC.at[kind, s], at)
            b.RC[kind, s, p.oy] = (
                part[s, p.c, p.oy].astype(F32) + b.RC[kind, s, p.oy].astype(F32)
            ).astype(BF16)
            send(b, "ry", b.RC.at[kind, s, p.oy], b.RY.at[kind, s], at, at, p.across)

        loop(n, to_across)
    for kind, part in enumerate((b.PO, b.PG)):

        def to_source(k, kind=kind, part=part):
            s = p.other(k + 1)
            at = kind * n + s
            arrived(b, p, "ry", b.RY.at[kind, s], at)
            total = (
                part[s, p.c, p.y].astype(F32)
                + b.RC[kind, s, p.y].astype(F32)
                + b.RY[kind, s].astype(F32)
            ).astype(BF16)

            @pl.when(k < n - 1)
            def _():
                b.RC[kind, s, p.y] = total
                send(b, "rz", b.RC.at[kind, s, p.y], b.RO.at[kind, p.e], at, kind * n + p.e, p.along(s))

            @pl.when(k == n - 1)
            def _():
                b.RO[kind, p.e] = total

        loop(n, to_source)


def slots_back(g, p, b):
    n = g.ne
    lane = iota((g.CP, 128), 1)

    def rows_of(k):
        s = p.other(k)

        @pl.when(k > 0)
        def _():
            arrived(b, p, "rz", b.RO.at[0, s], s)
            arrived(b, p, "rz", b.RO.at[1, s], n + s)

        rows = pack_rows(g, s)
        out = b.RO[0, s].astype(F32)
        dots = jnp.sum(out * b.UPK[s].astype(F32), axis=1, keepdims=True)
        top = dots.astype(BF16).astype(F32)
        b.RB[rows, 0 : g.DH] = (out * b.GC[s][:, 0:1]).astype(BF16)
        b.RB[rows, g.DH : 2 * g.DH] = b.RO[1, s]
        b.RB[rows, 2 * g.DH :] = jnp.where(
            lane == s, top, jnp.where(lane == s + 64, dots - top, 0.0)
        ).astype(BF16)

    loop(n, rows_of)


def unpack(g, p, b):
    for at, (image, device) in enumerate(((p.hy, p.across), (p.hdiag, p.diag), (p.hcore, p.core))):
        rows = tokens_of(g, image)
        b.UN[at] = nn(b.PT[rows, :], b.RB[...]).astype(BF16)
        send(b, "un", b.UN.at[at], b.TR.at[p.c, p.y], at, p.h, device)
    b.TR[p.c, p.y] = nn(b.PT[tokens_of(g, p.h), :], b.RB[...]).astype(BF16)
    for hh, cc, yy in ((p.hcore, p.oc, p.y), (p.hy, p.c, p.oy), (p.hdiag, p.oc, p.oy)):
        arrived(b, p, "un", b.TR.at[cc, yy], hh)


def tokens_back(g, p, b):
    lane = iota((16, 128), 1)
    b.GA[...] = jnp.zeros_like(b.GA)

    for blk in range(2):

        def rows16(i, blk=blk):
            local = pl.ds(pl.multiple_of(i * 16, 16), 16)
            rows = pl.ds(pl.multiple_of(blk * g.IP + i * 16, 16), 16)
            hidden = b.HID[rows, :]
            for q in range(2):
                cols = slice(q * g.DH, (q + 1) * g.DH)
                b.o_mixed[rows, cols] = (
                    hidden[:, cols] + b.TR[blk, q, local, 0 : g.DH].astype(F32)
                ).astype(BF16)
            gate = b.TR[blk, 0, local, 2 * g.DH :].astype(F32) + b.TR[
                blk, 1, local, 2 * g.DH :
            ].astype(F32)
            gate = jnp.where(lane < g.ne, gate + pltpu.roll(gate, 64, 1), 0.0)
            probs = b.PRB[rows, :]
            grad = probs * (gate - jnp.sum(probs * gate, axis=1, keepdims=True))
            b.GL[rows, :] = grad.astype(BF16)

        loop(g.IP // 16, rows16)
    for blk in range(2):
        rows = slice(blk * g.IP, (blk + 1) * g.IP)
        b.GHID[rows, :] = nt(b.GL[rows, :], b.RW[...])
    for blk in range(2):

        def rows16b(i, blk=blk):
            local = pl.ds(pl.multiple_of(i * 16, 16), 16)
            rows = pl.ds(pl.multiple_of(blk * g.IP + i * 16, 16), 16)
            normed, inverse = normalize(b.HID[rows, :])
            upstream = b.GHID[rows, :] + jnp.concatenate(
                [b.TR[blk, q, local, g.DH : 2 * g.DH].astype(F32) for q in range(2)], axis=1
            )
            prod = upstream * normed
            b.GA[8:16, :] += prod[0:8, :] + prod[8:16, :]
            b.ACT2[rows, :] = (normed * b.GN[1:2, :]).astype(BF16)
            hidden = b.up[rows, :].astype(F32) + norm_backward(
                upstream, normed, inverse, b.GN[1:2, :]
            )
            b.GHID[rows, :] = hidden
            b.GHL[rows, :] = hidden.astype(BF16)
            normed, _ = normalize(b.x[rows, :].astype(F32))
            b.ACT1[rows, :] = (normed * b.GN[0:1, :]).astype(BF16)

        loop(g.IP // 16, rows16b)


def attention_back(g, p, b):
    low, high = masks(g.IP)
    zero = jnp.zeros((g.IP, 128), BF16)
    scale = HD**-0.5
    b.DA[...] = jnp.zeros_like(b.DA)

    def group(k):
        yk = lax.rem(p.oy + k, 2)
        gi = 2 * yk + lax.rem(p.oc + lax.div(k, 2), 2)
        for blk in range(2):
            rows = slice(blk * g.IP, (blk + 1) * g.IP)
            grad = nn(b.GHL[rows, :], b.W[gi, :, 512:768]).astype(BF16)
            tiles = [grad[:, 0:128], grad[:, 128:256]]
            dq, dk, dv = [], [], []
            for j in range(3):
                probs = b.PB[gi, blk * 3 + j]
                gt = tiles[(j + 1) // 2]
                qt = b.QKV[gi, rows, (j // 2) * 128 : (j // 2) * 128 + 128]
                kt = b.QKV[gi, rows, 384 + (j // 2) * 128 : 384 + (j // 2) * 128 + 128]
                vt = b.QKV[gi, rows, 128 + ((j + 1) // 2) * 128 : 256 + ((j + 1) // 2) * 128]
                grad_probs = nt(jnp.where(low if j == 1 else high, gt, zero), vt)
                wide = probs.astype(F32)
                grad_scores = wide * (
                    grad_probs - jnp.sum(wide * grad_probs, axis=1, keepdims=True)
                )
                grad_scores = (grad_scores * scale).astype(BF16)
                dv.append(tn(probs, gt))
                dq.append(nn(grad_scores, kt))
                dk.append(tn(grad_scores, qt))
            b.GJ[rows, 0:128] = jnp.where(low, dq[0], dq[1]).astype(BF16)
            b.GJ[rows, 128:256] = jnp.where(low, dq[2], dv[0]).astype(BF16)
            b.GJ[rows, 256:384] = jnp.where(low, dv[1], dv[2]).astype(BF16)
            b.GJ[rows, 384:512] = jnp.where(low, dk[0], dk[1]).astype(BF16)
            b.GJ[rows, 512:640] = jnp.where(low, dk[2], 0.0).astype(BF16)
        for blk in range(2):
            rows = slice(blk * g.IP, (blk + 1) * g.IP)
            b.DA[rows, :] += nt(b.GJ[rows, :], b.W[gi, :, 0:640])
        for m in range(g.D // 256):
            cols = slice(m * 256, m * 256 + 256)
            first = tn(b.ACT1[:, cols], b.GJ[...])
            second = tn(b.GHL[:, cols], b.ATT[gi])
            b.DW[gi, cols, 0:512] = first[:, 0:512].astype(BF16)
            b.DW[gi, cols, 512:640] = (first[:, 512:] + second[:, 0:128]).astype(BF16)
            b.DW[gi, cols, 640:768] = second[:, 128:].astype(BF16)

        @pl.when(k < 2)
        def _():
            send(b, "dc", b.DW.at[gi], b.RDC.at[yk], yk, yk, p.core)

    loop(4, group)


def inputs_back(g, p, b):
    def rows16(i):
        rows = pl.ds(pl.multiple_of(i * 16, 16), 16)
        normed, inverse = normalize(b.x[rows, :].astype(F32))
        upstream = b.DA[rows, :]
        prod = upstream * normed
        b.GA[0:8, :] += prod[0:8, :] + prod[8:16, :]
        b.GIN[rows, :] = (
            b.GHID[rows, :] + norm_backward(upstream, normed, inverse, b.GN[0:1, :])
        ).astype(BF16)

    loop(2 * g.IP // 16, rows16)
    for blk in range(2):
        part = b.GIN.at[blk * g.IP : (blk + 1) * g.IP, :]
        send(b, "iy", part, b.o_gin.at[blk, p.h], blk, blk, p.across)
        send(b, "ic", part, b.o_gin.at[blk, p.h], blk, blk, p.core)
    for blk in range(2):
        b.o_gin[blk, p.h] = b.GIN[blk * g.IP : (blk + 1) * g.IP, :]


def inputs_end(g, p, b):
    for blk in range(2):
        part = b.o_gin.at[blk, p.hy]
        arrived(b, p, "iy", part, blk)
        send(b, "id", part, part, blk, blk, p.core)
    for blk in range(2):
        arrived(b, p, "ic", b.o_gin.at[blk, p.hcore], blk)
        arrived(b, p, "id", b.o_gin.at[blk, p.hdiag], blk)


def weights_back(g, p, b):
    for i in range(2):
        rows = pl.ds(pl.multiple_of(i * g.DH, 16), g.DH)
        if i == 0:
            arrived(b, p, "dc", b.RDC.at[p.oy], p.oy)
        b.DW[p.hy, rows, :] = (b.DW[p.hy, rows, :].astype(F32) + b.RDC[p.oy, rows, :].astype(F32)).astype(BF16)
        send(b, "dy", b.DW.at[p.hy, rows, :], b.RDY.at[rows, :], i, i, p.across)


def weights_back_on(g, p, b):
    arrived(b, p, "dc", b.RDC.at[p.y], p.y)

    def total(rows):
        return (
            b.DW[p.h, rows, :].astype(F32)
            + b.RDC[p.y, rows, :].astype(F32)
            + b.RDY[rows, :].astype(F32)
        )

    for i in range(2):
        arrived(b, p, "dy", b.RDY.at[pl.ds(i * g.DH, g.DH), :], i)
    if not g.aligned:
        b.o_dw[...] = total(slice(0, g.D)).astype(BF16)
        return
    half = g.D // 2
    away = pl.ds(pl.multiple_of(p.od * half, 16), half)
    b.DW[p.h, away, :] = total(away).astype(BF16)
    send(b, "dx", b.DW.at[p.h, away, :], b.RDX, 0, 0, p.twin)
    arrived(b, p, "dx", b.RDX, 0)

    def piece(k):
        e2 = p.other(k + 1)
        local = pl.ds(pl.multiple_of(e2 * g.PR, 16), g.PR)
        mine = total(piece_rows(g, p.d, e2)) + b.RDX[local, :].astype(F32)

        @pl.when(k < g.ne - 1)
        def _():
            b.SDZ[e2] = mine.astype(BF16)
            send(b, "dz", b.SDZ.at[e2], b.RDZ.at[p.e], k, p.e, p.along(e2))

        @pl.when(k == g.ne - 1)
        def _():
            b.o_dw[...] = mine

    loop(g.ne, piece)

    def add(k):
        e2 = p.other(k + 1)
        arrived(b, p, "dz", b.RDZ.at[e2], e2)
        b.o_dw[...] += b.RDZ[e2].astype(F32)

    loop(g.ne - 1, add)


def small_back(g, p, b):
    sub = iota((128, g.D), 0)
    one = jnp.sum(b.GA[0:8, :], axis=0, keepdims=True)
    two = jnp.sum(b.GA[8:16, :], axis=0, keepdims=True)
    gains = jnp.where(sub == 120, one, jnp.where(sub == 122, two, 0.0))
    b.GM[...] = tn(b.ACT2[...], b.GL[...]) + jnp.transpose(gains)
    if g.aligned:
        half = g.D // 2
        b.SMX[...] = b.GM[pl.ds(pl.multiple_of(p.od * half, 16), half), :].astype(BF16)
        send(b, "sx", b.SMX, b.RMX, 0, 0, p.twin)


def small_back_on(g, p, b):
    if g.aligned:
        arrived(b, p, "sx", b.RMX, 0)

        def piece(k):
            e2 = p.other(k + 1)
            mine = b.GM[piece_rows(g, p.d, e2), :] + b.RMX[
                pl.ds(pl.multiple_of(e2 * g.PR, 16), g.PR), :
            ].astype(F32)

            @pl.when(k < g.ne - 1)
            def _():
                b.SMZ[e2] = mine.astype(BF16)
                send(b, "sz", b.SMZ.at[e2], b.RMZ.at[p.e], k, p.e, p.along(e2))

            @pl.when(k == g.ne - 1)
            def _():
                b.o_small[...] = mine

        loop(g.ne, piece)

        def add(k):
            e2 = p.other(k + 1)
            arrived(b, p, "sz", b.RMZ.at[e2], e2)
            b.o_small[...] += b.RMZ[e2].astype(F32)

        loop(g.ne - 1, add)
    else:
        b.o_small[...] = b.GM[...]
    b.SMC[...] = b.o_small[...].astype(BF16)
    send(b, "sc", b.SMC, b.RMC, 0, 0, p.core)
    arrived(b, p, "sc", b.RMC, 0)
    b.SMY[...] = (b.SMC[...].astype(F32) + b.RMC[...].astype(F32)).astype(BF16)
    send(b, "sy", b.SMY, b.RMY, 0, 0, p.across)
    arrived(b, p, "sy", b.RMY, 0)
    b.o_small[...] = b.SMY[...].astype(F32) + b.RMY[...].astype(F32)


def second_sends_end(g, p, b):
    n = g.ne
    left(b, p, "gi", b.SI, 0)
    left(b, p, "gb", b.SB, 0)

    def rets(k):
        left(b, p, "rc", b.RC.at[0, 0], k)
        left(b, p, "ry", b.RY.at[0, 0], k)

    loop(2 * n, rets)

    def away(k):
        s = p.other(k + 1)
        left(b, p, "rz", b.RY.at[0, 0], s)
        left(b, p, "rz", b.RY.at[0, 0], n + s)
        if g.aligned:
            left(b, p, "dz", b.SDZ.at[0], k)
            left(b, p, "sz", b.SMZ.at[0], k)

    loop(n - 1, away)
    for at in range(3):
        left(b, p, "un", b.UN.at[0], at)
    for i in range(2):
        left(b, p, "dc", b.RDC.at[0], i)
        left(b, p, "dy", b.RDY.at[pl.ds(0, g.DH), :], i)
        for name in ("iy", "ic", "id"):
            left(b, p, name, b.o_gin.at[0, 0], i)
    if g.aligned:
        left(b, p, "dx", b.RDX, 0)
        left(b, p, "sx", b.SMX, 0)
    left(b, p, "sc", b.SMC, 0)
    left(b, p, "sy", b.SMY, 0)


def second_kernel(g, b):
    p = Place(g)
    p.enter()
    returns(g, p, b)
    grads_of_expert_out(g, p, b)
    slots_back(g, p, b)
    unpack(g, p, b)
    tokens_back(g, p, b)
    attention_back(g, p, b)
    inputs_back(g, p, b)
    small_back(g, p, b)
    weights_back(g, p, b)
    inputs_end(g, p, b)
    weights_back_on(g, p, b)
    small_back_on(g, p, b)
    grads_of_expert_in(g, p, b)
    second_sends_end(g, p, b)


def call(body, g, inputs, outs, scratch, sems, number, flops):
    names = [*inputs, *outs, *scratch]
    names += [name + end for name in sems for end in ("_s", "_r")]

    def kernel(*refs):
        body(g, types.SimpleNamespace(**dict(zip(names, refs, strict=True))))

    vmem = pl.BlockSpec(memory_space=pltpu.VMEM)
    made = pl.pallas_call(
        kernel,
        out_shape=[jax.ShapeDtypeStruct(*o) for o in outs.values()],
        in_specs=[vmem] * len(inputs),
        out_specs=[vmem] * len(outs),
        scratch_shapes=[pltpu.VMEM(*s) for s in scratch.values()]
        + [pltpu.SemaphoreType.DMA((n,)) for n in sems.values() for _ in range(2)],
        compiler_params=pltpu.CompilerParams(
            collective_id=number, has_side_effects=True, vmem_limit_bytes=LIMIT
        ),
        cost_estimate=pl.CostEstimate(flops=flops, bytes_accessed=2**24, transcendentals=0),
    )(*inputs.values())
    return dict(zip(outs, made, strict=True))


def shards(
    inputs, w_qkv, w_out, w_router, gain_one, gain_two, w_in, w_back, experts, priority, cotangent, *, mesh
):
    model, rows = inputs.shape[2], inputs.shape[1]
    g = Sizes(mesh, model, rows, w_in.shape[2])
    n, ip, cp, dh = g.ne, g.IP, g.CP, g.DH
    assert inputs.shape[0] == 2
    h = lax.axis_index("head")
    pad = ((0, 0), (0, 0), (0, ip - SEQ), (0, 0))
    x_all = inputs.reshape(2, g.NI, SEQ, model)
    x = jnp.pad(lax.dynamic_slice_in_dim(x_all, h, 1, 1), pad).reshape(2 * ip, model)
    up_all = jnp.pad(cotangent.reshape(2, g.NI, SEQ, model), pad)
    up_own = lax.dynamic_slice_in_dim(up_all, h, 1, 1).reshape(2 * ip, model)
    part = jnp.concatenate([w_qkv[:, 0], w_qkv[:, 2], w_qkv[:, 1], w_out.T], axis=1)
    gains = jnp.stack([gain_one, gain_two], axis=1)
    top = gains.astype(BF16)
    rest = (gains - top.astype(F32)).astype(BF16)
    small = jnp.concatenate(
        [
            w_router,
            jnp.zeros((w_router.shape[0], 120 - n), BF16),
            top[:, :1],
            rest[:, :1],
            top[:, 1:],
            rest[:, 1:],
            jnp.zeros((w_router.shape[0], 4), BF16),
        ],
        axis=1,
    )
    if not g.aligned:
        part = lax.all_gather(part, ("dp", "expert"), axis=0, tiled=True)
        small = lax.all_gather(small, ("dp", "expert"), axis=0, tiled=True)
    info = jnp.concatenate([experts, priority[:, :, None]], axis=2).astype(F32)
    info = jnp.pad(info.reshape(2, g.NI, SEQ, 3), pad, constant_values=-1000.0)
    mc = jnp.pad(info.reshape(2, g.TP, 3), ((0, 0), (0, 0), (0, 5)))
    mr = jnp.swapaxes(mc, 1, 2)
    np_ = pieces(g)
    one = call(
        first_kernel,
        g,
        dict(x=x, up=up_all.reshape(2, g.TP, model), wp=part, mp=small, wi=w_in[0], wb=w_back[0], mc=mc, mr=mr),
        dict(
            W=((4, model, model), BF16),
            RW=((model, 128), BF16),
            GN=((8, model), F32),
            QKV=((4, 2 * ip, 640), BF16),
            PB=((4, 6, ip, ip), BF16),
            ATT=((4, 2 * ip, 256), BF16),
            HID=((2 * ip, model), F32),
            PRB=((2 * ip, 128), F32),
            PT=((g.TP, g.SL), BF16),
            UPK=((n, cp, dh), BF16),
            GC=((n, cp, 128), F32),
            PO=((n, 2, 2, cp, dh), BF16),
            PG=((n, 2, 2, cp, dh), BF16),
            KI=((dh, g.F), F32),
            KB=((g.F, dh), F32),
            SI=((dh, g.F), BF16),
            SB=((g.F, dh), BF16),
        ),
        dict(
            DI=((2, dh, g.F), F32),
            DB=((2, g.F, dh), F32),
            MI=((model, 128), BF16),
            L=((g.TP, g.TP), BF16),
            O=((g.TP, 128), BF16),
            P=((g.SL, g.TP), BF16),
            ACT1=((2 * ip, model), BF16),
            ACT2=((2 * ip, model), BF16),
            PRH=((2 * ip, 128), BF16),
            TA=((4, ip, dh), BF16),
            TG=((4, ip, 128), BF16),
            US=((n, 2, cp, model), BF16),
            XS=((n, 2, 2, cp, dh), BF16),
            PKA=((n, cp, dh), BF16),
            PKU=((n, cp, model), BF16),
            WI=((2, dh, g.F), BF16),
            WB=((2, g.F, dh), BF16),
            GP=((g.R, model), BF16),
            HQ=((g.R, g.F), BF16),
            GR=((g.R, g.F), BF16),
        ),
        dict(wz=n, mz=n, wx=n, mx=n, wy=np_, wc=np_, wd=np_, ta=4, tp=4, uz=n, uc=n, xz=n, xy=n, xc=n, xd=n, ei=1, eb=1),
        1,
        14 * 10**9,
    )
    keep = ("W", "RW", "GN", "QKV", "PB", "ATT", "HID", "PRB", "PT", "UPK", "GC", "PO", "PG", "KI", "KB", "SI", "SB")
    rows_out = g.PR if g.aligned else model
    extra = (
        dict(
            RDX=((model // 2, model), BF16),
            SDZ=((n, g.PR, model), BF16),
            RDZ=((n, g.PR, model), BF16),
            SMX=((model // 2, 128), BF16),
            RMX=((model // 2, 128), BF16),
            SMZ=((n, g.PR, 128), BF16),
            RMZ=((n, g.PR, 128), BF16),
        )
        if g.aligned
        else {}
    )
    two = call(
        second_kernel,
        g,
        dict(x=x, up=up_own, **{name: one[name] for name in keep}),
        dict(
            o_mixed=((2 * ip, model), BF16),
            o_gin=((2, 4, ip, model), BF16),
            o_dw=((rows_out, model), F32 if g.aligned else BF16),
            o_small=((rows_out, 128), F32),
            o_gi=((dh, g.F), F32),
            o_gb=((g.F, dh), F32),
        ),
        dict(
            RC=((2, n, 2, cp, dh), BF16),
            RY=((2, n, cp, dh), BF16),
            RO=((2, n, cp, dh), BF16),
            RB=((g.SL, 2 * dh + 128), BF16),
            UN=((3, ip, 2 * dh + 128), BF16),
            TR=((2, 2, ip, 2 * dh + 128), BF16),
            GL=((2 * ip, 128), BF16),
            GA=((16, model), F32),
            ACT1=((2 * ip, model), BF16),
            ACT2=((2 * ip, model), BF16),
            GHID=((2 * ip, model), F32),
            GHL=((2 * ip, model), BF16),
            DA=((2 * ip, model), F32),
            GJ=((2 * ip, 640), BF16),
            DW=((4, model, model), BF16),
            RDC=((2, model, model), BF16),
            RDY=((model, model), BF16),
            GIN=((2 * ip, model), BF16),
            GM=((model, 128), F32),
            SMC=((rows_out, 128), BF16),
            RMC=((rows_out, 128), BF16),
            SMY=((rows_out, 128), BF16),
            RMY=((rows_out, 128), BF16),
            XI=((dh, g.F), BF16),
            XB=((g.F, dh), BF16),
            **extra,
        ),
        dict(rc=2 * n, ry=2 * n, rz=2 * n, un=4, gi=1, gb=1, dc=2, dy=2, dx=1, dz=n, sx=1, sz=n, sc=1, sy=1, iy=2, ic=2, id=2),
        2,
        14 * 10**9,
    )
    mixed = two["o_mixed"].reshape(2, ip, model)[:, :SEQ]
    grad_inputs = two["o_gin"][:, :, :SEQ].reshape(2, rows, model)
    dw, ds = two["o_dw"], two["o_small"]
    if not g.aligned:
        dw = lax.psum_scatter(dw, ("dp", "expert"), scatter_dimension=0, tiled=True)
        ds = lax.psum_scatter(ds.astype(BF16), ("dp", "expert"), scatter_dimension=0, tiled=True)
        dw, ds = dw.astype(F32), ds.astype(F32)
    lw = g.LW
    grad_qkv = jnp.stack([dw[:, :lw], dw[:, 2 * lw : 3 * lw], dw[:, lw : 2 * lw]], axis=1)
    return (
        mixed,
        grad_inputs,
        grad_qkv,
        dw[:, 3 * lw :].T,
        ds[:, :n],
        ds[:, 120],
        ds[:, 122],
        two["o_gi"][None],
        two["o_gb"][None],
    )


def solution(mesh):
    both = ("dp", "expert")
    in_specs = (
        P(both, None, None),
        P(both, None, "head"),
        P("head", both),
        P(both, None),
        P(both),
        P(both),
        P("expert", "dp", "head"),
        P("expert", "head", "dp"),
        P(both, None, None),
        P(both, None),
        P(both, None, None),
    )
    out_specs = (
        P(both, "head", None),
        P(both, None, None),
        P(both, None, "head"),
        P("head", both),
        P(both, None),
        P(both),
        P(both),
        P("expert", "dp", "head"),
        P("expert", "head", "dp"),
    )
    return jax.shard_map(
        functools.partial(shards, mesh=mesh),
        mesh=mesh,
        in_specs=in_specs,
        out_specs=out_specs,
        check_vma=False,
    )
```

time: 923 us -> 335 us (0.36); the launches traced: 910 us -> 334 us
  Pallas kernels: 0 us -> 302 us
  local copies, waits for them, and re-layouts: 321 us -> 28.2 us
  blocking collectives: 194 us -> 0 us
  waiting for transfers between devices: 132 us -> 0 us
  matrix products: 85.9 us -> 0 us
  other arithmetic: 84.6 us -> 2.87 us
  starting transfers between devices: 72.8 us -> 0 us
  between operations: 19.9 us -> 0.78 us
    pallas_call x0 -> x2, Pallas kernels: none -> 302 us  [call(): pl.pallas_call(kernel, out_shape=[jax.ShapeDtypeStruct(*o) for o in outs....]
    all_gather x5 -> x0, blocking collectives: 123 us -> none  [the longest x1 42.7 us: shards(): lax.all_gather(w_qkv, ('dp', 'expert'), axis=0, tiled=True)]
    gather x14 -> x0, local copies, waits for them, and re-layouts: 99 us -> none  [the longest x4 42.1 us: route_slots(): ordered = jnp.concatenate([chosen[by_rank, 0], chosen[by_rank, 1]])]
    dot_general x42 -> x0, matrix products: 85.9 us -> none  [the longest x2 8.3 us: shards(): jnp.dot(grad_arrived, second_w.T, preferred_element_type=jnp.float32)]
    unnamed x2 -> x0, blocking collectives: 70.5 us -> none
    scatter x10 -> x0, local copies, waits for them, and re-layouts: 63.6 us -> none  [the longest x8 52.9 us: pack_pairs(): buffer.at[target[:, 0]].set(first_rows).at[target[:, 1]].set(second_rows)]
    all_to_all x12 -> x0, waiting for transfers between devices: 63.5 us -> none  [the longest x4 29.4 us: sent_and_summed(): lax.all_to_all(pieces, axis, split_axis=0, concat_axis=0, tiled=True)]
    all_to_all x12 -> x0, starting transfers between devices: 56.4 us -> none  [the longest x4 18.9 us: sent_and_summed(): lax.all_to_all(pieces, axis, split_axis=0, concat_axis=0, tiled=True)]
  transfers between devices with their start and end apart: 27 -> 0, of which waited for: 10 -> 0; matrix products, arithmetic and copies ran while one was open for 44% -> 0% of each run, Pallas kernels for 0% -> 0%
where the time goes in v1:
time: 335 us; the launch traced here: 334 us
  Pallas kernels  302 us (90%)
  local copies, waits for them, and re-layouts  28.2 us (8%)
    pallas_call x2, Pallas kernels, call(): pl.pallas_call(kernel, out_shape=[jax.ShapeDtypeStruct(*o) for o in outs....  302 us
    unnamed x14, local copies, waits for them, and re-layouts  8.16 us

profile of v1, /device:TPU:0, one launch (start us, length us, event | category | flops | bytes accessed | tf_op | source)
XLA Modules:
  0.0 334.1 jit_solution(1519594069645793140)
XLA Ops:
  0.6 0.7 subtract_convert_fusion
  1.3 0.7 fusion
  2.0 0.8 concatenate.17
  2.8 0.8 concatenate.16
  3.6 0.1 reshape.51
  3.8 0.1 copy.59
  3.9 0.1 copy.58
  4.0 0.1 copy.57
  4.1 0.1 copy.56
  4.3 0.8 copy.55
  5.1 0.7 concatenate.15.refs_3_
  5.8 0.9 copy.54
  6.7 0.6 pad_bitcast_fusion.refs_7_
  7.3 0.9 slice_bitcast_fusion.6
  8.2 0.8 pad_maximum_fusion.1.refs_2_
  9.0 0.3 copy.67
  9.3 1.0 pad.19.clone.refs_6_
  10.2 2.6 reshape.48
  12.9 0.9 constant_dynamic-slice_fusion
  13.8 1.7 pad.17
  15.4 2.6 reshape.46
  18.1 0.9 pad.16
  19.0 114.9 %shard_map.178 = (bf16[4,768,768]{2,1,0:T(8,128)(2,1)}, bf16[768,128]{1,0:T(8,128)(2,1)}, f32[8,768]{1,0:T(8,128)}, bf16[4,416,640]{2,1,0:T(8,128)(2,1)}, bf16[4...) custom-call(bf16[416,768]{1,0:T(8,128)(2,1)} %bitcast.36, ...), custom_call_target="tpu_custom_call" | custom-call | flops 14000000000 | bytes 16777216 | tf_op jit(solution)/shard_map/pallas_call | solution.py:990
  133.9 187.3 %shard_map.179 = (bf16[416,768]{1,0:T(8,128)(2,1)}, bf16[2,4,208,768]{3,2,1,0:T(8,128)(2,1)}, f32[96,768]{1,0:T(8,128)}, f32[96,128]{1,0:T(8,128)}, f32[384,768]{1,0:T(8,128)}, /*index=5*/f32[768,384]{1,0:T(8,128)}) custom-call(bf16[416,768]{1,0:T(8,128)(2,1)} %bitcast.37, bf16[416,768]{1,0:T(8,128)(2,1)} %bitcast.35, ...), custom_call_target="tpu_custom_call" | custom-call | flops 14000000000 | bytes 16777216 | tf_op jit(solution)/shard_map/pallas_call | solution.py:990
  321.3 0.0 copy-start.2
  321.3 0.0 copy-start.1
  321.3 1.2 slice.64
  322.5 1.3 copy.66
  323.8 0.0 copy-done.2
  323.8 0.7 slice_reduce_fusion
  324.5 0.7 copy.65
  325.1 0.0 copy-done.1
  325.1 0.1 slice_bitcast_fusion
  325.2 0.7 copy.64
  326.0 0.7 pad_maximum_fusion
  326.7 1.9 slice.56
  328.6 2.1 reshape.53
  330.7 0.0 copy-start
  330.7 2.5 copy.72
  333.1 0.0 copy-done
  333.1 1.0 copy.73
  (8 shorter events, 0.1 us)
Async XLA Ops:
  321.3 2.5 copy-start.2
  321.3 3.8 %copy-start.1 = (f32[96,768]{1,0:T(8,128)S(1)}, f32[96,768]{1,0:T(8,128)}, u32[]{:S(2)}) copy-start(f32[96,768]{1,0:T(8,128)} %get-tuple-element.51) | copy-start | bytes 884740
  330.7 2.5 copy-start

commit v2 on v1

--- a/solution.py
+++ b/solution.py
@@ -12,7 +12,7 @@
 SEQ = 196
 MESH = pl.DeviceIdType.MESH
 F32, BF16 = jnp.float32, jnp.bfloat16
-LIMIT = 62 * 2**20
+LIMIT = 63 * 2**20
 
 
 def up16(n):
@@ -322,24 +322,32 @@
     loop(4, group)
 
 
+def rows16s(count, body):
+    run = count // 32
+
+    def step(i):
+        for j in range(run):
+            body(pl.ds(pl.multiple_of((i * run + j) * 16, 16), 16))
+
+    loop(2, step)
+
+
 def first_norm(g, b):
-    def rows16(i):
-        rows = pl.ds(pl.multiple_of(i * 16, 16), 16)
+    def rows16(rows):
         x = b.x[rows, :].astype(F32)
         normed, _ = normalize(x)
         b.ACT1[rows, :] = (normed * b.GN[0:1, :]).astype(BF16)
         b.HID[rows, :] = x
 
-    loop(2 * g.IP // 16, rows16)
+    rows16s(2 * g.IP, rows16)
 
 
 def second_norm(g, b):
-    def rows16(i):
-        rows = pl.ds(pl.multiple_of(i * 16, 16), 16)
+    def rows16(rows):
         normed, _ = normalize(b.HID[rows, :])
         b.ACT2[rows, :] = (normed * b.GN[1:2, :]).astype(BF16)
 
-    loop(2 * g.IP // 16, rows16)
+    rows16s(2 * g.IP, rows16)
     lane = iota((g.IP, 128), 1)
     for blk in range(2):
         rows = slice(blk * g.IP, (blk + 1) * g.IP)
@@ -390,7 +398,6 @@
         e2 = p.other(k + 1)
         rows = nn(b.P[pack_rows(g, e2), :], b.up[p.c]).astype(BF16)
         b.PKU[e2] = rows
-        b.UPK[e2] = b.PKU[e2, :, half_of(g, p.y)]
 
         @pl.when(k < g.ne - 1)
         def _():
@@ -448,33 +455,23 @@
     loop(g.ne, pack)
 
 
-def slots_on(g, p, b):
-    def relay(k):
-        e2 = p.other(k + 1)
-        part = b.XS.at[e2, p.c, p.y]
-        arrived(b, p, "xz", part, e2)
-        send(b, "xy", part, part, e2, e2, p.across)
-        send(b, "xc", part, part, e2, e2, p.core)
-
-    loop(g.ne - 1, relay)
-
-
-def slots_in(g, p, b):
-    def relay(k):
-        e2 = p.other(k)
-        part = b.XS.at[e2, p.c, p.oy]
-        arrived(b, p, "xy", part, e2)
-        send(b, "xd", part, part, e2, e2, p.core)
-
-    loop(g.ne, relay)
-
-    def rest(k):
-        e2 = p.other(k)
-        arrived(b, p, "xc", b.XS.at[e2, p.oc, p.y], e2)
-        arrived(b, p, "xd", b.XS.at[e2, p.oc, p.oy], e2)
-        arrived(b, p, "uc", b.US.at[e2, p.oc], e2)
-
-    loop(g.ne, rest)
+def slots_on(g, p, b, e2):
+    part = b.XS.at[e2, p.c, p.y]
+    arrived(b, p, "xz", part, e2)
+    send(b, "xy", part, part, e2, e2, p.across)
+    send(b, "xc", part, part, e2, e2, p.core)
+
+
+def slots_over(g, p, b, e2):
+    part = b.XS.at[e2, p.c, p.oy]
+    arrived(b, p, "xy", part, e2)
+    send(b, "xd", part, part, e2, e2, p.core)
+
+
+def slots_in(g, p, b, e2):
+    arrived(b, p, "xc", b.XS.at[e2, p.oc, p.y], e2)
+    arrived(b, p, "xd", b.XS.at[e2, p.oc, p.oy], e2)
+    arrived(b, p, "uc", b.US.at[e2, p.oc], e2)
 
 
 def experts_out(g, p, b):
@@ -494,37 +491,78 @@
     return value, slope
 
 
-def expert(g, b):
+def expert(g, b, first):
     base = g.CP - 16
-    eye = iota((g.CP, g.DH), 0) == iota((g.CP, g.DH), 1)
-
-    def sources(t):
-        first = t * g.SG
+    row = iota((g.CP, g.DH), 0)
+    eye = row == iota((g.CP, g.DH), 1)
+    for i in range(g.SG):
+        for blk in range(2):
+            tail = b.XS[first + i, blk, 0, base:, :].astype(F32)
+            gate = tail[g.CAP - base : g.CAP - base + 1] + tail[g.CAP - base + 1 : g.CAP - base + 2]
+            gate = jnp.sum(jnp.where(eye, gate, 0.0), axis=1, keepdims=True)
+            at = (i * 2 + blk) * g.CP
+            b.GP[at : at + g.CP, :] = (b.US[first + i, blk].astype(F32) * gate).astype(BF16)
+    x = [b.XS[pl.ds(first, g.SG), :, q].reshape(g.R, g.DH) for q in range(2)]
+    for n in range(g.F // 256):
+        cols = slice(n * 256, n * 256 + 256)
+        pre = nn(x[0], b.WI[0, :, cols]) + nn(x[1], b.WI[1, :, cols])
+        value, slope = gelu_parts(pre)
+        b.HQ[:, cols] = value.astype(BF16)
+        grad = nt(b.GP[:, : g.DH], b.WB[0, cols, :]) + nt(b.GP[:, g.DH :], b.WB[1, cols, :])
+        b.GR[:, cols] = (grad * slope).astype(BF16)
+    shape = (g.SG, 2, g.CP, g.DH)
+    dots = []
+    for q in range(2):
+        out = nn(b.HQ[...], b.WB[q]).astype(BF16)
+        b.PO[pl.ds(first, g.SG), :, q] = out.reshape(shape)
+        up = b.US[pl.ds(first, g.SG), :, :, q * g.DH : (q + 1) * g.DH].reshape(g.R, g.DH)
+        dots.append(jnp.sum(out.astype(F32) * up.astype(F32), axis=1, keepdims=True))
+        b.DB[q] += tn(b.HQ[...], b.GP[:, q * g.DH : (q + 1) * g.DH])
+        b.DI[q] += tn(x[q], b.GR[...])
+    dots = dots[0] + dots[1]
+    for q in range(2):
+        back = nt(b.GR[...], b.WI[q])
         for i in range(g.SG):
             for blk in range(2):
-                tail = b.XS[first + i, blk, 0, base:, :].astype(F32)
-                row = tail[g.CAP - base : g.CAP - base + 1] + tail[g.CAP - base + 1 : g.CAP - base + 2]
-                gate = jnp.sum(jnp.where(eye, row, 0.0), axis=1, keepdims=True)
                 at = (i * 2 + blk) * g.CP
-                b.GP[at : at + g.CP, :] = (b.US[first + i, blk].astype(F32) * gate).astype(BF16)
-        x = [b.XS[pl.ds(first, g.SG), :, q].reshape(g.R, g.DH) for q in range(2)]
-        for n in range(g.F // 256):
-            cols = slice(n * 256, n * 256 + 256)
-            pre = nn(x[0], b.WI[0, :, cols]) + nn(x[1], b.WI[1, :, cols])
-            value, slope = gelu_parts(pre)
-            b.HQ[:, cols] = value.astype(BF16)
-            grad = nt(b.GP[:, : g.DH], b.WB[0, cols, :]) + nt(b.GP[:, g.DH :], b.WB[1, cols, :])
-            b.GR[:, cols] = (grad * slope).astype(BF16)
-        shape = (g.SG, 2, g.CP, g.DH)
-        for q in range(2):
-            b.PO[pl.ds(first, g.SG), :, q] = nn(b.HQ[...], b.WB[q]).astype(BF16).reshape(shape)
-            b.PG[pl.ds(first, g.SG), :, q] = nt(b.GR[...], b.WI[q]).astype(BF16).reshape(shape)
-            b.DB[q] += tn(b.HQ[...], b.GP[:, q * g.DH : (q + 1) * g.DH])
-            b.DI[q] += tn(x[q], b.GR[...])
-
+                along = jnp.sum(jnp.where(eye, dots[at : at + g.CP], 0.0), axis=0, keepdims=True)
+                if q == 1:
+                    along = along - along.astype(BF16).astype(F32)
+                b.PG[first + i, blk, q] = jnp.where(
+                    row == g.CAP, along, back[at : at + g.CP]
+                ).astype(BF16)
+
+
+def experts(g, p, b):
     b.DB[...] = jnp.zeros_like(b.DB)
     b.DI[...] = jnp.zeros_like(b.DI)
-    loop(g.ne // g.SG, sources)
+    n = g.ne
+    if g.SG > 1:
+        loop(n - 1, lambda k: slots_on(g, p, b, p.other(k + 1)))
+        loop(n, lambda k: slots_over(g, p, b, p.other(k)))
+        loop(n, lambda k: slots_in(g, p, b, p.other(k)))
+        arrived(b, p, "ei", b.WI.at[p.od], 0)
+        arrived(b, p, "eb", b.WB.at[p.od], 0)
+        loop(n // g.SG, lambda t: expert(g, b, t * g.SG))
+        return
+    slots_over(g, p, b, p.e)
+    slots_in(g, p, b, p.e)
+    arrived(b, p, "ei", b.WI.at[p.od], 0)
+    arrived(b, p, "eb", b.WB.at[p.od], 0)
+
+    def source(k):
+        @pl.when(k == 1)
+        def _():
+            loop(n - 1, lambda i: slots_on(g, p, b, p.other(i + 1)))
+
+        @pl.when(k > 0)
+        def _():
+            slots_over(g, p, b, p.other(k))
+            slots_in(g, p, b, p.other(k))
+
+        expert(g, b, p.other(k))
+
+    loop(n, source)
 
 
 def first_sends_end(g, p, b):
@@ -586,11 +624,7 @@
     cotangent_on(g, p, b)
     tokens_in(g, p, b)
     slots_out(g, p, b)
-    slots_on(g, p, b)
-    slots_in(g, p, b)
-    arrived(b, p, "ei", b.WI.at[p.od], 0)
-    arrived(b, p, "eb", b.WB.at[p.od], 0)
-    expert(g, b)
+    experts(g, p, b)
     b.KI[...] = b.DI[p.d]
     b.KB[...] = b.DB[p.d]
     b.SI[...] = b.DI[p.od].astype(BF16)
@@ -610,134 +644,143 @@
     b.o_gb[...] = b.KB[...] + b.XB[...].astype(F32)
 
 
-def returns(g, p, b):
+def part_of(b, kind):
+    return b.PG if kind else b.PO
+
+
+def returns_start(g, p, b, kind):
+    def to_core(k):
+        s = p.other(k + 1)
+        at = kind * g.ne + s
+        send(b, "rc", part_of(b, kind).at[s, p.oc], b.RC.at[kind, s], at, at, p.core)
+
+    loop(g.ne, to_core)
+
+
+def returns_over(g, p, b, kind):
+    def to_across(k):
+        s = p.other(k + 1)
+        at = kind * g.ne + s
+        arrived(b, p, "rc", b.RC.at[kind, s], at)
+        b.RC[kind, s, p.oy] = (
+            part_of(b, kind)[s, p.c, p.oy].astype(F32) + b.RC[kind, s, p.oy].astype(F32)
+        ).astype(BF16)
+        send(b, "ry", b.RC.at[kind, s, p.oy], b.RY.at[kind, s], at, at, p.across)
+
+    loop(g.ne, to_across)
+
+
+def returns_on(g, p, b, kind):
     n = g.ne
-    for kind, part in enumerate((b.PO, b.PG)):
-
-        def to_core(k, kind=kind, part=part):
-            s = p.other(k + 1)
-            send(b, "rc", part.at[s, p.oc], b.RC.at[kind, s], kind * n + s, kind * n + s, p.core)
-
-        loop(n, to_core)
-    for kind, part in enumerate((b.PO, b.PG)):
-
-        def to_across(k, kind=kind, part=part):
-            s = p.other(k + 1)
-            at = kind * n + s
-            arrived(b, p, "rc", b.RC.at[kind, s], at)
-            b.RC[kind, s, p.oy] = (
-                part[s, p.c, p.oy].astype(F32) + b.RC[kind, s, p.oy].astype(F32)
-            ).astype(BF16)
-            send(b, "ry", b.RC.at[kind, s, p.oy], b.RY.at[kind, s], at, at, p.across)
-
-        loop(n, to_across)
-    for kind, part in enumerate((b.PO, b.PG)):
-
-        def to_source(k, kind=kind, part=part):
-            s = p.other(k + 1)
-            at = kind * n + s
-            arrived(b, p, "ry", b.RY.at[kind, s], at)
-            total = (
-                part[s, p.c, p.y].astype(F32)
-                + b.RC[kind, s, p.y].astype(F32)
-                + b.RY[kind, s].astype(F32)
-            ).astype(BF16)
-
-            @pl.when(k < n - 1)
-            def _():
-                b.RC[kind, s, p.y] = total
-                send(b, "rz", b.RC.at[kind, s, p.y], b.RO.at[kind, p.e], at, kind * n + p.e, p.along(s))
-
-            @pl.when(k == n - 1)
-            def _():
-                b.RO[kind, p.e] = total
-
-        loop(n, to_source)
-
-
-def slots_back(g, p, b):
+
+    def to_source(k):
+        s = p.other(k + 1)
+        at = kind * n + s
+        arrived(b, p, "ry", b.RY.at[kind, s], at)
+        total = (
+            part_of(b, kind)[s, p.c, p.y].astype(F32)
+            + b.RC[kind, s, p.y].astype(F32)
+            + b.RY[kind, s].astype(F32)
+        ).astype(BF16)
+
+        @pl.when(k < n - 1)
+        def _():
+            b.RC[kind, s, p.y] = total
+            send(b, "rz", b.RC.at[kind, s, p.y], b.RO.at[kind, p.e], at, kind * n + p.e, p.along(s))
+
+        @pl.when(k == n - 1)
+        def _():
+            b.RO[kind, p.e] = total
+
+    loop(n, to_source)
+
+
+def slots_back(g, p, b, kind):
     n = g.ne
     lane = iota((g.CP, 128), 1)
+    base = g.CP - 16
+    eye = iota((g.CP, g.DH), 0) == iota((g.CP, g.DH), 1)
 
     def rows_of(k):
         s = p.other(k)
 
         @pl.when(k > 0)
         def _():
-            arrived(b, p, "rz", b.RO.at[0, s], s)
-            arrived(b, p, "rz", b.RO.at[1, s], n + s)
+            arrived(b, p, "rz", b.RO.at[kind, s], kind * n + s)
 
         rows = pack_rows(g, s)
-        out = b.RO[0, s].astype(F32)
-        dots = jnp.sum(out * b.UPK[s].astype(F32), axis=1, keepdims=True)
-        top = dots.astype(BF16).astype(F32)
-        b.RB[rows, 0 : g.DH] = (out * b.GC[s][:, 0:1]).astype(BF16)
-        b.RB[rows, g.DH : 2 * g.DH] = b.RO[1, s]
-        b.RB[rows, 2 * g.DH :] = jnp.where(
-            lane == s, top, jnp.where(lane == s + 64, dots - top, 0.0)
-        ).astype(BF16)
+        if kind:
+            b.RG[rows, 0 : g.DH] = b.RO[1, s]
+            dots = b.RO[1, s, base:, :].astype(F32)[g.CAP - base : g.CAP - base + 1]
+            dots = jnp.sum(jnp.where(eye, dots, 0.0), axis=1, keepdims=True)
+            b.RG[rows, g.DH :] = jnp.where(lane == s, dots, 0.0).astype(BF16)
+        else:
+            b.RB[rows, :] = (b.RO[0, s].astype(F32) * b.GC[s][:, 0:1]).astype(BF16)
 
     loop(n, rows_of)
 
 
-def unpack(g, p, b):
+def unpack(g, p, b, kind):
+    name = "ug" if kind else "uo"
+    rhs, out, landed = (b.RG, b.UG, b.TR) if kind else (b.RB, b.UO, b.TO)
+
+    def rows(image):
+        return nn(b.PT[tokens_of(g, image), :], rhs[...]).astype(BF16)
+
     for at, (image, device) in enumerate(((p.hy, p.across), (p.hdiag, p.diag), (p.hcore, p.core))):
-        rows = tokens_of(g, image)
-        b.UN[at] = nn(b.PT[rows, :], b.RB[...]).astype(BF16)
-        send(b, "un", b.UN.at[at], b.TR.at[p.c, p.y], at, p.h, device)
-    b.TR[p.c, p.y] = nn(b.PT[tokens_of(g, p.h), :], b.RB[...]).astype(BF16)
+        out[at] = rows(image)
+        send(b, name, out.at[at], landed.at[p.y, tokens_of(g, p.c), :], at, p.h, device)
+    landed[p.y, tokens_of(g, p.c), :] = rows(p.h)
+
+
+def unpacked(g, p, b, kind):
+    name = "ug" if kind else "uo"
+    landed = b.TR if kind else b.TO
     for hh, cc, yy in ((p.hcore, p.oc, p.y), (p.hy, p.c, p.oy), (p.hdiag, p.oc, p.oy)):
-        arrived(b, p, "un", b.TR.at[cc, yy], hh)
+        arrived(b, p, name, landed.at[yy, tokens_of(g, cc), :], hh)
+
+
+def mix(g, b):
+    def rows16(rows):
+        for q in range(2):
+            cols = slice(q * g.DH, (q + 1) * g.DH)
+            b.o_mixed[rows, cols] = (b.HID[rows, cols] + b.TO[q, rows, :].astype(F32)).astype(BF16)
+
+    rows16s(2 * g.IP, rows16)
 
 
 def tokens_back(g, p, b):
-    lane = iota((16, 128), 1)
+    lane = iota((g.IP, 128), 1)
     b.GA[...] = jnp.zeros_like(b.GA)
-
-    for blk in range(2):
-
-        def rows16(i, blk=blk):
-            local = pl.ds(pl.multiple_of(i * 16, 16), 16)
-            rows = pl.ds(pl.multiple_of(blk * g.IP + i * 16, 16), 16)
-            hidden = b.HID[rows, :]
-            for q in range(2):
-                cols = slice(q * g.DH, (q + 1) * g.DH)
-                b.o_mixed[rows, cols] = (
-                    hidden[:, cols] + b.TR[blk, q, local, 0 : g.DH].astype(F32)
-                ).astype(BF16)
-            gate = b.TR[blk, 0, local, 2 * g.DH :].astype(F32) + b.TR[
-                blk, 1, local, 2 * g.DH :
-            ].astype(F32)
-            gate = jnp.where(lane < g.ne, gate + pltpu.roll(gate, 64, 1), 0.0)
-            probs = b.PRB[rows, :]
-            grad = probs * (gate - jnp.sum(probs * gate, axis=1, keepdims=True))
-            b.GL[rows, :] = grad.astype(BF16)
-
-        loop(g.IP // 16, rows16)
     for blk in range(2):
         rows = slice(blk * g.IP, (blk + 1) * g.IP)
+        gate = b.TR[0, rows, g.DH :].astype(F32) + b.TR[1, rows, g.DH :].astype(F32)
+        probs = b.PRB[rows, :]
+        grad = probs * (gate - jnp.sum(probs * gate, axis=1, keepdims=True))
+        b.GL[rows, :] = grad.astype(BF16)
         b.GHID[rows, :] = nt(b.GL[rows, :], b.RW[...])
-    for blk in range(2):
-
-        def rows16b(i, blk=blk):
-            local = pl.ds(pl.multiple_of(i * 16, 16), 16)
-            rows = pl.ds(pl.multiple_of(blk * g.IP + i * 16, 16), 16)
-            normed, inverse = normalize(b.HID[rows, :])
-            upstream = b.GHID[rows, :] + jnp.concatenate(
-                [b.TR[blk, q, local, g.DH : 2 * g.DH].astype(F32) for q in range(2)], axis=1
-            )
-            prod = upstream * normed
-            b.GA[8:16, :] += prod[0:8, :] + prod[8:16, :]
-            b.ACT2[rows, :] = (normed * b.GN[1:2, :]).astype(BF16)
-            hidden = b.up[rows, :].astype(F32) + norm_backward(
-                upstream, normed, inverse, b.GN[1:2, :]
-            )
-            b.GHID[rows, :] = hidden
-            b.GHL[rows, :] = hidden.astype(BF16)
-            normed, _ = normalize(b.x[rows, :].astype(F32))
-            b.ACT1[rows, :] = (normed * b.GN[0:1, :]).astype(BF16)
-
-        loop(g.IP // 16, rows16b)
+
+    def rows16(rows):
+        normed, inverse = normalize(b.HID[rows, :])
+        upstream = b.GHID[rows, :] + jnp.concatenate(
+            [b.TR[q, rows, 0 : g.DH].astype(F32) for q in range(2)], axis=1
+        )
+        prod = upstream * normed
+        b.GA[8:16, :] += prod[0:8, :] + prod[8:16, :]
+        b.ACT2[rows, :] = (normed * b.GN[1:2, :]).astype(BF16)
+        hidden = b.up[rows, :].astype(F32) + norm_backward(upstream, normed, inverse, b.GN[1:2, :])
+        b.GHID[rows, :] = hidden
+        b.GHL[rows, :] = hidden.astype(BF16)
+
+    rows16s(2 * g.IP, rows16)
+
+
+def first_norm_again(g, b):
+    def rows16(rows):
+        normed, _ = normalize(b.x[rows, :].astype(F32))
+        b.ACT1[rows, :] = (normed * b.GN[0:1, :]).astype(BF16)
+
+    rows16s(2 * g.IP, rows16)
 
 
 def attention_back(g, p, b):
@@ -747,6 +790,15 @@
     b.DA[...] = jnp.zeros_like(b.DA)
 
     def group(k):
+        @pl.when(k == 1)
+        def _():
+            returns_on(g, p, b, 0)
+
+        @pl.when(k == 2)
+        def _():
+            slots_back(g, p, b, 0)
+            unpack(g, p, b, 0)
+
         yk = lax.rem(p.oy + k, 2)
         gi = 2 * yk + lax.rem(p.oc + lax.div(k, 2), 2)
         for blk in range(2):
@@ -789,12 +841,27 @@
         def _():
             send(b, "dc", b.DW.at[gi], b.RDC.at[yk], yk, yk, p.core)
 
+        @pl.when(k >= 2)
+        def _():
+            arrived(b, p, "dc", b.RDC.at[yk], yk)
+            if g.aligned:
+
+                def to_twin(i):
+                    e2 = p.other(i + 1)
+                    rows = piece_rows(g, p.od, e2)
+                    at = yk * g.ne + e2
+                    b.DW[gi, rows, :] = (
+                        b.DW[gi, rows, :].astype(F32) + b.RDC[yk, rows, :].astype(F32)
+                    ).astype(BF16)
+                    send(b, "dx", b.DW.at[gi, rows, :], b.RDX.at[yk, e2], at, at, p.twin)
+
+                loop(g.ne, to_twin)
+
     loop(4, group)
 
 
 def inputs_back(g, p, b):
-    def rows16(i):
-        rows = pl.ds(pl.multiple_of(i * 16, 16), 16)
+    def rows16(rows):
         normed, inverse = normalize(b.x[rows, :].astype(F32))
         upstream = b.DA[rows, :]
         prod = upstream * normed
@@ -803,7 +870,7 @@
             b.GHID[rows, :] + norm_backward(upstream, normed, inverse, b.GN[0:1, :])
         ).astype(BF16)
 
-    loop(2 * g.IP // 16, rows16)
+    rows16s(2 * g.IP, rows16)
     for blk in range(2):
         part = b.GIN.at[blk * g.IP : (blk + 1) * g.IP, :]
         send(b, "iy", part, b.o_gin.at[blk, p.h], blk, blk, p.across)
@@ -823,39 +890,43 @@
 
 
 def weights_back(g, p, b):
-    for i in range(2):
-        rows = pl.ds(pl.multiple_of(i * g.DH, 16), g.DH)
-        if i == 0:
-            arrived(b, p, "dc", b.RDC.at[p.oy], p.oy)
-        b.DW[p.hy, rows, :] = (b.DW[p.hy, rows, :].astype(F32) + b.RDC[p.oy, rows, :].astype(F32)).astype(BF16)
-        send(b, "dy", b.DW.at[p.hy, rows, :], b.RDY.at[rows, :], i, i, p.across)
+    if not g.aligned:
+        b.DW[p.hy] = (b.DW[p.hy].astype(F32) + b.RDC[p.oy].astype(F32)).astype(BF16)
+        send(b, "dy", b.DW.at[p.hy], b.RDY, 0, 0, p.across)
+        return
+
+    def to_across(i):
+        e2 = p.other(i + 1)
+        rows = piece_rows(g, p.d, e2)
+        arrived(b, p, "dx", b.RDX.at[p.oy, e2], p.oy * g.ne + e2)
+        b.RDX[p.oy, e2] = (
+            b.DW[p.hy, rows, :].astype(F32)
+            + b.RDC[p.oy, rows, :].astype(F32)
+            + b.RDX[p.oy, e2].astype(F32)
+        ).astype(BF16)
+        send(b, "dy", b.RDX.at[p.oy, e2], b.RDY.at[e2], e2, e2, p.across)
+
+    loop(g.ne, to_across)
 
 
 def weights_back_on(g, p, b):
-    arrived(b, p, "dc", b.RDC.at[p.y], p.y)
-
-    def total(rows):
-        return (
+    if not g.aligned:
+        arrived(b, p, "dy", b.RDY, 0)
+        total = b.DW[p.h].astype(F32) + b.RDC[p.y].astype(F32) + b.RDY[...].astype(F32)
+        b.o_dw[...] = total.astype(BF16)
+        return
+
+    def piece(k):
+        e2 = p.other(k + 1)
+        rows = piece_rows(g, p.d, e2)
+        arrived(b, p, "dx", b.RDX.at[p.y, e2], p.y * g.ne + e2)
+        arrived(b, p, "dy", b.RDY.at[e2], e2)
+        mine = (
             b.DW[p.h, rows, :].astype(F32)
             + b.RDC[p.y, rows, :].astype(F32)
-            + b.RDY[rows, :].astype(F32)
+            + b.RDX[p.y, e2].astype(F32)
+            + b.RDY[e2].astype(F32)
         )
-
-    for i in range(2):
-        arrived(b, p, "dy", b.RDY.at[pl.ds(i * g.DH, g.DH), :], i)
-    if not g.aligned:
-        b.o_dw[...] = total(slice(0, g.D)).astype(BF16)
-        return
-    half = g.D // 2
-    away = pl.ds(pl.multiple_of(p.od * half, 16), half)
-    b.DW[p.h, away, :] = total(away).astype(BF16)
-    send(b, "dx", b.DW.at[p.h, away, :], b.RDX, 0, 0, p.twin)
-    arrived(b, p, "dx", b.RDX, 0)
-
-    def piece(k):
-        e2 = p.other(k + 1)
-        local = pl.ds(pl.multiple_of(e2 * g.PR, 16), g.PR)
-        mine = total(piece_rows(g, p.d, e2)) + b.RDX[local, :].astype(F32)
 
         @pl.when(k < g.ne - 1)
         def _():
@@ -867,6 +938,11 @@
             b.o_dw[...] = mine
 
     loop(g.ne, piece)
+
+
+def weights_back_end(g, p, b):
+    if not g.aligned:
+        return
 
     def add(k):
         e2 = p.other(k + 1)
@@ -947,15 +1023,23 @@
 
     loop(n - 1, away)
     for at in range(3):
-        left(b, p, "un", b.UN.at[0], at)
+        left(b, p, "ug", b.UG.at[0], at)
+        left(b, p, "uo", b.UO.at[0], at)
     for i in range(2):
         left(b, p, "dc", b.RDC.at[0], i)
-        left(b, p, "dy", b.RDY.at[pl.ds(0, g.DH), :], i)
         for name in ("iy", "ic", "id"):
             left(b, p, name, b.o_gin.at[0, 0], i)
     if g.aligned:
-        left(b, p, "dx", b.RDX, 0)
         left(b, p, "sx", b.SMX, 0)
+
+        def moved(k):
+            left(b, p, "dx", b.RDX.at[0, 0], k)
+            left(b, p, "dx", b.RDX.at[0, 0], g.ne + k)
+            left(b, p, "dy", b.RDY.at[0], k)
+
+        loop(n, moved)
+    else:
+        left(b, p, "dy", b.RDY, 0)
     left(b, p, "sc", b.SMC, 0)
     left(b, p, "sy", b.SMY, 0)
 
@@ -963,19 +1047,28 @@
 def second_kernel(g, b):
     p = Place(g)
     p.enter()
-    returns(g, p, b)
+    returns_start(g, p, b, 1)
+    returns_start(g, p, b, 0)
     grads_of_expert_out(g, p, b)
-    slots_back(g, p, b)
-    unpack(g, p, b)
+    returns_over(g, p, b, 1)
+    first_norm_again(g, b)
+    returns_on(g, p, b, 1)
+    slots_back(g, p, b, 1)
+    unpack(g, p, b, 1)
+    unpacked(g, p, b, 1)
+    returns_over(g, p, b, 0)
     tokens_back(g, p, b)
     attention_back(g, p, b)
     inputs_back(g, p, b)
+    weights_back(g, p, b)
     small_back(g, p, b)
-    weights_back(g, p, b)
     inputs_end(g, p, b)
     weights_back_on(g, p, b)
+    unpacked(g, p, b, 0)
+    mix(g, b)
     small_back_on(g, p, b)
     grads_of_expert_in(g, p, b)
+    weights_back_end(g, p, b)
     second_sends_end(g, p, b)
 
 
@@ -1053,7 +1146,6 @@
             HID=((2 * ip, model), F32),
             PRB=((2 * ip, 128), F32),
             PT=((g.TP, g.SL), BF16),
-            UPK=((n, cp, dh), BF16),
             GC=((n, cp, 128), F32),
             PO=((n, 2, 2, cp, dh), BF16),
             PG=((n, 2, 2, cp, dh), BF16),
@@ -1088,11 +1180,11 @@
         1,
         14 * 10**9,
     )
-    keep = ("W", "RW", "GN", "QKV", "PB", "ATT", "HID", "PRB", "PT", "UPK", "GC", "PO", "PG", "KI", "KB", "SI", "SB")
+    keep = ("W", "RW", "GN", "QKV", "PB", "ATT", "HID", "PRB", "PT", "GC", "PO", "PG", "KI", "KB", "SI", "SB")
     rows_out = g.PR if g.aligned else model
     extra = (
         dict(
-            RDX=((model // 2, model), BF16),
+            RDX=((2, n, g.PR, model), BF16),
             SDZ=((n, g.PR, model), BF16),
             RDZ=((n, g.PR, model), BF16),
             SMX=((model // 2, 128), BF16),
@@ -1119,9 +1211,12 @@
             RC=((2, n, 2, cp, dh), BF16),
             RY=((2, n, cp, dh), BF16),
             RO=((2, n, cp, dh), BF16),
-            RB=((g.SL, 2 * dh + 128), BF16),
-            UN=((3, ip, 2 * dh + 128), BF16),
-            TR=((2, 2, ip, 2 * dh + 128), BF16),
+            RG=((g.SL, dh + 128), BF16),
+            RB=((g.SL, dh), BF16),
+            UG=((3, ip, dh + 128), BF16),
+            UO=((3, ip, dh), BF16),
+            TR=((2, 2 * ip, dh + 128), BF16),
+            TO=((2, 2 * ip, dh), BF16),
             GL=((2 * ip, 128), BF16),
             GA=((16, model), F32),
             ACT1=((2 * ip, model), BF16),
@@ -1132,7 +1227,7 @@
             GJ=((2 * ip, 640), BF16),
             DW=((4, model, model), BF16),
             RDC=((2, model, model), BF16),
-            RDY=((model, model), BF16),
+            RDY=((n, g.PR, model) if g.aligned else (model, model), BF16),
             GIN=((2 * ip, model), BF16),
             GM=((model, 128), F32),
             SMC=((rows_out, 128), BF16),
@@ -1143,7 +1238,7 @@
             XB=((g.F, dh), BF16),
             **extra,
         ),
-        dict(rc=2 * n, ry=2 * n, rz=2 * n, un=4, gi=1, gb=1, dc=2, dy=2, dx=1, dz=n, sx=1, sz=n, sc=1, sy=1, iy=2, ic=2, id=2),
+        dict(rc=2 * n, ry=2 * n, rz=2 * n, ug=4, uo=4, gi=1, gb=1, dc=2, dy=n, dx=2 * n, dz=n, sx=1, sz=n, sc=1, sy=1, iy=2, ic=2, id=2),
         2,
         14 * 10**9,
     )

time: 335 us -> 259 us (0.77)
  Pallas kernels: 302 us -> 227 us
    pallas_call x2, Pallas kernels: 302 us -> 227 us  [call(): pl.pallas_call(kernel, out_shape=[jax.ShapeDtypeStruct(*o) for o in outs....]
where the time goes in v2:
time: 259 us
  Pallas kernels  227 us (88%)
  local copies, waits for them, and re-layouts  28.2 us (11%)
  other arithmetic  2.87 us (1%)
    pallas_call x2, Pallas kernels, call(): pl.pallas_call(kernel, out_shape=[jax.ShapeDtypeStruct(*o) for o in outs....  227 us
    unnamed x14, local copies, waits for them, and re-layouts  8.16 us

profile of v2, /device:TPU:0, one launch (start us, length us, event | category | flops | bytes accessed | tf_op | source)
XLA Modules:
  0.0 258.7 jit_solution(5468872223807224668)
XLA Ops:
  0.6 0.7 subtract_convert_fusion
  1.3 0.7 fusion
  2.0 0.8 concatenate.17
  2.8 0.8 concatenate.16
  3.6 0.1 reshape.51
  3.8 0.1 copy.59
  3.9 0.1 copy.58
  4.0 0.1 copy.57
  4.1 0.1 copy.56
  4.3 0.8 copy.55
  5.1 0.7 concatenate.15.refs_3_
  5.8 0.9 copy.54
  6.7 0.6 pad_bitcast_fusion.refs_7_
  7.3 0.9 slice_bitcast_fusion.6
  8.2 0.8 pad_maximum_fusion.1.refs_2_
  9.0 0.3 copy.67
  9.3 1.0 pad.19.clone.refs_6_
  10.2 2.6 %reshape.48 = bf16[2,4,196,768]{3,2,1,0:T(8,128)(2,1)S(1)} reshape(bf16[2,784,768]{2,1,0:T(8,128)(2,1)} %param.21) | data formatting | bytes 4816896 | tf_op jit(solution)/shard_map/reshape | solution.py:1109
  12.9 0.9 constant_dynamic-slice_fusion
  13.8 1.7 pad.17
  15.4 2.6 %reshape.46 = bf16[2,4,196,768]{3,2,1,0:T(8,128)(2,1)S(1)} reshape(bf16[2,784,768]{2,1,0:T(8,128)(2,1)} %param.11) | data formatting | bytes 4816896 | tf_op jit(solution)/shard_map/reshape | solution.py:1107
  18.1 0.9 pad.16
  19.0 101.5 %shard_map.178 = (bf16[4,768,768]{2,1,0:T(8,128)(2,1)}, bf16[768,128]{1,0:T(8,128)(2,1)}, f32[8,768]{1,0:T(8,128)}, bf16[4,416,640]{2,1,0:T(8,128)(2,1)}, bf16[4...) custom-call(bf16[416,768]{1,0:T(8,128)(2,1)} %bitcast.36, ...), custom_call_target="tpu_custom_call" | custom-call | flops 14000000000 | bytes 16777216 | tf_op jit(solution)/shard_map/pallas_call | solution.py:1083
  120.5 125.4 %shard_map.179 = (bf16[416,768]{1,0:T(8,128)(2,1)}, bf16[2,4,208,768]{3,2,1,0:T(8,128)(2,1)}, f32[96,768]{1,0:T(8,128)}, f32[96,128]{1,0:T(8,128)}, f32[384,768]{1,0:T(8,128)}, /*index=5*/f32[768,384]{1,0:T(8,128)}) custom-call(bf16[416,768]{1,0:T(8,128)(2,1)} %bitcast.37, bf16[416,768]{1,0:T(8,128)(2,1)} %bitcast.35, ...), custom_call_target="tpu_custom_call" | custom-call | flops 14000000000 | bytes 16777216 | tf_op jit(solution)/shard_map/pallas_call | solution.py:1083
  245.9 0.0 copy-start.2
  245.9 0.0 copy-start.1
  245.9 1.2 slice.64
  247.1 1.3 copy.66
  248.4 0.0 copy-done.2
  248.4 0.7 slice_reduce_fusion
  249.1 0.7 copy.65
  249.7 0.0 copy-done.1
  249.7 0.1 slice_bitcast_fusion
  249.8 0.7 copy.64
  250.6 0.7 pad_maximum_fusion
  251.3 1.9 slice.56
  253.2 2.1 reshape.53
  255.3 0.0 copy-start
  255.3 2.5 copy.72
  257.7 0.0 copy-done
  257.7 1.0 copy.73
  (8 shorter events, 0.1 us)
Async XLA Ops:
  245.9 2.5 copy-start.2
  245.9 3.8 %copy-start.1 = (f32[96,768]{1,0:T(8,128)S(1)}, f32[96,768]{1,0:T(8,128)}, u32[]{:S(2)}) copy-start(f32[96,768]{1,0:T(8,128)} %get-tuple-element.49) | copy-start | bytes 884740
  255.3 2.5 copy-start

commit v3 on v2

--- a/solution.py
+++ b/solution.py
@@ -73,6 +73,8 @@
         self.NI = rows // SEQ
         self.TP = self.NI * self.IP
         self.SL = self.ne * self.CP
+        self.WIN = self.IP - 16
+        self.LAG = SEQ - self.WIN
         self.F = hidden
         self.PR = model // (self.nd * self.ne)
         self.aligned = self.PR % 16 == 0
@@ -82,6 +84,7 @@
         self.R = self.SG * 2 * self.CP
         self.LW = model // self.nh
         assert self.nd == 2 and self.nh == 4 and self.NI == 4 and self.LW == 3 * HD
+        assert (self.NI - 1) * self.WIN + self.IP <= rows and (self.NI - 1) * self.LAG + SEQ <= self.IP
         assert self.ne <= 64 and 0 <= self.CAP - (self.CP - 16) <= 14
 
 
@@ -143,8 +146,71 @@
     copy(b, name, ref, ref, si, 0, p.core).wait_send()
 
 
-def route(g, p, b):
-    c = p.c
+def fetch(b, name, src, dst, i=0):
+    pltpu.make_async_copy(src, dst, getattr(b, name + "_s").at[i]).start()
+
+
+def fetched(b, name, src, dst, i=0):
+    pltpu.make_async_copy(src, dst, getattr(b, name + "_s").at[i]).wait()
+
+
+def stow(b, *names):
+    for name in names:
+        fetch(b, "k" + name, getattr(b, name), getattr(b, "h" + name))
+
+
+def stowed(b, *names):
+    for name in names:
+        fetched(b, "k" + name, getattr(b, name), getattr(b, "h" + name))
+
+
+def load(b, *names):
+    for name in names:
+        fetch(b, "k" + name, getattr(b, "h" + name), getattr(b, name))
+
+
+def loaded(b, *names):
+    for name in names:
+        fetched(b, "k" + name, getattr(b, "h" + name), getattr(b, name))
+
+
+def shift(g, image, back=False):
+    row, col = iota((g.IP, g.IP), 0), iota((g.IP, g.IP), 1)
+    if back:
+        hot = (row == col + g.LAG * image) & (col < SEQ)
+    else:
+        hot = (col == row + g.LAG * image) & (row < SEQ)
+    return jnp.where(hot, 1.0, 0.0).astype(BF16)
+
+
+def window(g, image):
+    return pl.ds(pl.multiple_of(image * g.WIN, 16), g.IP)
+
+
+def rows_out(g, p, b):
+    for j in range(2):
+        rows = slice(j * g.IP, (j + 1) * g.IP)
+        fetch(b, "ldx", b.xin.at[p.y, window(g, 2 * p.c + j), :], b.X.at[rows, :], j)
+        fetch(b, "ldu", b.uin.at[p.y, window(g, 2 * p.c + j), :], b.UPO.at[rows, :], j)
+    fetch(b, "ldb", b.uin.at[p.c], b.UB)
+
+
+def rows_in(g, p, b):
+    for j in range(2):
+        rows = slice(j * g.IP, (j + 1) * g.IP)
+        fetched(b, "ldx", b.xin.at[p.y, window(g, 2 * p.c + j), :], b.X.at[rows, :], j)
+        fetched(b, "ldu", b.uin.at[p.y, window(g, 2 * p.c + j), :], b.UPO.at[rows, :], j)
+        hot = shift(g, 2 * p.c + j)
+        b.X[rows, :] = nn(hot, b.X[rows, :]).astype(BF16)
+        b.UPO[rows, :] = nn(hot, b.UPO[rows, :]).astype(BF16)
+    fetched(b, "ldb", b.uin.at[p.c], b.UB)
+    for i in range(g.NI):
+        b.UPP[i * g.IP : (i + 1) * g.IP, :] = nn(
+            shift(g, i), b.UB[i * g.WIN : i * g.WIN + g.IP, :]
+        ).astype(BF16)
+
+
+def route(g, b, c, both):
     pr_row, e0r, e1r = b.mr[c, 2:3, :], b.mr[c, 0:1, :], b.mr[c, 1:2, :]
     lane = fiota((g.IP, 128), 1)
     base = jnp.zeros((1, 128), F32)
@@ -156,7 +222,7 @@
         b.O[rows, :] = jnp.where((lane == e0c) | (lane == e1c + 64.0), 1.0, 0.0).astype(BF16)
         base = base + jnp.sum(jnp.where(lane == e0c + 64.0, 1.0, 0.0), axis=0, keepdims=True)
     slot_lane = fiota((g.IP, g.SL), 1)
-    for i in range(g.NI):
+    for i in range(g.NI if both else 0):
         rows = slice(i * g.IP, (i + 1) * g.IP)
         col = b.mc[c, rows, :]
         e0c, e1c = col[:, 0:1], col[:, 1:2]
@@ -334,7 +400,7 @@
 
 def first_norm(g, b):
     def rows16(rows):
-        x = b.x[rows, :].astype(F32)
+        x = b.X[rows, :].astype(F32)
         normed, _ = normalize(x)
         b.ACT1[rows, :] = (normed * b.GN[0:1, :]).astype(BF16)
         b.HID[rows, :] = x
@@ -373,30 +439,27 @@
     return pl.ds(pl.multiple_of(i * g.DH, 128), g.DH)
 
 
-def tokens_of(g, blk):
-    return pl.ds(pl.multiple_of(blk * g.IP, 16), g.IP)
+def own_rows(g, c):
+    return pl.ds(pl.multiple_of(c * 2 * g.IP, 16), 2 * g.IP)
 
 
 def tokens_out(g, p, b):
-    for at, (device, yy, cc) in enumerate(
-        ((p.across, p.oy, p.c), (p.diag, p.oy, p.oc), (p.core, p.y, p.oc))
-    ):
-        send(b, "ta", b.ACT2.at[tokens_of(g, cc), half_of(g, yy)], b.TA.at[p.h], at, p.h, device)
-        send(b, "tp", b.PRH.at[tokens_of(g, cc), :], b.TG.at[p.h], at, p.h, device)
-    b.TA[p.h] = b.ACT2[tokens_of(g, p.c), half_of(g, p.y)]
-    b.TG[p.h] = b.PRH[tokens_of(g, p.c), :]
+    rows = own_rows(g, p.c)
+    send(b, "ta", b.ACT2.at[:, half_of(g, p.oc)], b.TA.at[rows, :], 0, 0, p.core)
+    send(b, "tp", b.PRH, b.TG.at[rows, :], 0, 0, p.core)
+    b.TA[rows, :] = b.ACT2[:, half_of(g, p.c)]
+    b.TG[rows, :] = b.PRH[...]
 
 
 def tokens_in(g, p, b):
-    for src in (p.hcore, p.hy, p.hdiag):
-        arrived(b, p, "ta", b.TA.at[src], src)
-        arrived(b, p, "tp", b.TG.at[src], src)
+    arrived(b, p, "ta", b.TA.at[own_rows(g, p.oc), :], 0)
+    arrived(b, p, "tp", b.TG.at[own_rows(g, p.oc), :], 0)
 
 
 def cotangent_out(g, p, b):
     def pack(k):
         e2 = p.other(k + 1)
-        rows = nn(b.P[pack_rows(g, e2), :], b.up[p.c]).astype(BF16)
+        rows = nn(b.P[pack_rows(g, e2), :], b.UPP[...]).astype(BF16)
         b.PKU[e2] = rows
 
         @pl.when(k < g.ne - 1)
@@ -429,8 +492,8 @@
     def pack(k):
         e2 = p.other(k + 1)
         hot = b.P[pack_rows(g, e2), :]
-        tok = nn(hot, b.TA[...].reshape(g.TP, g.DH))
-        gates = nn(hot, b.TG[...].reshape(g.TP, 128))
+        tok = nn(hot, b.TA[...])
+        gates = nn(hot, b.TG[...])
         gate = jnp.sum(
             jnp.where((lane == e2) | (lane == e2 + 64), gates, 0.0), axis=1, keepdims=True
         )
@@ -443,12 +506,12 @@
         @pl.when(k < g.ne - 1)
         def _():
             b.PKA[e2] = rows
-            send(b, "xz", b.PKA.at[e2], b.XS.at[p.e, p.c, p.y], k, p.e, p.along(e2))
+            send(b, "xz", b.PKA.at[e2], b.XS.at[p.e, p.y, p.c], k, p.e, p.along(e2))
 
         @pl.when(k == g.ne - 1)
         def _():
-            part = b.XS.at[p.e, p.c, p.y]
-            b.XS[p.e, p.c, p.y] = rows
+            part = b.XS.at[p.e, p.y, p.c]
+            b.XS[p.e, p.y, p.c] = rows
             send(b, "xy", part, part, p.e, p.e, p.across)
             send(b, "xc", part, part, p.e, p.e, p.core)
 
@@ -456,21 +519,21 @@
 
 
 def slots_on(g, p, b, e2):
-    part = b.XS.at[e2, p.c, p.y]
+    part = b.XS.at[e2, p.y, p.c]
     arrived(b, p, "xz", part, e2)
     send(b, "xy", part, part, e2, e2, p.across)
     send(b, "xc", part, part, e2, e2, p.core)
 
 
 def slots_over(g, p, b, e2):
-    part = b.XS.at[e2, p.c, p.oy]
+    part = b.XS.at[e2, p.oy, p.c]
     arrived(b, p, "xy", part, e2)
     send(b, "xd", part, part, e2, e2, p.core)
 
 
 def slots_in(g, p, b, e2):
-    arrived(b, p, "xc", b.XS.at[e2, p.oc, p.y], e2)
-    arrived(b, p, "xd", b.XS.at[e2, p.oc, p.oy], e2)
+    arrived(b, p, "xc", b.XS.at[e2, p.y, p.oc], e2)
+    arrived(b, p, "xd", b.XS.at[e2, p.oy, p.oc], e2)
     arrived(b, p, "uc", b.US.at[e2, p.oc], e2)
 
 
@@ -479,6 +542,49 @@
     b.WB[p.d] = b.wb[...]
     send(b, "ei", b.wi, b.WI.at[p.d], 0, 0, p.twin)
     send(b, "eb", b.wb, b.WB.at[p.d], 0, 0, p.twin)
+
+
+def back_core(g, p, b, part, s):
+    send(b, "rc", part.at[s, :, p.oc], b.RC.at[s], s, s, p.core)
+
+
+def back_over(g, p, b, part, s):
+    arrived(b, p, "rc", b.RC.at[s], s)
+    b.RC[s, p.oy] = (part[s, p.oy, p.c].astype(F32) + b.RC[s, p.oy].astype(F32)).astype(BF16)
+    send(b, "ry", b.RC.at[s, p.oy], b.RY.at[s], s, s, p.across)
+
+
+def back_on(g, p, b, part, s):
+    arrived(b, p, "ry", b.RY.at[s], s)
+    total = (
+        part[s, p.y, p.c].astype(F32) + b.RC[s, p.y].astype(F32) + b.RY[s].astype(F32)
+    ).astype(BF16)
+
+    @pl.when(s != p.e)
+    def _():
+        b.RC[s, p.y] = total
+        send(b, "rz", b.RC.at[s, p.y], b.RO.at[p.e], s, p.e, p.along(s))
+
+    @pl.when(s == p.e)
+    def _():
+        b.RO[p.e] = total
+
+
+def back_in(g, p, b):
+    def rows_of(k):
+        s = p.other(k + 1)
+        arrived(b, p, "rz", b.RO.at[s], s)
+
+    loop(g.ne - 1, rows_of)
+
+
+def back_end(g, p, b):
+    def rets(s):
+        left(b, p, "rc", b.RC.at[0], s)
+        left(b, p, "ry", b.RY.at[0], s)
+
+    loop(g.ne, rets)
+    loop(g.ne - 1, lambda k: left(b, p, "rz", b.RY.at[0], p.other(k + 1)))
 
 
 def gelu_parts(u):
@@ -544,6 +650,9 @@
         arrived(b, p, "ei", b.WI.at[p.od], 0)
         arrived(b, p, "eb", b.WB.at[p.od], 0)
         loop(n // g.SG, lambda t: expert(g, b, t * g.SG))
+        loop(n, lambda k: back_core(g, p, b, b.PG, p.other(k)))
+        loop(n, lambda k: back_over(g, p, b, b.PG, p.other(k)))
+        loop(n, lambda k: back_on(g, p, b, b.PG, p.other(k)))
         return
     slots_over(g, p, b, p.e)
     slots_in(g, p, b, p.e)
@@ -557,12 +666,16 @@
 
         @pl.when(k > 0)
         def _():
+            back_over(g, p, b, b.PG, p.other(k - 1))
             slots_over(g, p, b, p.other(k))
             slots_in(g, p, b, p.other(k))
 
         expert(g, b, p.other(k))
+        back_core(g, p, b, b.PG, p.other(k))
 
     loop(n, source)
+    back_over(g, p, b, b.PG, p.other(n - 1))
+    loop(n, lambda k: back_on(g, p, b, b.PG, p.other(k)))
 
 
 def first_sends_end(g, p, b):
@@ -587,9 +700,8 @@
             left(b, p, name, piece_of(g, b.W, p.h, i), i)
 
     loop(pieces(g), w)
-    for at in range(3):
-        left(b, p, "ta", b.TA.at[0], at)
-        left(b, p, "tp", b.TG.at[0], at)
+    left(b, p, "ta", b.TA.at[own_rows(g, 0), :], 0)
+    left(b, p, "tp", b.TG.at[own_rows(g, 0), :], 0)
 
     def slots(k):
         left(b, p, "uz", b.PKU.at[0], k)
@@ -607,146 +719,133 @@
     left(b, p, "eb", b.wb, 0)
 
 
+KEEP = ("X", "UPO", "W", "RW", "GN", "QKV", "PB", "ATT", "HID", "PRB", "PT", "GC", "PO", "RO", "KI", "KB", "SI", "SB")
+
+
 def first_kernel(g, b):
     p = Place(g)
+    rows_out(g, p, b)
     p.enter()
     weights_out(g, p, b)
-    route(g, p, b)
+    rows_in(g, p, b)
+    route(g, b, p.c, False)
     weights_on(g, p, b)
     cotangent_out(g, p, b)
     weights_end(g, p, b)
     experts_out(g, p, b)
+    route(g, b, p.y, True)
     small_weights(g, b)
     first_norm(g, b)
+    stow(b, "X", "UPO", "RW", "GN", "PT")
     attention(g, p, b)
+    stow(b, "W", "QKV", "PB", "ATT", "HID")
     second_norm(g, b)
+    stow(b, "PRB")
     tokens_out(g, p, b)
     cotangent_on(g, p, b)
     tokens_in(g, p, b)
     slots_out(g, p, b)
+    stow(b, "GC")
     experts(g, p, b)
+    stow(b, "PO")
     b.KI[...] = b.DI[p.d]
     b.KB[...] = b.DB[p.d]
     b.SI[...] = b.DI[p.od].astype(BF16)
     b.SB[...] = b.DB[p.od].astype(BF16)
+    stow(b, "KI", "KB", "SI", "SB")
+    back_in(g, p, b)
+    stow(b, "RO")
     first_sends_end(g, p, b)
+    back_end(g, p, b)
+    stowed(b, *KEEP)
 
 
 def grads_of_expert_out(g, p, b):
-    send(b, "gi", b.SI, b.XI, 0, 0, p.twin)
-    send(b, "gb", b.SB, b.XB, 0, 0, p.twin)
+    send(b, "gi", b.hSI, b.XI, 0, 0, p.twin)
+    send(b, "gb", b.hSB, b.XB, 0, 0, p.twin)
 
 
 def grads_of_expert_in(g, p, b):
+    loaded(b, "KI", "KB")
     arrived(b, p, "gi", b.XI, 0)
     b.o_gi[...] = b.KI[...] + b.XI[...].astype(F32)
     arrived(b, p, "gb", b.XB, 0)
     b.o_gb[...] = b.KB[...] + b.XB[...].astype(F32)
 
 
-def part_of(b, kind):
-    return b.PG if kind else b.PO
-
-
-def returns_start(g, p, b, kind):
-    def to_core(k):
-        s = p.other(k + 1)
-        at = kind * g.ne + s
-        send(b, "rc", part_of(b, kind).at[s, p.oc], b.RC.at[kind, s], at, at, p.core)
-
-    loop(g.ne, to_core)
-
-
-def returns_over(g, p, b, kind):
-    def to_across(k):
-        s = p.other(k + 1)
-        at = kind * g.ne + s
-        arrived(b, p, "rc", b.RC.at[kind, s], at)
-        b.RC[kind, s, p.oy] = (
-            part_of(b, kind)[s, p.c, p.oy].astype(F32) + b.RC[kind, s, p.oy].astype(F32)
-        ).astype(BF16)
-        send(b, "ry", b.RC.at[kind, s, p.oy], b.RY.at[kind, s], at, at, p.across)
-
-    loop(g.ne, to_across)
-
-
-def returns_on(g, p, b, kind):
-    n = g.ne
-
-    def to_source(k):
-        s = p.other(k + 1)
-        at = kind * n + s
-        arrived(b, p, "ry", b.RY.at[kind, s], at)
-        total = (
-            part_of(b, kind)[s, p.c, p.y].astype(F32)
-            + b.RC[kind, s, p.y].astype(F32)
-            + b.RY[kind, s].astype(F32)
-        ).astype(BF16)
-
-        @pl.when(k < n - 1)
-        def _():
-            b.RC[kind, s, p.y] = total
-            send(b, "rz", b.RC.at[kind, s, p.y], b.RO.at[kind, p.e], at, kind * n + p.e, p.along(s))
-
-        @pl.when(k == n - 1)
-        def _():
-            b.RO[kind, p.e] = total
-
-    loop(n, to_source)
-
-
 def slots_back(g, p, b, kind):
-    n = g.ne
     lane = iota((g.CP, 128), 1)
     base = g.CP - 16
     eye = iota((g.CP, g.DH), 0) == iota((g.CP, g.DH), 1)
 
-    def rows_of(k):
-        s = p.other(k)
-
-        @pl.when(k > 0)
-        def _():
-            arrived(b, p, "rz", b.RO.at[kind, s], kind * n + s)
-
+    def rows_of(s):
         rows = pack_rows(g, s)
         if kind:
-            b.RG[rows, 0 : g.DH] = b.RO[1, s]
-            dots = b.RO[1, s, base:, :].astype(F32)[g.CAP - base : g.CAP - base + 1]
+            b.RG[rows, 0 : g.DH] = b.RB[s]
+            dots = b.RB[s, base:, :].astype(F32)[g.CAP - base : g.CAP - base + 1]
             dots = jnp.sum(jnp.where(eye, dots, 0.0), axis=1, keepdims=True)
             b.RG[rows, g.DH :] = jnp.where(lane == s, dots, 0.0).astype(BF16)
         else:
-            b.RB[rows, :] = (b.RO[0, s].astype(F32) * b.GC[s][:, 0:1]).astype(BF16)
-
-    loop(n, rows_of)
+            b.RG[rows, 0 : g.DH] = (b.RO[s].astype(F32) * b.GC[s][:, 0:1]).astype(BF16)
+
+    loop(g.ne, rows_of)
 
 
 def unpack(g, p, b, kind):
-    name = "ug" if kind else "uo"
-    rhs, out, landed = (b.RG, b.UG, b.TR) if kind else (b.RB, b.UO, b.TO)
-
-    def rows(image):
-        return nn(b.PT[tokens_of(g, image), :], rhs[...]).astype(BF16)
-
-    for at, (image, device) in enumerate(((p.hy, p.across), (p.hdiag, p.diag), (p.hcore, p.core))):
-        out[at] = rows(image)
-        send(b, name, out.at[at], landed.at[p.y, tokens_of(g, p.c), :], at, p.h, device)
-    landed[p.y, tokens_of(g, p.c), :] = rows(p.h)
+    name, width = ("ug", g.DH + 128) if kind else ("uo", g.DH)
+    out, landed = (b.UG, b.TR) if kind else (b.UO, b.TO)
+
+    def rows(c, j):
+        image = pl.ds(pl.multiple_of((2 * c + j) * g.IP, 16), g.IP)
+        return nn(b.PT[image, :], b.RG[:, 0:width]).astype(BF16)
+
+    for j in range(2):
+        here = slice(j * g.IP, (j + 1) * g.IP)
+        out[here, :] = rows(p.oc, j)
+        send(b, name, out.at[here, :], landed.at[p.c, here, :], j, j, p.core)
+    for j in range(2):
+        landed[p.c, j * g.IP : (j + 1) * g.IP, :] = rows(p.c, j)
 
 
 def unpacked(g, p, b, kind):
-    name = "ug" if kind else "uo"
-    landed = b.TR if kind else b.TO
-    for hh, cc, yy in ((p.hcore, p.oc, p.y), (p.hy, p.c, p.oy), (p.hdiag, p.oc, p.oy)):
-        arrived(b, p, name, landed.at[yy, tokens_of(g, cc), :], hh)
-
-
-def mix(g, b):
+    name, landed = ("ug", b.TR) if kind else ("uo", b.TO)
+    for j in range(2):
+        arrived(b, p, name, landed.at[p.oc, j * g.IP : (j + 1) * g.IP, :], j)
+
+
+def mix(g, p, b):
     def rows16(rows):
         for q in range(2):
             cols = slice(q * g.DH, (q + 1) * g.DH)
-            b.o_mixed[rows, cols] = (b.HID[rows, cols] + b.TO[q, rows, :].astype(F32)).astype(BF16)
+            b.MX[rows, cols] = (b.HID[rows, cols] + b.TO[q, rows, :].astype(F32)).astype(BF16)
 
     rows16s(2 * g.IP, rows16)
+    for j in range(2):
+        part = b.MX.at[j * g.IP : (j + 1) * g.IP, :]
+        here = (p.c == p.y) & (p.c == j)
+
+        @pl.when(here)
+        def _(j=j):
+            b.MIX[p.y] = b.MX[j * g.IP : (j + 1) * g.IP, :]
+
+        @pl.when(jnp.logical_not(here))
+        def _(j=j, part=part):
+            send(b, "mo", part, b.MIX.at[p.y], j, p.y, (p.d, p.e, 2 * p.c + j))
+
+
+def mixed_in(g, p, b):
+    for blk in range(2):
+
+        @pl.when(jnp.logical_not((p.y == blk) & (p.c == p.y)))
+        def _(blk=blk):
+            arrived(b, p, "mo", b.MIX.at[blk], blk)
+
+        b.o_mixed[blk] = b.MIX[blk, 0:SEQ, :]
+    for j in range(2):
+
+        @pl.when(jnp.logical_not((p.c == p.y) & (p.c == j)))
+        def _(j=j):
+            left(b, p, "mo", b.MIX.at[0], j)
 
 
 def tokens_back(g, p, b):
@@ -768,7 +867,7 @@
         prod = upstream * normed
         b.GA[8:16, :] += prod[0:8, :] + prod[8:16, :]
         b.ACT2[rows, :] = (normed * b.GN[1:2, :]).astype(BF16)
-        hidden = b.up[rows, :].astype(F32) + norm_backward(upstream, normed, inverse, b.GN[1:2, :])
+        hidden = b.UPO[rows, :].astype(F32) + norm_backward(upstream, normed, inverse, b.GN[1:2, :])
         b.GHID[rows, :] = hidden
         b.GHL[rows, :] = hidden.astype(BF16)
 
@@ -777,7 +876,7 @@
 
 def first_norm_again(g, b):
     def rows16(rows):
-        normed, _ = normalize(b.x[rows, :].astype(F32))
+        normed, _ = normalize(b.X[rows, :].astype(F32))
         b.ACT1[rows, :] = (normed * b.GN[0:1, :]).astype(BF16)
 
     rows16s(2 * g.IP, rows16)
@@ -792,12 +891,18 @@
     def group(k):
         @pl.when(k == 1)
         def _():
-            returns_on(g, p, b, 0)
+            loop(g.ne, lambda i: back_on(g, p, b, b.PO, p.other(i + 1)))
 
         @pl.when(k == 2)
         def _():
+            back_in(g, p, b)
             slots_back(g, p, b, 0)
             unpack(g, p, b, 0)
+
+        @pl.when(k == 3)
+        def _():
+            unpacked(g, p, b, 0)
+            mix(g, p, b)
 
         yk = lax.rem(p.oy + k, 2)
         gi = 2 * yk + lax.rem(p.oc + lax.div(k, 2), 2)
@@ -862,7 +967,7 @@
 
 def inputs_back(g, p, b):
     def rows16(rows):
-        normed, inverse = normalize(b.x[rows, :].astype(F32))
+        normed, inverse = normalize(b.X[rows, :].astype(F32))
         upstream = b.DA[rows, :]
         prod = upstream * normed
         b.GA[0:8, :] += prod[0:8, :] + prod[8:16, :]
@@ -871,22 +976,45 @@
         ).astype(BF16)
 
     rows16s(2 * g.IP, rows16)
+    for j in range(2):
+        rows = slice(j * g.IP, (j + 1) * g.IP)
+        image = 2 * p.c + j
+        b.GIN[rows, :] = nn(shift(g, image, True), b.GIN[rows, :]).astype(BF16)
+        b.EG[j, 0] = b.GIN[j * g.IP : j * g.IP + 16, :]
+        b.EG[j, 1] = b.GIN[(j + 1) * g.IP - 16 : (j + 1) * g.IP, :]
+        for name, device in (("i", p.across), ("j", p.core)):
+            middle = b.GIN.at[j * g.IP + 16 : (j + 1) * g.IP - 16, :]
+            send(b, name + "m", middle, b.o_gin.at[p.y, middle_of(g, image), :], j, j, device)
+            send(b, name + "e", b.EG.at[j], b.ED.at[p.y, image], j, j, device)
+        b.o_gin[p.y, middle_of(g, image), :] = b.GIN[j * g.IP + 16 : (j + 1) * g.IP - 16, :]
+        b.ED[p.y, image] = b.EG[j]
+
+
+def middle_of(g, image):
+    return pl.ds(pl.multiple_of(image * g.WIN + 16, 16), g.WIN - 16)
+
+
+def inputs_end(g, p, b):
+    for j in range(2):
+        image = 2 * p.c + j
+        middle, edge = b.o_gin.at[p.oy, middle_of(g, image), :], b.ED.at[p.oy, image]
+        arrived(b, p, "im", middle, j)
+        send(b, "km", middle, middle, j, j, p.core)
+        arrived(b, p, "ie", edge, j)
+        send(b, "ke", edge, edge, j, j, p.core)
+
+
+def inputs_last(g, p, b):
+    for j in range(2):
+        image = 2 * p.oc + j
+        for name, yy in (("j", p.y), ("k", p.oy)):
+            arrived(b, p, name + "m", b.o_gin.at[yy, middle_of(g, image), :], j)
+            arrived(b, p, name + "e", b.ED.at[yy, image], j)
     for blk in range(2):
-        part = b.GIN.at[blk * g.IP : (blk + 1) * g.IP, :]
-        send(b, "iy", part, b.o_gin.at[blk, p.h], blk, blk, p.across)
-        send(b, "ic", part, b.o_gin.at[blk, p.h], blk, blk, p.core)
-    for blk in range(2):
-        b.o_gin[blk, p.h] = b.GIN[blk * g.IP : (blk + 1) * g.IP, :]
-
-
-def inputs_end(g, p, b):
-    for blk in range(2):
-        part = b.o_gin.at[blk, p.hy]
-        arrived(b, p, "iy", part, blk)
-        send(b, "id", part, part, blk, blk, p.core)
-    for blk in range(2):
-        arrived(b, p, "ic", b.o_gin.at[blk, p.hcore], blk)
-        arrived(b, p, "id", b.o_gin.at[blk, p.hdiag], blk)
+        b.o_gin[blk, 0:16, :] = b.ED[blk, 0, 0]
+        for i in range(1, g.NI):
+            b.o_gin[blk, i * g.WIN : i * g.WIN + 16, :] = b.ED[blk, i, 0] + b.ED[blk, i - 1, 1]
+        b.o_gin[blk, g.NI * g.WIN : g.NI * g.WIN + 16, :] = b.ED[blk, g.NI - 1, 1]
 
 
 def weights_back(g, p, b):
@@ -1004,31 +1132,24 @@
 
 def second_sends_end(g, p, b):
     n = g.ne
-    left(b, p, "gi", b.SI, 0)
-    left(b, p, "gb", b.SB, 0)
-
-    def rets(k):
-        left(b, p, "rc", b.RC.at[0, 0], k)
-        left(b, p, "ry", b.RY.at[0, 0], k)
-
-    loop(2 * n, rets)
+    left(b, p, "gi", b.XI, 0)
+    left(b, p, "gb", b.XB, 0)
+
+    back_end(g, p, b)
 
     def away(k):
-        s = p.other(k + 1)
-        left(b, p, "rz", b.RY.at[0, 0], s)
-        left(b, p, "rz", b.RY.at[0, 0], n + s)
         if g.aligned:
             left(b, p, "dz", b.SDZ.at[0], k)
             left(b, p, "sz", b.SMZ.at[0], k)
 
     loop(n - 1, away)
-    for at in range(3):
-        left(b, p, "ug", b.UG.at[0], at)
-        left(b, p, "uo", b.UO.at[0], at)
     for i in range(2):
         left(b, p, "dc", b.RDC.at[0], i)
-        for name in ("iy", "ic", "id"):
-            left(b, p, name, b.o_gin.at[0, 0], i)
+        left(b, p, "ug", b.UG.at[0 : g.IP, :], i)
+        left(b, p, "uo", b.UO.at[0 : g.IP, :], i)
+        for name in ("i", "j", "k"):
+            left(b, p, name + "m", b.o_gin.at[0, middle_of(g, 0), :], i)
+            left(b, p, name + "e", b.ED.at[0, 0], i)
     if g.aligned:
         left(b, p, "sx", b.SMX, 0)
 
@@ -1046,53 +1167,60 @@
 
 def second_kernel(g, b):
     p = Place(g)
+    fetch(b, "kRO", b.hRO, b.RB)
+    names = ("PT", "HID", "PRB", "RW", "GN", "UPO", "X", "PO", "GC", "W", "QKV", "PB", "ATT", "KI", "KB")
+    load(b, *names)
     p.enter()
-    returns_start(g, p, b, 1)
-    returns_start(g, p, b, 0)
+    loop(g.ne, lambda k: send(b, "rc", b.hPO.at[p.other(k), :, p.oc], b.RC.at[p.other(k)], p.other(k), p.other(k), p.core))
     grads_of_expert_out(g, p, b)
-    returns_over(g, p, b, 1)
+    fetched(b, "kRO", b.hRO, b.RB)
+    slots_back(g, p, b, 1)
+    loaded(b, "PT")
+    unpack(g, p, b, 1)
+    loaded(b, "GN", "X")
     first_norm_again(g, b)
-    returns_on(g, p, b, 1)
-    slots_back(g, p, b, 1)
-    unpack(g, p, b, 1)
     unpacked(g, p, b, 1)
-    returns_over(g, p, b, 0)
+    loaded(b, "PO")
+    loop(g.ne, lambda k: back_over(g, p, b, b.PO, p.other(k + 1)))
+    loaded(b, "HID", "PRB", "RW", "UPO")
     tokens_back(g, p, b)
+    loaded(b, "W", "QKV", "PB", "ATT", "GC")
     attention_back(g, p, b)
     inputs_back(g, p, b)
     weights_back(g, p, b)
     small_back(g, p, b)
     inputs_end(g, p, b)
     weights_back_on(g, p, b)
-    unpacked(g, p, b, 0)
-    mix(g, b)
     small_back_on(g, p, b)
+    mixed_in(g, p, b)
     grads_of_expert_in(g, p, b)
+    inputs_last(g, p, b)
     weights_back_end(g, p, b)
     second_sends_end(g, p, b)
 
 
-def call(body, g, inputs, outs, scratch, sems, number, flops):
-    names = [*inputs, *outs, *scratch]
-    names += [name + end for name in sems for end in ("_s", "_r")]
+def call(body, g, inputs, far, outs, far_outs, scratch, sems, number, flops):
+    names = [*inputs, *far, *outs, *far_outs, *scratch]
+    single = [n for n in sems if n[0] == "k" and n[1].isupper() or n.startswith("ld")]
+    names += [name + end for name in sems for end in (("_s",) if name in single else ("_s", "_r"))]
 
     def kernel(*refs):
         body(g, types.SimpleNamespace(**dict(zip(names, refs, strict=True))))
 
-    vmem = pl.BlockSpec(memory_space=pltpu.VMEM)
+    vmem, anywhere = pl.BlockSpec(memory_space=pltpu.VMEM), pl.BlockSpec(memory_space=pl.ANY)
     made = pl.pallas_call(
         kernel,
-        out_shape=[jax.ShapeDtypeStruct(*o) for o in outs.values()],
-        in_specs=[vmem] * len(inputs),
-        out_specs=[vmem] * len(outs),
+        out_shape=[jax.ShapeDtypeStruct(*o) for o in [*outs.values(), *far_outs.values()]],
+        in_specs=[vmem] * len(inputs) + [anywhere] * len(far),
+        out_specs=[vmem] * len(outs) + [anywhere] * len(far_outs),
         scratch_shapes=[pltpu.VMEM(*s) for s in scratch.values()]
-        + [pltpu.SemaphoreType.DMA((n,)) for n in sems.values() for _ in range(2)],
+        + [pltpu.SemaphoreType.DMA((n,)) for name, n in sems.items() for _ in range(1 if name in single else 2)],
         compiler_params=pltpu.CompilerParams(
             collective_id=number, has_side_effects=True, vmem_limit_bytes=LIMIT
         ),
         cost_estimate=pl.CostEstimate(flops=flops, bytes_accessed=2**24, transcendentals=0),
-    )(*inputs.values())
-    return dict(zip(outs, made, strict=True))
+    )(*inputs.values(), *far.values())
+    return dict(zip([*outs, *far_outs], made, strict=True))
 
 
 def shards(
@@ -1102,12 +1230,7 @@
     g = Sizes(mesh, model, rows, w_in.shape[2])
     n, ip, cp, dh = g.ne, g.IP, g.CP, g.DH
     assert inputs.shape[0] == 2
-    h = lax.axis_index("head")
     pad = ((0, 0), (0, 0), (0, ip - SEQ), (0, 0))
-    x_all = inputs.reshape(2, g.NI, SEQ, model)
-    x = jnp.pad(lax.dynamic_slice_in_dim(x_all, h, 1, 1), pad).reshape(2 * ip, model)
-    up_all = jnp.pad(cotangent.reshape(2, g.NI, SEQ, model), pad)
-    up_own = lax.dynamic_slice_in_dim(up_all, h, 1, 1).reshape(2 * ip, model)
     part = jnp.concatenate([w_qkv[:, 0], w_qkv[:, 2], w_qkv[:, 1], w_out.T], axis=1)
     gains = jnp.stack([gain_one, gain_two], axis=1)
     top = gains.astype(BF16)
@@ -1132,29 +1255,41 @@
     mc = jnp.pad(info.reshape(2, g.TP, 3), ((0, 0), (0, 0), (0, 5)))
     mr = jnp.swapaxes(mc, 1, 2)
     np_ = pieces(g)
+    kept = dict(
+        X=((2 * ip, model), BF16),
+        UPO=((2 * ip, model), BF16),
+        W=((4, model, model), BF16),
+        RW=((model, 128), BF16),
+        GN=((8, model), F32),
+        QKV=((4, 2 * ip, 640), BF16),
+        PB=((4, 6, ip, ip), BF16),
+        ATT=((4, 2 * ip, 256), BF16),
+        HID=((2 * ip, model), F32),
+        PRB=((2 * ip, 128), F32),
+        PT=((g.TP, g.SL), BF16),
+        GC=((n, cp, 128), F32),
+        PO=((n, 2, 2, cp, dh), BF16),
+        RO=((n, cp, dh), BF16),
+        KI=((dh, g.F), F32),
+        KB=((g.F, dh), F32),
+        SI=((dh, g.F), BF16),
+        SB=((g.F, dh), BF16),
+    )
+    assert set(kept) == set(KEEP)
     one = call(
         first_kernel,
         g,
-        dict(x=x, up=up_all.reshape(2, g.TP, model), wp=part, mp=small, wi=w_in[0], wb=w_back[0], mc=mc, mr=mr),
+        dict(wp=part, mp=small, wi=w_in[0], wb=w_back[0], mc=mc, mr=mr),
+        dict(xin=inputs, uin=cotangent),
+        {},
+        {"h" + name: made for name, made in kept.items()},
         dict(
-            W=((4, model, model), BF16),
-            RW=((model, 128), BF16),
-            GN=((8, model), F32),
-            QKV=((4, 2 * ip, 640), BF16),
-            PB=((4, 6, ip, ip), BF16),
-            ATT=((4, 2 * ip, 256), BF16),
-            HID=((2 * ip, model), F32),
-            PRB=((2 * ip, 128), F32),
-            PT=((g.TP, g.SL), BF16),
-            GC=((n, cp, 128), F32),
-            PO=((n, 2, 2, cp, dh), BF16),
+            **kept,
             PG=((n, 2, 2, cp, dh), BF16),
-            KI=((dh, g.F), F32),
-            KB=((g.F, dh), F32),
-            SI=((dh, g.F), BF16),
-            SB=((g.F, dh), BF16),
-        ),
-        dict(
+            RC=((n, 2, cp, dh), BF16),
+            RY=((n, cp, dh), BF16),
+            UB=((rows, model), BF16),
+            UPP=((g.TP, model), BF16),
             DI=((2, dh, g.F), F32),
             DB=((2, g.F, dh), F32),
             MI=((model, 128), BF16),
@@ -1164,8 +1299,8 @@
             ACT1=((2 * ip, model), BF16),
             ACT2=((2 * ip, model), BF16),
             PRH=((2 * ip, 128), BF16),
-            TA=((4, ip, dh), BF16),
-            TG=((4, ip, 128), BF16),
+            TA=((g.TP, dh), BF16),
+            TG=((g.TP, 128), BF16),
             US=((n, 2, cp, model), BF16),
             XS=((n, 2, 2, cp, dh), BF16),
             PKA=((n, cp, dh), BF16),
@@ -1176,11 +1311,11 @@
             HQ=((g.R, g.F), BF16),
             GR=((g.R, g.F), BF16),
         ),
-        dict(wz=n, mz=n, wx=n, mx=n, wy=np_, wc=np_, wd=np_, ta=4, tp=4, uz=n, uc=n, xz=n, xy=n, xc=n, xd=n, ei=1, eb=1),
+        dict(wz=n, mz=n, wx=n, mx=n, wy=np_, wc=np_, wd=np_, ta=1, tp=1, uz=n, uc=n, xz=n, xy=n, xc=n, xd=n, ei=1, eb=1,
+             rc=n, ry=n, rz=n, ldx=2, ldu=2, ldb=1, **{"k" + name: 1 for name in KEEP}),
         1,
         14 * 10**9,
     )
-    keep = ("W", "RW", "GN", "QKV", "PB", "ATT", "HID", "PRB", "PT", "GC", "PO", "PG", "KI", "KB", "SI", "SB")
     rows_out = g.PR if g.aligned else model
     extra = (
         dict(
@@ -1198,25 +1333,32 @@
     two = call(
         second_kernel,
         g,
-        dict(x=x, up=up_own, **{name: one[name] for name in keep}),
+        {},
+        {"h" + name: one["h" + name] for name in KEEP},
         dict(
-            o_mixed=((2 * ip, model), BF16),
-            o_gin=((2, 4, ip, model), BF16),
+            o_mixed=((2, SEQ, model), BF16),
+            o_gin=((2, rows, model), BF16),
             o_dw=((rows_out, model), F32 if g.aligned else BF16),
             o_small=((rows_out, 128), F32),
             o_gi=((dh, g.F), F32),
             o_gb=((g.F, dh), F32),
         ),
+        {},
         dict(
-            RC=((2, n, 2, cp, dh), BF16),
-            RY=((2, n, cp, dh), BF16),
-            RO=((2, n, cp, dh), BF16),
+            **{name: made for name, made in kept.items() if name not in ("SI", "SB", "RO")},
+            RO=((n, cp, dh), BF16),
+            RB=((n, cp, dh), BF16),
+            RC=((n, 2, cp, dh), BF16),
+            RY=((n, cp, dh), BF16),
             RG=((g.SL, dh + 128), BF16),
-            RB=((g.SL, dh), BF16),
-            UG=((3, ip, dh + 128), BF16),
-            UO=((3, ip, dh), BF16),
+            UG=((2 * ip, dh + 128), BF16),
+            UO=((2 * ip, dh), BF16),
             TR=((2, 2 * ip, dh + 128), BF16),
             TO=((2, 2 * ip, dh), BF16),
+            MX=((2 * ip, model), BF16),
+            MIX=((2, ip, model), BF16),
+            EG=((2, 2, 16, model), BF16),
+            ED=((2, 4, 2, 16, model), BF16),
             GL=((2 * ip, 128), BF16),
             GA=((16, model), F32),
             ACT1=((2 * ip, model), BF16),
@@ -1238,12 +1380,11 @@
             XB=((g.F, dh), BF16),
             **extra,
         ),
-        dict(rc=2 * n, ry=2 * n, rz=2 * n, ug=4, uo=4, gi=1, gb=1, dc=2, dy=n, dx=2 * n, dz=n, sx=1, sz=n, sc=1, sy=1, iy=2, ic=2, id=2),
+        dict(rc=n, ry=n, rz=n, ug=2, uo=2, mo=2, gi=1, gb=1, dc=2, dy=n, dx=2 * n, dz=n, sx=1, sz=n, sc=1, sy=1, im=2, ie=2, jm=2, je=2, km=2, ke=2,
+             **{"k" + name: 1 for name in KEEP if name not in ("SI", "SB")}),
         2,
         14 * 10**9,
     )
-    mixed = two["o_mixed"].reshape(2, ip, model)[:, :SEQ]
-    grad_inputs = two["o_gin"][:, :, :SEQ].reshape(2, rows, model)
     dw, ds = two["o_dw"], two["o_small"]
     if not g.aligned:
         dw = lax.psum_scatter(dw, ("dp", "expert"), scatter_dimension=0, tiled=True)
@@ -1252,8 +1393,8 @@
     lw = g.LW
     grad_qkv = jnp.stack([dw[:, :lw], dw[:, 2 * lw : 3 * lw], dw[:, lw : 2 * lw]], axis=1)
     return (
-        mixed,
-        grad_inputs,
+        two["o_mixed"],
+        two["o_gin"],
         grad_qkv,
         dw[:, 3 * lw :].T,
         ds[:, :n],

time: 259 us -> 219 us (0.85)
  Pallas kernels: 227 us -> 195 us
  local copies, waits for them, and re-layouts: 28.2 us -> 19.7 us
    pallas_call x2, Pallas kernels: 227 us -> 195 us  [call(): pl.pallas_call(kernel, out_shape=[jax.ShapeDtypeStruct(*o) for o in [*out...]
    reshape x3 -> x0, local copies, waits for them, and re-layouts: 7.33 us -> none  [the longest x1 2.61 us: shards(): x_all = inputs.reshape(2, g.NI, SEQ, model)]
    unnamed x14 -> x15, local copies, waits for them, and re-layouts: 8.16 us -> 11.5 us
    slice x2 -> x0, local copies, waits for them, and re-layouts: 3.02 us -> none  [the longest x1 1.85 us: shards(): grad_inputs = two['o_gin'][:, :, :SEQ].reshape(2, rows, model)]
where the time goes in v3:
time: 219 us; the launch traced here: 218 us
  Pallas kernels  195 us (89%)
  local copies, waits for them, and re-layouts  19.7 us (9%)
  other arithmetic  2.87 us (1%)
    pallas_call x2, Pallas kernels, call(): pl.pallas_call(kernel, out_shape=[jax.ShapeDtypeStruct(*o) for o in [*out...  195 us
    unnamed x15, local copies, waits for them, and re-layouts  11.5 us

profile of v3, /device:TPU:0, one launch (start us, length us, event | category | flops | bytes accessed | tf_op | source)
XLA Modules:
  0.0 218.1 jit_solution(17925881654085962777)
XLA Ops:
  0.6 0.7 subtract_convert_fusion
  1.3 0.7 fusion
  2.0 0.8 concatenate.17
  2.8 0.8 concatenate.16
  3.6 0.1 reshape.25
  3.8 0.1 copy.56
  3.9 0.1 copy.55
  4.0 0.1 copy.54
  4.1 0.1 copy.53
  4.3 0.8 copy.52
  5.1 0.7 concatenate.15.refs_1_
  5.8 0.9 copy.51
  6.7 0.6 pad_bitcast_fusion.refs_5_
  7.3 0.9 slice_bitcast_fusion.6
  8.2 0.8 pad_maximum_fusion.1.refs_0_
  9.0 0.3 copy.63
  9.3 1.0 pad.9.clone.refs_4_
  10.2 106.4 %shard_map.178 = (bf16[416,768]{1,0:T(8,128)(2,1)}, bf16[416,768]{1,0:T(8,128)(2,1)}, bf16[4,768,768]{2,1,0:T(8,128)(2,1)}, bf16[768,128]{1,0:T(8,128)(2,1)}, f3...) custom-call(bf16[96,768]{1,0:T(8,128)(2,1)} %pad_maximum_fusion.1.re, ...), custom_call_target="tpu_custom_call" | custom-call | flops 14000000000 | bytes 16777216 | tf_op jit(solution)/shard_map/pallas_call | solution.py:1211
  116.7 88.3 %shard_map.179 = (bf16[2,196,768]{2,1,0:T(8,128)(2,1)}, bf16[2,784,768]{2,1,0:T(8,128)(2,1)}, f32[96,768]{1,0:T(8,128)}, f32[96,128]{1,0:T(8,128)}, f32[384,768]{1,0:T(8,128)}, /*index=5*/f32[768,384]{1,0:T(8,128)}) custom-call(bf16[416,768]{1,0:T(8,128)(2,1)} %get-tuple-element.33.refs_0_, bf16[416,768]{1,0:T(8,128)(2,1)} %get-tuple-element.34.refs_1_, ...), custom_call_target="tpu_custom_call" | custom-call | flops 14000000000 | bytes 16777216 | tf_op jit(solution)/shard_map/pallas_call | solution.py:1211
  205.1 0.0 copy-start
  205.1 2.5 %copy.60 = bf16[2,196,768]{2,0,1:T(2,128)(2,1)} copy(bf16[2,196,768]{2,1,0:T(8,128)(2,1)} %get-tuple-element.84) | data formatting | bytes 1204224
  207.6 1.6 slice_reduce_fusion
  209.2 1.4 copy.62
  210.6 1.2 slice_bitcast_fusion
  211.8 0.7 copy.61
  212.5 0.7 pad_maximum_fusion
  213.3 0.0 copy-done
  213.3 0.0 copy-start.2
  213.3 1.4 copy.69
  214.7 0.7 copy-done.2
  215.4 0.0 copy-start.1
  215.4 1.0 copy.70
  216.4 0.7 copy-done.1
  217.1 1.0 copy.71
  (7 shorter events, 0.1 us)
Async XLA Ops:
  205.1 8.2 %copy-start = (bf16[2,784,768]{2,1,0:T(8,128)(2,1)S(1)}, bf16[2,784,768]{2,1,0:T(8,128)(2,1)}, u32[]{:S(2)}) copy-start(bf16[2,784,768]{2,1,0:T(8,128)(2,1)} %get-tuple-element.116) | copy-start | bytes 7225348
  213.3 2.1 copy-start.2
  215.4 1.7 copy-start.1

commit v4 on v3

--- a/solution.py
+++ b/solution.py
@@ -85,6 +85,7 @@
         self.LW = model // self.nh
         assert self.nd == 2 and self.nh == 4 and self.NI == 4 and self.LW == 3 * HD
         assert (self.NI - 1) * self.WIN + self.IP <= rows and (self.NI - 1) * self.LAG + SEQ <= self.IP
+        assert self.ne & (self.ne - 1) == 0
         assert self.ne <= 64 and 0 <= self.CAP - (self.CP - 16) <= 14
 
 
@@ -106,12 +107,16 @@
         self.twin = (self.od, self.e, self.h)
 
     def other(self, k):
-        return lax.rem(self.e + k, self.ne)
+        index, bit = 0, 1
+        while bit < self.ne:
+            index = index + lax.rem(lax.div(self.e, bit) + k // bit, 2) * bit
+            bit *= 2
+        return index
 
     def along(self, e2):
         return (self.d, e2, self.h)
 
-    def enter(self):
+    def enter(self, wide=False):
         barrier = pltpu.get_barrier_semaphore()
 
         def tell(device):
@@ -120,7 +125,9 @@
         for device in (self.core, self.across, self.diag, self.twin):
             tell(device)
         loop(self.ne - 1, lambda k: tell(self.along(self.other(k + 1))))
-        pl.semaphore_wait(barrier, 4 + self.ne - 1)
+        if wide:
+            loop(self.ne - 1, lambda k: tell((self.od, self.other(k + 1), self.h)))
+        pl.semaphore_wait(barrier, 4 + (self.ne - 1) * (2 if wide else 1))
 
 
 def copy(b, name, src, dst, si, ri, device):
@@ -192,7 +199,7 @@
         rows = slice(j * g.IP, (j + 1) * g.IP)
         fetch(b, "ldx", b.xin.at[p.y, window(g, 2 * p.c + j), :], b.X.at[rows, :], j)
         fetch(b, "ldu", b.uin.at[p.y, window(g, 2 * p.c + j), :], b.UPO.at[rows, :], j)
-    fetch(b, "ldb", b.uin.at[p.c], b.UB)
+    fetch(b, "ldb", b.uin.at[p.c, :, half_of(g, p.y)], b.UB)
 
 
 def rows_in(g, p, b):
@@ -203,7 +210,7 @@
         hot = shift(g, 2 * p.c + j)
         b.X[rows, :] = nn(hot, b.X[rows, :]).astype(BF16)
         b.UPO[rows, :] = nn(hot, b.UPO[rows, :]).astype(BF16)
-    fetched(b, "ldb", b.uin.at[p.c], b.UB)
+    fetched(b, "ldb", b.uin.at[p.c, :, half_of(g, p.y)], b.UB)
     for i in range(g.NI):
         b.UPP[i * g.IP : (i + 1) * g.IP, :] = nn(
             shift(g, i), b.UB[i * g.WIN : i * g.WIN + g.IP, :]
@@ -362,6 +369,16 @@
 
     def group(k):
         group_in(g, p, b, k)
+
+        @pl.when(k == 1)
+        def _():
+            loop(g.ne // 2 - 1, lambda i: cotangent_on(g, p, b, p.other(i + 1)))
+            cotangent_over(g, p, b, p.e)
+
+        @pl.when(k == 3)
+        def _():
+            loop(g.ne - g.ne // 2, lambda i: cotangent_on(g, p, b, p.other(i + g.ne // 2)))
+
         gi = 2 * lax.rem(p.y + lax.div(k, 2), 2) + lax.rem(p.c + k, 2)
         for blk in range(2):
             rows = slice(blk * g.IP, (blk + 1) * g.IP)
@@ -458,30 +475,35 @@
 
 def cotangent_out(g, p, b):
     def pack(k):
-        e2 = p.other(k + 1)
+        e2 = p.other(k)
         rows = nn(b.P[pack_rows(g, e2), :], b.UPP[...]).astype(BF16)
-        b.PKU[e2] = rows
-
-        @pl.when(k < g.ne - 1)
+
+        @pl.when(k > 0)
         def _():
-            send(b, "uz", b.PKU.at[e2], b.US.at[p.e, p.c], k, p.e, p.along(e2))
-
-        @pl.when(k == g.ne - 1)
+            b.PKU[e2] = rows
+            send(b, "uz", b.PKU.at[e2], b.US.at[p.e, p.c, p.y], k, p.e, p.along(e2))
+
+        @pl.when(k == 0)
         def _():
-            b.US[p.e, p.c] = rows
-            send(b, "uc", b.US.at[p.e, p.c], b.US.at[p.e, p.c], p.e, p.e, p.core)
+            part = b.US.at[p.e, p.c, p.y]
+            b.US[p.e, p.c, p.y] = rows
+            send(b, "uy", part, part, p.e, p.e, p.across)
+            send(b, "uc", part, part, p.e, p.e, p.core)
 
     loop(g.ne, pack)
 
 
-def cotangent_on(g, p, b):
-    def relay(k):
-        e2 = p.other(k + 1)
-        part = b.US.at[e2, p.c]
-        arrived(b, p, "uz", part, e2)
-        send(b, "uc", part, part, e2, e2, p.core)
-
-    loop(g.ne - 1, relay)
+def cotangent_on(g, p, b, e2):
+    part = b.US.at[e2, p.c, p.y]
+    arrived(b, p, "uz", part, e2)
+    send(b, "uy", part, part, e2, e2, p.across)
+    send(b, "uc", part, part, e2, e2, p.core)
+
+
+def cotangent_over(g, p, b, e2):
+    part = b.US.at[e2, p.c, p.oy]
+    arrived(b, p, "uy", part, e2)
+    send(b, "ud", part, part, e2, e2, p.core)
 
 
 def slots_out(g, p, b):
@@ -490,7 +512,7 @@
     lane = iota((g.CP, 128), 1)
 
     def pack(k):
-        e2 = p.other(k + 1)
+        e2 = p.other(k)
         hot = b.P[pack_rows(g, e2), :]
         tok = nn(hot, b.TA[...])
         gates = nn(hot, b.TG[...])
@@ -503,12 +525,12 @@
         rows = jnp.where(row == g.CAP, top, jnp.where(row == g.CAP + 1, across - top, tok))
         rows = rows.astype(BF16)
 
-        @pl.when(k < g.ne - 1)
+        @pl.when(k > 0)
         def _():
             b.PKA[e2] = rows
             send(b, "xz", b.PKA.at[e2], b.XS.at[p.e, p.y, p.c], k, p.e, p.along(e2))
 
-        @pl.when(k == g.ne - 1)
+        @pl.when(k == 0)
         def _():
             part = b.XS.at[p.e, p.y, p.c]
             b.XS[p.e, p.y, p.c] = rows
@@ -534,14 +556,30 @@
 def slots_in(g, p, b, e2):
     arrived(b, p, "xc", b.XS.at[e2, p.y, p.oc], e2)
     arrived(b, p, "xd", b.XS.at[e2, p.oy, p.oc], e2)
-    arrived(b, p, "uc", b.US.at[e2, p.oc], e2)
-
-
-def experts_out(g, p, b):
-    b.WI[p.d] = b.wi[...]
-    b.WB[p.d] = b.wb[...]
-    send(b, "ei", b.wi, b.WI.at[p.d], 0, 0, p.twin)
-    send(b, "eb", b.wb, b.WB.at[p.d], 0, 0, p.twin)
+    arrived(b, p, "uc", b.US.at[e2, p.oc, p.y], e2)
+    arrived(b, p, "ud", b.US.at[e2, p.oc, p.oy], e2)
+
+
+CHUNKS = 4
+
+
+def chunk(rows, i):
+    size = rows // CHUNKS
+    return pl.ds(i * size, size)
+
+
+def experts_out(g, p, b, which):
+    for i in which:
+        name, src, dst = ("ei", b.wi, b.WI) if i < CHUNKS else ("eb", b.wb, b.WB)
+        rows = chunk(src.shape[0], i % CHUNKS)
+        send(b, name, src.at[rows, :], dst.at[p.d, rows, :], i % CHUNKS, i % CHUNKS, p.twin)
+
+
+def experts_in(g, p, b):
+    for i in range(CHUNKS):
+        arrived(b, p, "ei", b.WI.at[p.od, chunk(g.DH, i), :], i)
+    for i in range(CHUNKS):
+        arrived(b, p, "eb", b.WB.at[p.od, chunk(g.F, i), :], i)
 
 
 def back_core(g, p, b, part, s):
@@ -597,7 +635,7 @@
     return value, slope
 
 
-def expert(g, b, first):
+def expert(g, b, first, between=None):
     base = g.CP - 16
     row = iota((g.CP, g.DH), 0)
     eye = row == iota((g.CP, g.DH), 1)
@@ -607,7 +645,10 @@
             gate = tail[g.CAP - base : g.CAP - base + 1] + tail[g.CAP - base + 1 : g.CAP - base + 2]
             gate = jnp.sum(jnp.where(eye, gate, 0.0), axis=1, keepdims=True)
             at = (i * 2 + blk) * g.CP
-            b.GP[at : at + g.CP, :] = (b.US[first + i, blk].astype(F32) * gate).astype(BF16)
+            for q in range(2):
+                b.GP[at : at + g.CP, q * g.DH : (q + 1) * g.DH] = (
+                    b.US[first + i, blk, q].astype(F32) * gate
+                ).astype(BF16)
     x = [b.XS[pl.ds(first, g.SG), :, q].reshape(g.R, g.DH) for q in range(2)]
     for n in range(g.F // 256):
         cols = slice(n * 256, n * 256 + 256)
@@ -616,12 +657,14 @@
         b.HQ[:, cols] = value.astype(BF16)
         grad = nt(b.GP[:, : g.DH], b.WB[0, cols, :]) + nt(b.GP[:, g.DH :], b.WB[1, cols, :])
         b.GR[:, cols] = (grad * slope).astype(BF16)
+    if between is not None:
+        between()
     shape = (g.SG, 2, g.CP, g.DH)
     dots = []
     for q in range(2):
         out = nn(b.HQ[...], b.WB[q]).astype(BF16)
         b.PO[pl.ds(first, g.SG), :, q] = out.reshape(shape)
-        up = b.US[pl.ds(first, g.SG), :, :, q * g.DH : (q + 1) * g.DH].reshape(g.R, g.DH)
+        up = b.US[pl.ds(first, g.SG), :, q].reshape(g.R, g.DH)
         dots.append(jnp.sum(out.astype(F32) * up.astype(F32), axis=1, keepdims=True))
         b.DB[q] += tn(b.HQ[...], b.GP[:, q * g.DH : (q + 1) * g.DH])
         b.DI[q] += tn(x[q], b.GR[...])
@@ -644,38 +687,43 @@
     b.DI[...] = jnp.zeros_like(b.DI)
     n = g.ne
     if g.SG > 1:
+        loop(n - 1, lambda k: cotangent_over(g, p, b, p.other(k + 1)))
         loop(n - 1, lambda k: slots_on(g, p, b, p.other(k + 1)))
         loop(n, lambda k: slots_over(g, p, b, p.other(k)))
         loop(n, lambda k: slots_in(g, p, b, p.other(k)))
-        arrived(b, p, "ei", b.WI.at[p.od], 0)
-        arrived(b, p, "eb", b.WB.at[p.od], 0)
+        experts_in(g, p, b)
         loop(n // g.SG, lambda t: expert(g, b, t * g.SG))
         loop(n, lambda k: back_core(g, p, b, b.PG, p.other(k)))
         loop(n, lambda k: back_over(g, p, b, b.PG, p.other(k)))
-        loop(n, lambda k: back_on(g, p, b, b.PG, p.other(k)))
+        loop(n - 1, lambda k: back_on(g, p, b, b.PG, p.other(k)))
         return
+    loop(n - 1, lambda k: cotangent_over(g, p, b, p.other(k + 1)))
     slots_over(g, p, b, p.e)
     slots_in(g, p, b, p.e)
-    arrived(b, p, "ei", b.WI.at[p.od], 0)
-    arrived(b, p, "eb", b.WB.at[p.od], 0)
+    experts_in(g, p, b)
 
     def source(k):
-        @pl.when(k == 1)
-        def _():
-            loop(n - 1, lambda i: slots_on(g, p, b, p.other(i + 1)))
-
         @pl.when(k > 0)
         def _():
             back_over(g, p, b, b.PG, p.other(k - 1))
             slots_over(g, p, b, p.other(k))
             slots_in(g, p, b, p.other(k))
 
-        expert(g, b, p.other(k))
+        def between():
+            @pl.when(k < n - 1)
+            def _():
+                slots_on(g, p, b, p.other(k + 1))
+
+            @pl.when(k > 1)
+            def _():
+                back_on(g, p, b, b.PG, p.other(k - 2))
+
+        expert(g, b, p.other(k), between)
         back_core(g, p, b, b.PG, p.other(k))
 
     loop(n, source)
+    back_on(g, p, b, b.PG, p.other(n - 2))
     back_over(g, p, b, b.PG, p.other(n - 1))
-    loop(n, lambda k: back_on(g, p, b, b.PG, p.other(k)))
 
 
 def first_sends_end(g, p, b):
@@ -704,19 +752,21 @@
     left(b, p, "tp", b.TG.at[own_rows(g, 0), :], 0)
 
     def slots(k):
-        left(b, p, "uz", b.PKU.at[0], k)
-        left(b, p, "xz", b.PKA.at[0], k)
+        left(b, p, "uz", b.PKU.at[0], k + 1)
+        left(b, p, "xz", b.PKA.at[0], k + 1)
 
     loop(n - 1, slots)
 
     def on(k):
-        left(b, p, "uc", b.US.at[0, 0], k)
+        for name in ("uy", "uc", "ud"):
+            left(b, p, name, b.US.at[0, 0, 0], k)
         for name in ("xy", "xc", "xd"):
             left(b, p, name, b.XS.at[0, 0, 0], k)
 
     loop(n, on)
-    left(b, p, "ei", b.wi, 0)
-    left(b, p, "eb", b.wb, 0)
+    for i in range(CHUNKS):
+        left(b, p, "ei", b.wi.at[chunk(g.DH, 0), :], i)
+        left(b, p, "eb", b.wb.at[chunk(g.F, 0), :], i)
 
 
 KEEP = ("X", "UPO", "W", "RW", "GN", "QKV", "PB", "ATT", "HID", "PRB", "PT", "GC", "PO", "RO", "KI", "KB", "SI", "SB")
@@ -727,12 +777,15 @@
     rows_out(g, p, b)
     p.enter()
     weights_out(g, p, b)
+    experts_out(g, p, b, range(2))
+    b.WI[p.d] = b.wi[...]
+    b.WB[p.d] = b.wb[...]
     rows_in(g, p, b)
     route(g, b, p.c, False)
     weights_on(g, p, b)
     cotangent_out(g, p, b)
     weights_end(g, p, b)
-    experts_out(g, p, b)
+    experts_out(g, p, b, range(2, 2 * CHUNKS))
     route(g, b, p.y, True)
     small_weights(g, b)
     first_norm(g, b)
@@ -742,7 +795,6 @@
     second_norm(g, b)
     stow(b, "PRB")
     tokens_out(g, p, b)
-    cotangent_on(g, p, b)
     tokens_in(g, p, b)
     slots_out(g, p, b)
     stow(b, "GC")
@@ -753,6 +805,7 @@
     b.SI[...] = b.DI[p.od].astype(BF16)
     b.SB[...] = b.DB[p.od].astype(BF16)
     stow(b, "KI", "KB", "SI", "SB")
+    back_on(g, p, b, b.PG, p.other(g.ne - 1))
     back_in(g, p, b)
     stow(b, "RO")
     first_sends_end(g, p, b)
@@ -889,23 +942,17 @@
     b.DA[...] = jnp.zeros_like(b.DA)
 
     def group(k):
-        @pl.when(k == 1)
-        def _():
-            loop(g.ne, lambda i: back_on(g, p, b, b.PO, p.other(i + 1)))
-
         @pl.when(k == 2)
         def _():
-            back_in(g, p, b)
-            slots_back(g, p, b, 0)
-            unpack(g, p, b, 0)
+            loop(g.ne // 2, lambda i: back_on(g, p, b, b.PO, p.other(i + 1)))
 
         @pl.when(k == 3)
         def _():
-            unpacked(g, p, b, 0)
-            mix(g, p, b)
-
-        yk = lax.rem(p.oy + k, 2)
-        gi = 2 * yk + lax.rem(p.oc + lax.div(k, 2), 2)
+            loop(g.ne - g.ne // 2, lambda i: back_on(g, p, b, b.PO, p.other(i + g.ne // 2 + 1)))
+            weights_back(g, p, b, 0, 1)
+
+        yk = lax.rem(p.oy + lax.div(k, 2), 2)
+        gi = 2 * yk + lax.rem(p.oc + k, 2)
         for blk in range(2):
             rows = slice(blk * g.IP, (blk + 1) * g.IP)
             grad = nn(b.GHL[rows, :], b.W[gi, :, 512:768]).astype(BF16)
@@ -942,11 +989,11 @@
             b.DW[gi, cols, 512:640] = (first[:, 512:] + second[:, 0:128]).astype(BF16)
             b.DW[gi, cols, 640:768] = second[:, 128:].astype(BF16)
 
-        @pl.when(k < 2)
+        @pl.when(lax.rem(k, 2) == 0)
         def _():
             send(b, "dc", b.DW.at[gi], b.RDC.at[yk], yk, yk, p.core)
 
-        @pl.when(k >= 2)
+        @pl.when(lax.rem(k, 2) == 1)
         def _():
             arrived(b, p, "dc", b.RDC.at[yk], yk)
             if g.aligned:
@@ -1017,14 +1064,15 @@
         b.o_gin[blk, g.NI * g.WIN : g.NI * g.WIN + 16, :] = b.ED[blk, g.NI - 1, 1]
 
 
-def weights_back(g, p, b):
+def weights_back(g, p, b, first, count):
     if not g.aligned:
-        b.DW[p.hy] = (b.DW[p.hy].astype(F32) + b.RDC[p.oy].astype(F32)).astype(BF16)
-        send(b, "dy", b.DW.at[p.hy], b.RDY, 0, 0, p.across)
+        if first == 0:
+            b.DW[p.hy] = (b.DW[p.hy].astype(F32) + b.RDC[p.oy].astype(F32)).astype(BF16)
+            send(b, "dy", b.DW.at[p.hy], b.RDY, 0, 0, p.across)
         return
 
     def to_across(i):
-        e2 = p.other(i + 1)
+        e2 = p.other(first + i + 1)
         rows = piece_rows(g, p.d, e2)
         arrived(b, p, "dx", b.RDX.at[p.oy, e2], p.oy * g.ne + e2)
         b.RDX[p.oy, e2] = (
@@ -1034,7 +1082,7 @@
         ).astype(BF16)
         send(b, "dy", b.RDX.at[p.oy, e2], b.RDY.at[e2], e2, e2, p.across)
 
-    loop(g.ne, to_across)
+    loop(count, to_across)
 
 
 def weights_back_on(g, p, b):
@@ -1086,48 +1134,53 @@
     two = jnp.sum(b.GA[8:16, :], axis=0, keepdims=True)
     gains = jnp.where(sub == 120, one, jnp.where(sub == 122, two, 0.0))
     b.GM[...] = tn(b.ACT2[...], b.GL[...]) + jnp.transpose(gains)
-    if g.aligned:
-        half = g.D // 2
-        b.SMX[...] = b.GM[pl.ds(pl.multiple_of(p.od * half, 16), half), :].astype(BF16)
-        send(b, "sx", b.SMX, b.RMX, 0, 0, p.twin)
+    if not g.aligned:
+        b.SMC[...] = b.GM[...].astype(BF16)
+        return
+    b.SMX[...] = b.GM[...].astype(BF16)
+    mine = p.d * g.ne + p.e
+
+    def to(k):
+        for far, d2 in enumerate((p.d, p.od)):
+            e2 = p.other(k)
+            part = b.SMX.at[piece_rows(g, d2, e2), :]
+
+            @pl.when((k > 0) | (far > 0))
+            def _(far=far, d2=d2, e2=e2, part=part):
+                send(b, "sp", part, b.RMP.at[mine], far * g.ne + k, mine, (d2, e2, p.h))
+
+    loop(g.ne, to)
 
 
 def small_back_on(g, p, b):
     if g.aligned:
-        arrived(b, p, "sx", b.RMX, 0)
-
-        def piece(k):
-            e2 = p.other(k + 1)
-            mine = b.GM[piece_rows(g, p.d, e2), :] + b.RMX[
-                pl.ds(pl.multiple_of(e2 * g.PR, 16), g.PR), :
-            ].astype(F32)
-
-            @pl.when(k < g.ne - 1)
-            def _():
-                b.SMZ[e2] = mine.astype(BF16)
-                send(b, "sz", b.SMZ.at[e2], b.RMZ.at[p.e], k, p.e, p.along(e2))
-
-            @pl.when(k == g.ne - 1)
-            def _():
-                b.o_small[...] = mine
-
-        loop(g.ne, piece)
-
-        def add(k):
-            e2 = p.other(k + 1)
-            arrived(b, p, "sz", b.RMZ.at[e2], e2)
-            b.o_small[...] += b.RMZ[e2].astype(F32)
-
-        loop(g.ne - 1, add)
-    else:
-        b.o_small[...] = b.GM[...]
-    b.SMC[...] = b.o_small[...].astype(BF16)
-    send(b, "sc", b.SMC, b.RMC, 0, 0, p.core)
-    arrived(b, p, "sc", b.RMC, 0)
-    b.SMY[...] = (b.SMC[...].astype(F32) + b.RMC[...].astype(F32)).astype(BF16)
-    send(b, "sy", b.SMY, b.RMY, 0, 0, p.across)
-    arrived(b, p, "sy", b.RMY, 0)
-    b.o_small[...] = b.SMY[...].astype(F32) + b.RMY[...].astype(F32)
+        mine = p.d * g.ne + p.e
+        b.RMP[mine] = b.SMX[piece_rows(g, p.d, p.e), :]
+
+        def come(k):
+            for far, d2 in enumerate((p.d, p.od)):
+                at = d2 * g.ne + p.other(k)
+
+                @pl.when((k > 0) | (far > 0))
+                def _(at=at):
+                    arrived(b, p, "sp", b.RMP.at[at], at)
+
+        loop(g.ne, come)
+        total = b.RMP[0].astype(F32)
+        for i in range(1, g.nd * g.ne):
+            total = total + b.RMP[i].astype(F32)
+        b.SMC[...] = total.astype(BF16)
+    for i, device in enumerate((p.core, p.across, p.diag)):
+        send(b, "sh", b.SMC, b.RMH.at[p.h], i, p.h, device)
+    b.RMH[p.h] = b.SMC[...]
+
+
+def small_back_end(g, p, b):
+    for h2 in (p.hcore, p.hy, p.hdiag):
+        arrived(b, p, "sh", b.RMH.at[h2], h2)
+    b.o_small[...] = (b.RMH[0].astype(F32) + b.RMH[1].astype(F32)) + (
+        b.RMH[2].astype(F32) + b.RMH[3].astype(F32)
+    )
 
 
 def second_sends_end(g, p, b):
@@ -1140,7 +1193,7 @@
     def away(k):
         if g.aligned:
             left(b, p, "dz", b.SDZ.at[0], k)
-            left(b, p, "sz", b.SMZ.at[0], k)
+            left(b, p, "sp", b.RMP.at[0], k + 1)
 
     loop(n - 1, away)
     for i in range(2):
@@ -1151,9 +1204,9 @@
             left(b, p, name + "m", b.o_gin.at[0, middle_of(g, 0), :], i)
             left(b, p, name + "e", b.ED.at[0, 0], i)
     if g.aligned:
-        left(b, p, "sx", b.SMX, 0)
 
         def moved(k):
+            left(b, p, "sp", b.RMP.at[0], g.ne + k)
             left(b, p, "dx", b.RDX.at[0, 0], k)
             left(b, p, "dx", b.RDX.at[0, 0], g.ne + k)
             left(b, p, "dy", b.RDY.at[0], k)
@@ -1161,40 +1214,52 @@
         loop(n, moved)
     else:
         left(b, p, "dy", b.RDY, 0)
-    left(b, p, "sc", b.SMC, 0)
-    left(b, p, "sy", b.SMY, 0)
+    for i in range(3):
+        left(b, p, "sh", b.SMC, i)
 
 
 def second_kernel(g, b):
     p = Place(g)
     fetch(b, "kRO", b.hRO, b.RB)
-    names = ("PT", "HID", "PRB", "RW", "GN", "UPO", "X", "PO", "GC", "W", "QKV", "PB", "ATT", "KI", "KB")
+    names = ("PT", "PO", "GN", "X", "HID", "PRB", "RW", "UPO", "GC", "W", "QKV", "PB", "ATT", "KI", "KB")
     load(b, *names)
-    p.enter()
-    loop(g.ne, lambda k: send(b, "rc", b.hPO.at[p.other(k), :, p.oc], b.RC.at[p.other(k)], p.other(k), p.other(k), p.core))
+    p.enter(g.aligned)
+
+    def outputs_out(k):
+        s = p.other(k + 1)
+        send(b, "rc", b.hPO.at[s, :, p.oc], b.RC.at[s], s, s, p.core)
+
+    loop(g.ne, outputs_out)
     grads_of_expert_out(g, p, b)
     fetched(b, "kRO", b.hRO, b.RB)
     slots_back(g, p, b, 1)
     loaded(b, "PT")
     unpack(g, p, b, 1)
+    loaded(b, "PO")
+    loop(g.ne, lambda k: back_over(g, p, b, b.PO, p.other(k + 1)))
     loaded(b, "GN", "X")
     first_norm_again(g, b)
     unpacked(g, p, b, 1)
-    loaded(b, "PO")
-    loop(g.ne, lambda k: back_over(g, p, b, b.PO, p.other(k + 1)))
     loaded(b, "HID", "PRB", "RW", "UPO")
     tokens_back(g, p, b)
     loaded(b, "W", "QKV", "PB", "ATT", "GC")
     attention_back(g, p, b)
+    weights_back(g, p, b, 1, 1)
     inputs_back(g, p, b)
-    weights_back(g, p, b)
     small_back(g, p, b)
+    weights_back(g, p, b, 2, g.ne - 2)
+    back_in(g, p, b)
+    slots_back(g, p, b, 0)
+    unpack(g, p, b, 0)
     inputs_end(g, p, b)
+    unpacked(g, p, b, 0)
+    mix(g, p, b)
+    small_back_on(g, p, b)
     weights_back_on(g, p, b)
-    small_back_on(g, p, b)
     mixed_in(g, p, b)
     grads_of_expert_in(g, p, b)
     inputs_last(g, p, b)
+    small_back_end(g, p, b)
     weights_back_end(g, p, b)
     second_sends_end(g, p, b)
 
@@ -1288,8 +1353,8 @@
             PG=((n, 2, 2, cp, dh), BF16),
             RC=((n, 2, cp, dh), BF16),
             RY=((n, cp, dh), BF16),
-            UB=((rows, model), BF16),
-            UPP=((g.TP, model), BF16),
+            UB=((rows, dh), BF16),
+            UPP=((g.TP, dh), BF16),
             DI=((2, dh, g.F), F32),
             DB=((2, g.F, dh), F32),
             MI=((model, 128), BF16),
@@ -1301,17 +1366,17 @@
             PRH=((2 * ip, 128), BF16),
             TA=((g.TP, dh), BF16),
             TG=((g.TP, 128), BF16),
-            US=((n, 2, cp, model), BF16),
+            US=((n, 2, 2, cp, dh), BF16),
             XS=((n, 2, 2, cp, dh), BF16),
             PKA=((n, cp, dh), BF16),
-            PKU=((n, cp, model), BF16),
+            PKU=((n, cp, dh), BF16),
             WI=((2, dh, g.F), BF16),
             WB=((2, g.F, dh), BF16),
             GP=((g.R, model), BF16),
             HQ=((g.R, g.F), BF16),
             GR=((g.R, g.F), BF16),
         ),
-        dict(wz=n, mz=n, wx=n, mx=n, wy=np_, wc=np_, wd=np_, ta=1, tp=1, uz=n, uc=n, xz=n, xy=n, xc=n, xd=n, ei=1, eb=1,
+        dict(wz=n, mz=n, wx=n, mx=n, wy=np_, wc=np_, wd=np_, ta=1, tp=1, uz=n, uy=n, uc=n, ud=n, xz=n, xy=n, xc=n, xd=n, ei=CHUNKS, eb=CHUNKS,
              rc=n, ry=n, rz=n, ldx=2, ldu=2, ldb=1, **{"k" + name: 1 for name in KEEP}),
         1,
         14 * 10**9,
@@ -1322,10 +1387,8 @@
             RDX=((2, n, g.PR, model), BF16),
             SDZ=((n, g.PR, model), BF16),
             RDZ=((n, g.PR, model), BF16),
-            SMX=((model // 2, 128), BF16),
-            RMX=((model // 2, 128), BF16),
-            SMZ=((n, g.PR, 128), BF16),
-            RMZ=((n, g.PR, 128), BF16),
+            SMX=((model, 128), BF16),
+            RMP=((g.nd * n, g.PR, 128), BF16),
         )
         if g.aligned
         else {}
@@ -1373,14 +1436,12 @@
             GIN=((2 * ip, model), BF16),
             GM=((model, 128), F32),
             SMC=((rows_out, 128), BF16),
-            RMC=((rows_out, 128), BF16),
-            SMY=((rows_out, 128), BF16),
-            RMY=((rows_out, 128), BF16),
+            RMH=((4, rows_out, 128), BF16),
             XI=((dh, g.F), BF16),
             XB=((g.F, dh), BF16),
             **extra,
         ),
-        dict(rc=n, ry=n, rz=n, ug=2, uo=2, mo=2, gi=1, gb=1, dc=2, dy=n, dx=2 * n, dz=n, sx=1, sz=n, sc=1, sy=1, im=2, ie=2, jm=2, je=2, km=2, ke=2,
+        dict(rc=n, ry=n, rz=n, ug=2, uo=2, mo=2, gi=1, gb=1, dc=2, dy=n, dx=2 * n, dz=n, sp=2 * n, sh=4, im=2, ie=2, jm=2, je=2, km=2, ke=2,
              **{"k" + name: 1 for name in KEEP if name not in ("SI", "SB")}),
         2,
         14 * 10**9,

time: 219 us -> 205 us (0.936)
  Pallas kernels: 195 us -> 181 us
    pallas_call x2, Pallas kernels: 195 us -> 181 us  [call(): pl.pallas_call(kernel, out_shape=[jax.ShapeDtypeStruct(*o) for o in [*out...]
where the time goes in v4:
time: 205 us
  Pallas kernels  181 us (88%)
  local copies, waits for them, and re-layouts  19.7 us (10%)
  other arithmetic  2.87 us (1%)
    pallas_call x2, Pallas kernels, call(): pl.pallas_call(kernel, out_shape=[jax.ShapeDtypeStruct(*o) for o in [*out...  181 us
    unnamed x15, local copies, waits for them, and re-layouts  11.5 us

profile of v4, /device:TPU:0, one launch (start us, length us, event | category | flops | bytes accessed | tf_op | source)
XLA Modules:
  0.0 204.5 jit_solution(3775208614070497099)
XLA Ops:
  0.6 0.7 subtract_convert_fusion
  1.3 0.7 fusion
  2.0 0.8 concatenate.17
  2.8 0.8 concatenate.16
  3.6 0.1 reshape.25
  3.8 0.1 copy.56
  3.9 0.1 copy.55
  4.0 0.1 copy.54
  4.1 0.1 copy.53
  4.3 0.8 copy.52
  5.1 0.7 concatenate.15.refs_1_
  5.8 0.9 copy.51
  6.7 0.6 pad_bitcast_fusion.refs_5_
  7.3 0.9 slice_bitcast_fusion.6
  8.2 0.8 pad_maximum_fusion.1.refs_0_
  9.0 0.3 copy.63
  9.3 1.0 pad.9.clone.refs_4_
  10.2 104.1 %shard_map.178 = (bf16[416,768]{1,0:T(8,128)(2,1)}, bf16[416,768]{1,0:T(8,128)(2,1)}, bf16[4,768,768]{2,1,0:T(8,128)(2,1)}, bf16[768,128]{1,0:T(8,128)(2,1)}, f3...) custom-call(bf16[96,768]{1,0:T(8,128)(2,1)} %pad_maximum_fusion.1.re, ...), custom_call_target="tpu_custom_call" | custom-call | flops 14000000000 | bytes 16777216 | tf_op jit(solution)/shard_map/pallas_call | solution.py:1276
  114.4 77.1 %shard_map.179 = (bf16[2,196,768]{2,1,0:T(8,128)(2,1)}, bf16[2,784,768]{2,1,0:T(8,128)(2,1)}, f32[96,768]{1,0:T(8,128)}, f32[96,128]{1,0:T(8,128)}, f32[384,768]{1,0:T(8,128)}, /*index=5*/f32[768,384]{1,0:T(8,128)}) custom-call(bf16[416,768]{1,0:T(8,128)(2,1)} %get-tuple-element.33.refs_0_, bf16[416,768]{1,0:T(8,128)(2,1)} %get-tuple-element.34.refs_1_, ...), custom_call_target="tpu_custom_call" | custom-call | flops 14000000000 | bytes 16777216 | tf_op jit(solution)/shard_map/pallas_call | solution.py:1276
  191.5 0.0 copy-start
  191.5 2.5 %copy.60 = bf16[2,196,768]{2,0,1:T(2,128)(2,1)} copy(bf16[2,196,768]{2,1,0:T(8,128)(2,1)} %get-tuple-element.84) | data formatting | bytes 1204224
  194.0 1.6 slice_reduce_fusion
  195.6 1.4 copy.62
  197.0 1.2 slice_bitcast_fusion
  198.2 0.7 copy.61
  199.0 0.7 pad_maximum_fusion
  199.7 0.0 copy-done
  199.7 0.0 copy-start.2
  199.7 1.4 copy.69
  201.1 0.7 copy-done.2
  201.8 0.0 copy-start.1
  201.8 1.0 copy.70
  202.8 0.7 copy-done.1
  203.5 1.0 copy.71
  (7 shorter events, 0.1 us)
Async XLA Ops:
  191.5 8.2 %copy-start = (bf16[2,784,768]{2,1,0:T(8,128)(2,1)S(1)}, bf16[2,784,768]{2,1,0:T(8,128)(2,1)}, u32[]{:S(2)}) copy-start(bf16[2,784,768]{2,1,0:T(8,128)(2,1)} %get-tuple-element.116) | copy-start | bytes 7225348
  199.7 2.1 %copy-start.2 = (f32[384,768]{1,0:T(8,128)S(1)}, f32[384,768]{1,0:T(8,128)}, u32[]{:S(2)}) copy-start(f32[384,768]{1,0:T(8,128)} %get-tuple-element.55) | copy-start | bytes 3538948
  201.8 1.7 copy-start.1

commit v5 on v4

--- a/solution.py
+++ b/solution.py
@@ -311,6 +311,10 @@
     loop(g.ne - 1, relay)
 
 
+def odd(e2):
+    return lax.rem(e2, 2) == 1
+
+
 def weights_end(g, p, b):
     if not g.aligned:
         return
@@ -321,11 +325,29 @@
         at = p.od * g.ne + e2
         part = b.W.at[p.h, rows, :]
         arrived(b, p, "wx", part, e2)
-        send(b, "wy", part, part, at, at, p.across)
+
+        @pl.when(jnp.logical_not(odd(e2)))
+        def _():
+            send(b, "wy", part, part, at, at, p.across)
+
         send(b, "wc", part, part, at, at, p.core)
         arrived(b, p, "mx", b.MI.at[rows, :], e2)
 
     loop(g.ne, relay)
+
+    def over(k):
+        e2 = p.other(k)
+        at = p.d * g.ne + e2
+        part = b.W.at[p.hy, piece_rows(g, p.d, e2), :]
+        arrived(b, p, "wy", part, at)
+
+        @pl.when(odd(e2))
+        def _():
+            send(b, "wv", part, part, e2, e2, p.twin)
+
+        send(b, "wd", part, part, at, at, p.core)
+
+    loop(g.ne, over)
 
 
 def pieces(g):
@@ -345,12 +367,27 @@
 
     @pl.when(k == 2)
     def _():
+        if not g.aligned:
+            arrived(b, p, "wy", b.W.at[p.hy], 0)
+            send(b, "wd", b.W.at[p.hy], b.W.at[p.hy], 0, 0, p.core)
+            return
+
         def on(i):
-            part = piece_of(g, b.W, p.hy, i)
-            arrived(b, p, "wy", part, i)
-            send(b, "wd", part, part, i, i, p.core)
-
-        loop(pieces(g), on)
+            e2 = p.other(i)
+            at = p.od * g.ne + e2
+            part = b.W.at[p.hy, piece_rows(g, p.od, e2), :]
+
+            @pl.when(jnp.logical_not(odd(e2)))
+            def _():
+                arrived(b, p, "wy", part, at)
+
+            @pl.when(odd(e2))
+            def _():
+                arrived(b, p, "wv", part, e2)
+
+            send(b, "wd", part, part, at, at, p.core)
+
+        loop(g.ne, on)
 
     @pl.when(k == 3)
     def _():
@@ -370,14 +407,12 @@
     def group(k):
         group_in(g, p, b, k)
 
-        @pl.when(k == 1)
-        def _():
-            loop(g.ne // 2 - 1, lambda i: cotangent_on(g, p, b, p.other(i + 1)))
-            cotangent_over(g, p, b, p.e)
-
         @pl.when(k == 3)
         def _():
-            loop(g.ne - g.ne // 2, lambda i: cotangent_on(g, p, b, p.other(i + g.ne // 2)))
+            part = b.US.at[p.e, p.c, p.y]
+            send(b, "uy", part, part, p.e, p.e, p.across)
+            send(b, "uc", part, part, p.e, p.e, p.core)
+            loop(g.ne - 1, lambda i: cotangent_on(g, p, b, p.other(i + 1)))
 
         gi = 2 * lax.rem(p.y + lax.div(k, 2), 2) + lax.rem(p.c + k, 2)
         for blk in range(2):
@@ -485,10 +520,7 @@
 
         @pl.when(k == 0)
         def _():
-            part = b.US.at[p.e, p.c, p.y]
             b.US[p.e, p.c, p.y] = rows
-            send(b, "uy", part, part, p.e, p.e, p.across)
-            send(b, "uc", part, part, p.e, p.e, p.core)
 
     loop(g.ne, pack)
 
@@ -657,8 +689,6 @@
         b.HQ[:, cols] = value.astype(BF16)
         grad = nt(b.GP[:, : g.DH], b.WB[0, cols, :]) + nt(b.GP[:, g.DH :], b.WB[1, cols, :])
         b.GR[:, cols] = (grad * slope).astype(BF16)
-    if between is not None:
-        between()
     shape = (g.SG, 2, g.CP, g.DH)
     dots = []
     for q in range(2):
@@ -666,8 +696,6 @@
         b.PO[pl.ds(first, g.SG), :, q] = out.reshape(shape)
         up = b.US[pl.ds(first, g.SG), :, q].reshape(g.R, g.DH)
         dots.append(jnp.sum(out.astype(F32) * up.astype(F32), axis=1, keepdims=True))
-        b.DB[q] += tn(b.HQ[...], b.GP[:, q * g.DH : (q + 1) * g.DH])
-        b.DI[q] += tn(x[q], b.GR[...])
     dots = dots[0] + dots[1]
     for q in range(2):
         back = nt(b.GR[...], b.WI[q])
@@ -680,6 +708,14 @@
                 b.PG[first + i, blk, q] = jnp.where(
                     row == g.CAP, along, back[at : at + g.CP]
                 ).astype(BF16)
+    if between is not None:
+        between(0)
+    for q in range(2):
+        b.DB[q] += tn(b.HQ[...], b.GP[:, q * g.DH : (q + 1) * g.DH])
+    if between is not None:
+        between(1)
+    for q in range(2):
+        b.DI[q] += tn(x[q], b.GR[...])
 
 
 def experts(g, p, b):
@@ -687,7 +723,7 @@
     b.DI[...] = jnp.zeros_like(b.DI)
     n = g.ne
     if g.SG > 1:
-        loop(n - 1, lambda k: cotangent_over(g, p, b, p.other(k + 1)))
+        loop(n, lambda k: cotangent_over(g, p, b, p.other(k)))
         loop(n - 1, lambda k: slots_on(g, p, b, p.other(k + 1)))
         loop(n, lambda k: slots_over(g, p, b, p.other(k)))
         loop(n, lambda k: slots_in(g, p, b, p.other(k)))
@@ -697,33 +733,31 @@
         loop(n, lambda k: back_over(g, p, b, b.PG, p.other(k)))
         loop(n - 1, lambda k: back_on(g, p, b, b.PG, p.other(k)))
         return
-    loop(n - 1, lambda k: cotangent_over(g, p, b, p.other(k + 1)))
+    loop(n, lambda k: cotangent_over(g, p, b, p.other(k)))
     slots_over(g, p, b, p.e)
     slots_in(g, p, b, p.e)
+    loop(n - 1, lambda k: slots_on(g, p, b, p.other(k + 1)))
     experts_in(g, p, b)
 
     def source(k):
         @pl.when(k > 0)
         def _():
-            back_over(g, p, b, b.PG, p.other(k - 1))
             slots_over(g, p, b, p.other(k))
             slots_in(g, p, b, p.other(k))
 
-        def between():
-            @pl.when(k < n - 1)
-            def _():
-                slots_on(g, p, b, p.other(k + 1))
-
-            @pl.when(k > 1)
-            def _():
-                back_on(g, p, b, b.PG, p.other(k - 2))
+        def between(step):
+            if step == 0:
+                back_core(g, p, b, b.PG, p.other(k))
+
+                @pl.when(k > 0)
+                def _():
+                    back_on(g, p, b, b.PG, p.other(k - 1))
+            else:
+                back_over(g, p, b, b.PG, p.other(k))
 
         expert(g, b, p.other(k), between)
-        back_core(g, p, b, b.PG, p.other(k))
 
     loop(n, source)
-    back_on(g, p, b, b.PG, p.other(n - 2))
-    back_over(g, p, b, b.PG, p.other(n - 1))
 
 
 def first_sends_end(g, p, b):
@@ -744,10 +778,27 @@
         loop(n, x)
 
     def w(i):
-        for name in ("wy", "wc", "wd"):
+        for name in ("wc", "wd"):
             left(b, p, name, piece_of(g, b.W, p.h, i), i)
 
     loop(pieces(g), w)
+    if g.aligned:
+
+        def across(e2):
+            part = piece_of(g, b.W, p.h, 0)
+            left(b, p, "wy", part, p.d * n + e2)
+
+            @pl.when(jnp.logical_not(odd(e2)))
+            def _():
+                left(b, p, "wy", part, p.od * n + e2)
+
+            @pl.when(odd(e2))
+            def _():
+                left(b, p, "wv", part, e2)
+
+        loop(n, across)
+    else:
+        left(b, p, "wy", b.W.at[0], 0)
     left(b, p, "ta", b.TA.at[own_rows(g, 0), :], 0)
     left(b, p, "tp", b.TG.at[own_rows(g, 0), :], 0)
 
@@ -815,7 +866,6 @@
 
 def grads_of_expert_out(g, p, b):
     send(b, "gi", b.hSI, b.XI, 0, 0, p.twin)
-    send(b, "gb", b.hSB, b.XB, 0, 0, p.twin)
 
 
 def grads_of_expert_in(g, p, b):
@@ -1248,6 +1298,7 @@
     inputs_back(g, p, b)
     small_back(g, p, b)
     weights_back(g, p, b, 2, g.ne - 2)
+    send(b, "gb", b.hSB, b.XB, 0, 0, p.twin)
     back_in(g, p, b)
     slots_back(g, p, b, 0)
     unpack(g, p, b, 0)
@@ -1376,7 +1427,7 @@
             HQ=((g.R, g.F), BF16),
             GR=((g.R, g.F), BF16),
         ),
-        dict(wz=n, mz=n, wx=n, mx=n, wy=np_, wc=np_, wd=np_, ta=1, tp=1, uz=n, uy=n, uc=n, ud=n, xz=n, xy=n, xc=n, xd=n, ei=CHUNKS, eb=CHUNKS,
+        dict(wv=n, wz=n, mz=n, wx=n, mx=n, wy=np_, wc=np_, wd=np_, ta=1, tp=1, uz=n, uy=n, uc=n, ud=n, xz=n, xy=n, xc=n, xd=n, ei=CHUNKS, eb=CHUNKS,
              rc=n, ry=n, rz=n, ldx=2, ldu=2, ldb=1, **{"k" + name: 1 for name in KEEP}),
         1,
         14 * 10**9,

time: 205 us -> 193 us (0.941)
  Pallas kernels: 181 us -> 169 us
    pallas_call x2, Pallas kernels: 181 us -> 169 us  [call(): pl.pallas_call(kernel, out_shape=[jax.ShapeDtypeStruct(*o) for o in [*out...]
where the time goes in v5:
time: 193 us
  Pallas kernels  169 us (88%)
  local copies, waits for them, and re-layouts  19.7 us (10%)
  other arithmetic  2.87 us (1%)
    pallas_call x2, Pallas kernels, call(): pl.pallas_call(kernel, out_shape=[jax.ShapeDtypeStruct(*o) for o in [*out...  169 us
    unnamed x15, local copies, waits for them, and re-layouts  11.5 us

profile of v5, /device:TPU:0, one launch (start us, length us, event | category | flops | bytes accessed | tf_op | source)
XLA Modules:
  0.0 192.7 jit_solution(6562254227495841302)
XLA Ops:
  0.6 0.7 subtract_convert_fusion
  1.3 0.7 fusion
  2.0 0.8 concatenate.17
  2.8 0.8 concatenate.16
  3.6 0.1 reshape.25
  3.8 0.1 copy.56
  3.9 0.1 copy.55
  4.0 0.1 copy.54
  4.1 0.1 copy.53
  4.3 0.8 copy.52
  5.1 0.7 concatenate.15.refs_1_
  5.8 0.9 copy.51
  6.7 0.6 pad_bitcast_fusion.refs_5_
  7.3 0.9 slice_bitcast_fusion.6
  8.2 0.8 pad_maximum_fusion.1.refs_0_
  9.0 0.3 copy.63
  9.3 1.0 pad.9.clone.refs_4_
  10.2 103.1 %shard_map.178 = (bf16[416,768]{1,0:T(8,128)(2,1)}, bf16[416,768]{1,0:T(8,128)(2,1)}, bf16[4,768,768]{2,1,0:T(8,128)(2,1)}, bf16[768,128]{1,0:T(8,128)(2,1)}, f3...) custom-call(bf16[96,768]{1,0:T(8,128)(2,1)} %pad_maximum_fusion.1.re, ...), custom_call_target="tpu_custom_call" | custom-call | flops 14000000000 | bytes 16777216 | tf_op jit(solution)/shard_map/pallas_call | solution.py:1327
  113.4 66.3 %shard_map.179 = (bf16[2,196,768]{2,1,0:T(8,128)(2,1)}, bf16[2,784,768]{2,1,0:T(8,128)(2,1)}, f32[96,768]{1,0:T(8,128)}, f32[96,128]{1,0:T(8,128)}, f32[384,768]{1,0:T(8,128)}, /*index=5*/f32[768,384]{1,0:T(8,128)}) custom-call(bf16[416,768]{1,0:T(8,128)(2,1)} %get-tuple-element.33.refs_0_, bf16[416,768]{1,0:T(8,128)(2,1)} %get-tuple-element.34.refs_1_, ...), custom_call_target="tpu_custom_call" | custom-call | flops 14000000000 | bytes 16777216 | tf_op jit(solution)/shard_map/pallas_call | solution.py:1327
  179.7 0.0 copy-start
  179.7 2.5 %copy.60 = bf16[2,196,768]{2,0,1:T(2,128)(2,1)} copy(bf16[2,196,768]{2,1,0:T(8,128)(2,1)} %get-tuple-element.84) | data formatting | bytes 1204224
  182.2 1.6 slice_reduce_fusion
  183.8 1.4 copy.62
  185.2 1.2 slice_bitcast_fusion
  186.4 0.7 copy.61
  187.1 0.7 pad_maximum_fusion
  187.9 0.0 copy-done
  187.9 0.0 copy-start.2
  187.9 1.4 copy.69
  189.3 0.7 copy-done.2
  190.0 0.0 copy-start.1
  190.0 1.0 copy.70
  191.0 0.7 copy-done.1
  191.7 1.0 copy.71
  (7 shorter events, 0.1 us)
Async XLA Ops:
  179.7 8.2 %copy-start = (bf16[2,784,768]{2,1,0:T(8,128)(2,1)S(1)}, bf16[2,784,768]{2,1,0:T(8,128)(2,1)}, u32[]{:S(2)}) copy-start(bf16[2,784,768]{2,1,0:T(8,128)(2,1)} %get-tuple-element.116) | copy-start | bytes 7225348
  187.9 2.1 %copy-start.2 = (f32[384,768]{1,0:T(8,128)S(1)}, f32[384,768]{1,0:T(8,128)}, u32[]{:S(2)}) copy-start(f32[384,768]{1,0:T(8,128)} %get-tuple-element.55) | copy-start | bytes 3538948
  190.0 1.7 copy-start.1

commit v6 on v5

--- a/solution.py
+++ b/solution.py
@@ -828,7 +828,6 @@
     rows_out(g, p, b)
     p.enter()
     weights_out(g, p, b)
-    experts_out(g, p, b, range(2))
     b.WI[p.d] = b.wi[...]
     b.WB[p.d] = b.wb[...]
     rows_in(g, p, b)
@@ -836,7 +835,7 @@
     weights_on(g, p, b)
     cotangent_out(g, p, b)
     weights_end(g, p, b)
-    experts_out(g, p, b, range(2, 2 * CHUNKS))
+    experts_out(g, p, b, range(2 * CHUNKS))
     route(g, b, p.y, True)
     small_weights(g, b)
     first_norm(g, b)

time: 193 us -> 192 us (level)
  no operation moved by 1% of the time
where the time goes in v6:
time: 192 us; the launch traced here: 191 us
  Pallas kernels  168 us (88%)
  local copies, waits for them, and re-layouts  19.7 us (10%)
  other arithmetic  2.87 us (1%)
    pallas_call x2, Pallas kernels, call(): pl.pallas_call(kernel, out_shape=[jax.ShapeDtypeStruct(*o) for o in [*out...  168 us
    unnamed x15, local copies, waits for them, and re-layouts  11.5 us

profile of v6, /device:TPU:0, one launch (start us, length us, event | category | flops | bytes accessed | tf_op | source)
XLA Modules:
  0.0 191.0 jit_solution(7465758911592180871)
XLA Ops:
  0.6 0.7 subtract_convert_fusion
  1.3 0.7 fusion
  2.0 0.8 concatenate.17
  2.8 0.8 concatenate.16
  3.6 0.1 reshape.25
  3.8 0.1 copy.56
  3.9 0.1 copy.55
  4.0 0.1 copy.54
  4.1 0.1 copy.53
  4.3 0.8 copy.52
  5.1 0.7 concatenate.15.refs_1_
  5.8 0.9 copy.51
  6.7 0.6 pad_bitcast_fusion.refs_5_
  7.3 0.9 slice_bitcast_fusion.6
  8.2 0.8 pad_maximum_fusion.1.refs_0_
  9.0 0.3 copy.63
  9.3 1.0 pad.9.clone.refs_4_
  10.2 101.2 %shard_map.178 = (bf16[416,768]{1,0:T(8,128)(2,1)}, bf16[416,768]{1,0:T(8,128)(2,1)}, bf16[4,768,768]{2,1,0:T(8,128)(2,1)}, bf16[768,128]{1,0:T(8,128)(2,1)}, f3...) custom-call(bf16[96,768]{1,0:T(8,128)(2,1)} %pad_maximum_fusion.1.re, ...), custom_call_target="tpu_custom_call" | custom-call | flops 14000000000 | bytes 16777216 | tf_op jit(solution)/shard_map/pallas_call | solution.py:1326
  111.4 66.6 %shard_map.179 = (bf16[2,196,768]{2,1,0:T(8,128)(2,1)}, bf16[2,784,768]{2,1,0:T(8,128)(2,1)}, f32[96,768]{1,0:T(8,128)}, f32[96,128]{1,0:T(8,128)}, f32[384,768]{1,0:T(8,128)}, /*index=5*/f32[768,384]{1,0:T(8,128)}) custom-call(bf16[416,768]{1,0:T(8,128)(2,1)} %get-tuple-element.33.refs_0_, bf16[416,768]{1,0:T(8,128)(2,1)} %get-tuple-element.34.refs_1_, ...), custom_call_target="tpu_custom_call" | custom-call | flops 14000000000 | bytes 16777216 | tf_op jit(solution)/shard_map/pallas_call | solution.py:1326
  178.0 0.0 copy-start
  178.0 2.5 %copy.60 = bf16[2,196,768]{2,0,1:T(2,128)(2,1)} copy(bf16[2,196,768]{2,1,0:T(8,128)(2,1)} %get-tuple-element.84) | data formatting | bytes 1204224
  180.5 1.6 slice_reduce_fusion
  182.1 1.4 copy.62
  183.6 1.2 slice_bitcast_fusion
  184.7 0.7 copy.61
  185.5 0.7 pad_maximum_fusion
  186.2 0.0 copy-done
  186.2 0.0 copy-start.2
  186.2 1.4 copy.69
  187.6 0.7 copy-done.2
  188.3 0.0 copy-start.1
  188.3 1.0 copy.70
  189.3 0.7 copy-done.1
  190.0 1.0 copy.71
  (7 shorter events, 0.1 us)
Async XLA Ops:
  178.0 8.2 %copy-start = (bf16[2,784,768]{2,1,0:T(8,128)(2,1)S(1)}, bf16[2,784,768]{2,1,0:T(8,128)(2,1)}, u32[]{:S(2)}) copy-start(bf16[2,784,768]{2,1,0:T(8,128)(2,1)} %get-tuple-element.116) | copy-start | bytes 7225348
  186.2 2.1 %copy-start.2 = (f32[384,768]{1,0:T(8,128)S(1)}, f32[384,768]{1,0:T(8,128)}, u32[]{:S(2)}) copy-start(f32[384,768]{1,0:T(8,128)} %get-tuple-element.55) | copy-start | bytes 3538948
  188.3 1.7 copy-start.1
